TPU v7x, 128 devices: a whole 4x4x4 slice. The times are simulated.
128 devices in a mesh: ctx: 16 (over x, y_lo, core), enc: 8 (over z, y_hi).
Axes of the slice: x: 4, y: 4 (y_hi: 2, y_lo: 2; y = y_hi * 2 + y_lo), z: 4, core: 2. Of those that a mesh axis runs over, the one named last changes fastest.
Arguments:
- self_q: bfloat16 [4096, 4096], P('ctx', 'enc')
- self_k: bfloat16 [4096, 4096], P('ctx', 'enc')
- self_v: bfloat16 [4096, 4096], P('ctx', 'enc'), may hold values from -6 to 6
- cross_q: bfloat16 [4096, 4096], P('ctx', 'enc'), may hold values from -6 to 6
- cross_k_weight: bfloat16 [896, 4096], P(None, 'enc'), may hold values from -0.1875 to 0.1875
- cross_v_weight: bfloat16 [896, 4096], P(None, 'enc'), may hold values from -0.1875 to 0.1875
- span_ctx: bfloat16 [4096, 896], P('ctx'), may hold values from -6 to 6
- neighbours: bfloat16 [256, 128, 896], P(('ctx', 'enc')), may hold values from -6 to 6
- neighbour_ids: int32 [64, 2], P('ctx'), may hold values from 0 to 15, as said below
- enc_q: bfloat16 [896, 896], replicated, may hold values from -0.1875 to 0.1875
- enc_k: bfloat16 [896, 896], replicated, may hold values from -0.1875 to 0.1875
- enc_v: bfloat16 [896, 896], replicated, may hold values from -0.1875 to 0.1875
- enc_o: bfloat16 [896, 896], replicated, may hold values from -0.1875 to 0.1875
- mixed_grad: bfloat16 [4096, 4096], P('ctx', 'enc'), may hold values from -6 to 6
Outputs:
- mixed: bfloat16 [4096, 4096], P('ctx', 'enc')
- neighbour_grad: float32 [256, 128, 896], P(('ctx', 'enc'))
Inputs may be any that keep to these rules, and one draw needn't show every extreme that they name: `neighbour_ids`: within the 4 spans of one ctx index the 8 values are distinct slots; slot g of that index is held by enc index g // 2; in every such group some enc index has all of its 2 slots named.
All inputs are finite; a program needn't handle non-finite values.
Results may differ from a plain program's by a relative error of at most 0.025.
Values may be sent and summed in bfloat16 or wider, within the bound.
No kernel may reach another device: no remote copies, remote signals or barrier semaphores. Data moves between devices by JAX's collectives and lax.ppermute only.
A program may use at most 128 MiB of HBM per device.

v0:
```python
import math

import jax
import jax.numpy as jnp
from jax import lax
from jax.sharding import PartitionSpec as P

HSIZE = 128
EHEADS = 4
CL = 64
NL = 128


def encode(inputs, context, enc_q, enc_k, enc_v, enc_o):
    rows_in = inputs.shape[0]
    width_enc = inputs.shape[1]
    head_width = width_enc // EHEADS
    as_half = inputs.astype(jnp.bfloat16)
    queries = jnp.dot(as_half, enc_q, preferred_element_type=jnp.float32).astype(jnp.bfloat16)
    keys_enc = jnp.dot(context, enc_k, preferred_element_type=jnp.float32).astype(jnp.bfloat16)
    values_enc = jnp.dot(context, enc_v, preferred_element_type=jnp.float32).astype(jnp.bfloat16)
    q_heads = queries.reshape(rows_in, EHEADS, head_width).astype(jnp.float32)
    k_heads = keys_enc.reshape(-1, EHEADS, head_width).astype(jnp.float32)
    v_heads = values_enc.reshape(-1, EHEADS, head_width).astype(jnp.float32)
    scores = jnp.einsum("qhd,khd->hqk", q_heads, k_heads) / math.sqrt(head_width)
    weights = jax.nn.softmax(scores, axis=-1).astype(jnp.bfloat16).astype(jnp.float32)
    mixed_heads = (
        jnp.einsum("hqk,khd->qhd", weights, v_heads)
        .reshape(rows_in, width_enc)
        .astype(jnp.bfloat16)
    )
    return inputs + jnp.dot(mixed_heads, enc_o, preferred_element_type=jnp.float32)


def local(
    self_q,
    self_k,
    self_v,
    cross_q,
    cross_k_weight,
    cross_v_weight,
    span_ctx,
    neighbours,
    neighbour_ids,
    enc_q,
    enc_k,
    enc_v,
    enc_o,
    mixed_grad,
):
    rows_here = self_q.shape[0]
    width_here = self_q.shape[1]
    heads_here = width_here // HSIZE
    score_scale = 1.0 / math.sqrt(HSIZE)
    ctx_index = lax.axis_index("ctx")
    query_places = ctx_index * rows_here + jnp.arange(rows_here)
    queries = self_q.reshape(rows_here, heads_here, HSIZE)
    start_state = (
        jnp.zeros((heads_here, rows_here, HSIZE), jnp.float32),
        jnp.full((heads_here, rows_here), -1e30, jnp.float32),
        jnp.zeros((heads_here, rows_here), jnp.float32),
    )
    key_rows = lax.all_gather(self_k, "ctx", axis=0, tiled=True)
    count = key_rows.shape[0]
    block = math.gcd(count, 512)
    key_partitions = key_rows.reshape(count // block, block, heads_here, HSIZE)
    value_tiles = lax.all_gather(self_v, "ctx", axis=0, tiled=True).reshape(
        count // block, block, heads_here, HSIZE
    )
    tile_starts = jnp.arange(count // block) * block

    def one_tile(state_now, items):
        key_tile, value_tile, tile_start = items
        numer, row_top, row_total = state_now
        scores = (
            jnp.einsum("qhd,khd->hqk", queries, key_tile, preferred_element_type=jnp.float32)
            * score_scale
        )
        key_places = tile_start + jnp.arange(block)
        visible = (key_places[None, :] <= query_places[:, None]) & (key_places[None, :] >= 0)
        scores = jnp.where(visible[None], scores, -1e30)
        new_top = jnp.maximum(row_top, jnp.max(scores, axis=-1))
        rescale = jnp.exp(row_top - new_top)
        weights = jnp.where(visible[None], jnp.exp(scores - new_top[..., None]), 0.0)
        row_total = row_total * rescale + jnp.sum(weights, axis=-1)
        numer = numer * rescale[..., None] + jnp.einsum(
            "hqk,khd->hqd",
            weights.astype(jnp.bfloat16),
            value_tile,
            preferred_element_type=jnp.float32,
        )
        state_now = (numer, new_top, row_total)
        return (state_now, None)

    state_out, _ = lax.scan(one_tile, start_state, (key_partitions, value_tiles, tile_starts))
    numer, row_top, row_total = state_out
    self_out = (numer / row_total[..., None]).transpose(1, 0, 2).reshape(rows_here, width_here)
    enc_index = lax.axis_index("enc")
    slots_here = neighbours.shape[0]
    group_count = lax.axis_size("enc")
    local_spans = rows_here // CL
    my_slots = enc_index * slots_here + jnp.arange(slots_here)
    ids_flat = neighbour_ids.reshape(-1)
    span_of = jnp.arange(ids_flat.shape[0]) // neighbour_ids.shape[1]
    slot_hits = ids_flat[:, None] == my_slots[None, :]
    span_hits = span_of[:, None] == jnp.arange(local_spans)[None, :]
    span_per_slot = jnp.any(slot_hits[:, :, None] & span_hits[:, None, :], axis=0).astype(
        jnp.bfloat16
    )
    block_contexts = span_ctx.reshape(local_spans, CL, span_ctx.shape[1])
    selected = jnp.einsum(
        "th,hwo->two", span_per_slot, block_contexts, preferred_element_type=jnp.float32
    ).astype(jnp.bfloat16)

    def encode_slots(values_in):
        return jax.vmap(
            lambda single, context: encode(single, context, enc_q, enc_k, enc_v, enc_o)
        )(values_in, selected)

    encoded_f, pullback = jax.vjp(encode_slots, neighbours.astype(jnp.float32))
    encoded = encoded_f.astype(jnp.bfloat16)
    every_block = lax.all_gather(encoded, "enc", axis=0, tiled=True)
    used_blocks = jnp.take(every_block, ids_flat, axis=0)
    used_flat = used_blocks.reshape(-1, used_blocks.shape[2])
    cross_keys = jnp.dot(used_flat, cross_k_weight, preferred_element_type=jnp.float32).astype(
        jnp.bfloat16
    )
    cross_vals = jnp.dot(used_flat, cross_v_weight, preferred_element_type=jnp.float32).astype(
        jnp.bfloat16
    )
    cross_keys = cross_keys.reshape(local_spans, 2 * NL, heads_here, HSIZE)
    cross_vals = cross_vals.reshape(local_spans, 2 * NL, heads_here, HSIZE)
    cross_query = cross_q.reshape(local_spans, CL, heads_here, HSIZE)
    scores = (
        jnp.einsum("cqhd,ckhd->chqk", cross_query, cross_keys, preferred_element_type=jnp.float32)
        * score_scale
    )
    probs = jax.nn.softmax(scores, axis=-1)
    probs_half = probs.astype(jnp.bfloat16)
    cross_out = jnp.einsum(
        "chqk,ckhd->cqhd", probs_half, cross_vals, preferred_element_type=jnp.float32
    ).reshape(rows_here, width_here)
    mixed = (self_out + cross_out).astype(jnp.bfloat16)
    grad_heads = mixed_grad.reshape(local_spans, CL, heads_here, HSIZE)
    grad_probs = jnp.einsum(
        "cqhd,ckhd->chqk", grad_heads, cross_vals, preferred_element_type=jnp.float32
    )
    grad_scores = probs * (grad_probs - jnp.sum(probs * grad_probs, axis=-1, keepdims=True))
    grad_keys = (
        jnp.einsum(
            "chqk,cqhd->ckhd",
            grad_scores,
            cross_query.astype(jnp.float32),
            precision=lax.Precision.HIGHEST,
        )
        * score_scale
    ).astype(jnp.bfloat16)
    grad_vals = jnp.einsum(
        "chqk,cqhd->ckhd", probs_half, grad_heads, preferred_element_type=jnp.float32
    ).astype(jnp.bfloat16)
    used_gradient = jnp.dot(
        grad_keys.reshape(-1, width_here), cross_k_weight.T, preferred_element_type=jnp.float32
    )
    used_gradient = used_gradient + jnp.dot(
        grad_vals.reshape(-1, width_here), cross_v_weight.T, preferred_element_type=jnp.float32
    )
    used_gradient = used_gradient.reshape(ids_flat.shape[0], NL, -1)
    slot_lookup_table = (jnp.arange(group_count * slots_here)[:, None] == ids_flat[None, :]).astype(
        jnp.float32
    )
    grad_enc = lax.psum_scatter(
        jnp.einsum(
            "yz,zhq->yhq", slot_lookup_table, used_gradient, precision=lax.Precision.HIGHEST
        ).astype(jnp.bfloat16),
        "enc",
        scatter_dimension=0,
        tiled=True,
    ).astype(jnp.float32)
    neighbour_grad = pullback(grad_enc)[0]
    return (mixed, neighbour_grad)


def solution(mesh):
    return jax.shard_map(
        local,
        mesh=mesh,
        in_specs=(
            P("ctx", "enc"),
            P("ctx", "enc"),
            P("ctx", "enc"),
            P("ctx", "enc"),
            P(None, "enc"),
            P(None, "enc"),
            P("ctx", None),
            P(("ctx", "enc"), None, None),
            P("ctx", None),
            P(),
            P(),
            P(),
            P(),
            P("ctx", "enc"),
        ),
        out_specs=(P("ctx", "enc"), P(("ctx", "enc"), None, None)),
        check_vma=False,
    )
```

profile of v0, /device:TPU:0, one launch (start us, length us, event | category | flops | bytes accessed | tf_op | source)
XLA Modules:
  0.0 269.3 jit_solution(17825636033728572906)
XLA Ops:
  8.5 1.5 convolution_convert_fusion.5
  10.7 2.6 fusion.64
  13.2 1.2 reshape.243
  14.4 2.6 fusion.45
  17.0 1.3 copy.121
  19.4 1.9 fusion.61
  22.0 1.5 fusion.42
  25.9 1.7 reshape.249
  28.8 64.6 %all-gather.8.cloned.1.call-done = bf16[16,128,896]{2,1,0:T(8,128)(2,1)} async-done(((bf16[2,128,896]{2,1,0:T(8,128)(2,1)}), bf16[16,128,896]{2,1,0:T(8,128)(2,1)}) %all-gather.8.cloned.1.call-update) | async-done | bytes 3670032 | tf_op jit(solution)/shard_map/all_gather | solution.py:122
  93.4 2.9 %gather_fusion = bf16[8,128,896]{2,1,0:T(8,128)(2,1)S(1)} fusion(bf16[16,128,896]{2,1,0:T(8,128)(2,1)} %all-gather.8.cloned.1.call-done, s32[1024]{0:T(1024)S(1)} %pad_clamp_fusion), kind=kCustom, calls=%fused_computation | custom fusion | bytes 3670048 | tf_op jit(solution)/shard_map/jit(_take)/gather | solution.py:123
  96.7 1.3 copy-done.3
  98.0 2.2 convolution_convert_fusion.1
  100.2 1.3 reshape.246
  101.6 4.0 %convolution_convert_fusion.2 = bf16[1024,512]{1,0:T(8,128)(2,1)} fusion(bf16[1024,896]{1,0:T(8,128)(2,1)} %copy-done.3, bf16[896,512]{1,0:T(8,128)(2,1)} %param.21), kind=kOutput, calls=%fused_computation.52 | convolution fusion | flops 940048384 | bytes 3801088 | tf_op jit(solution)/shard_map/dot_general | solution.py:128
  105.5 2.2 reshape.245
  109.2 2.7 %fusion.111 = (f32[4,4,64]{2,1,0:T(4,128)S(1)}, f32[4,4,64,256]{3,2,1,0:T(8,128)S(1)}) fusion(f32[4,4,64,256]{3,2,1,0:T(8,128)S(1)} %fusion.38), kind=kOutput, calls=%fused_computation.140 | output fusion | flops 524543 | bytes 2101248 | tf_op jit(solution)/shard_map/sub | solution.py:138
  112.6 2.2 fusion.37
  115.7 4.8 %fusion.35 = bf16[4,256,4,128]{3,1,2,0:T(8,128)(2,1)} fusion(bf16[4,64,4,128]{3,2,1,0:T(4,128)(2,1)S(1)} %copy-done.26, f32[4,4,64]{2,1,0:T(4,128)S(1)} %get-tuple-element.142, f32[4,4,64,256]{3,2,1,0:T(8,128)} %copy-done.2), kind=kOutput, calls=%fused_computation.53 | convolution fusion | flops 68420864 | bytes 2363392 | tf_op jit(solution)/shard_map/chqk,cqhd->ckhd/dot_general | solution.py:158
  120.4 2.1 copy.136
  122.6 1.3 fusion.71
  123.9 1.3 convolution_add_fusion.1
  125.2 4.6 %fusion.19 = bf16[16,128,896]{2,0,1:T(8,128)(2,1)S(1)} fusion(f32[8,128,896]{2,1,0:T(8,128)S(1)} %bitcast.144, s32[8]{0:T(128)S(1)} %reshape.239), kind=kOutput, calls=%fused_computation.33 | convolution fusion | flops 177995904 | bytes 7340064 | tf_op jit(solution)/shard_map/yz,zhq->yhq/dot_general | solution.py:172
  129.8 2.6 copy.138
  132.5 3.4 %convolution_bitcast_fusion.1 = f32[4,64,4,128]{3,1,2,0:T(8,128)S(1)} fusion(bf16[4,256,4,128]{3,2,1,0:T(4,128)(2,1)S(1)} %copy-done.10, f32[4,4,64]{2,1,0:T(4,128)S(1)} %get-tuple-element.142, f32[4,4,64,256]{3,2,1,0:T(8,128)} %copy-done.2), kind=kOutput, calls=%fused_computation.68 | convolution fusion | flops 67896576 | bytes 2625536 | tf_op jit(solution)/shard_map/chqk,ckhd->cqhd/dot_general | solution.py:140
  136.3 6.9 %reshape.269 = bf16[8,512,4,128]{3,2,1,0:T(4,128)(2,1)} reshape(bf16[4096,512]{1,0:T(8,128)(2,1)} %all-gather.4.cloned.1.call-done) | data formatting | bytes 8388608 | tf_op jit(solution)/shard_map/reshape | solution.py:66
  143.2 26.1 %all-gather.6.cloned.1.call-done = bf16[4096,512]{1,0:T(8,128)(2,1)} async-done(((bf16[256,512]{1,0:T(8,128)(2,1)}), bf16[4096,512]{1,0:T(8,128)(2,1)}) %all-gather.6.cloned.1.call-update) | async-done | bytes 4194320 | tf_op jit(solution)/shard_map/all_gather | solution.py:67
  169.3 7.0 %reshape.270 = bf16[8,512,4,128]{3,2,1,0:T(4,128)(2,1)} reshape(bf16[4096,512]{1,0:T(8,128)(2,1)} %all-gather.6.cloned.1.call-done) | data formatting | bytes 8388608 | tf_op jit(solution)/shard_map/reshape | solution.py:67
  176.3 72.8 %while.15 = (s32[]{:T(128)}, f32[4,256,128]{2,1,0:T(8,128)S(1)}, f32[4,256]{1,0:T(4,128)S(1)}, f32[4,256]{1,0:T(4,128)S(1)}, s32[8]{0:T(128)S(1)}, /*index=5*/bf...) while((s32[]{:T(128)}, f32[4,256,128]{2,1,0:T(8,128)S(1)}, ...), condition=%wide.region_3.4_spmd.clone, body=%wide.region_0.3_spmd.clone.sunk | while | flops 275913472 | bytes 20782284 | solution.py:95
  178.4 1.6 constant_dynamic-slice_fusion.3
  180.0 1.8 fusion.138
  181.8 2.4 fusion.139
  187.6 1.6 constant_dynamic-slice_fusion.3
  189.2 1.8 fusion.138
  191.0 2.3 fusion.139
  193.3 1.1 convolution_add_fusion.3
  196.6 1.6 constant_dynamic-slice_fusion.3
  198.2 1.8 fusion.138
  200.1 2.3 fusion.139
  202.4 1.1 convolution_add_fusion.3
  205.7 1.6 constant_dynamic-slice_fusion.3
  207.3 1.8 fusion.138
  209.2 2.3 fusion.139
  211.5 1.1 convolution_add_fusion.3
  214.8 1.6 constant_dynamic-slice_fusion.3
  216.4 1.8 fusion.138
  218.2 2.3 fusion.139
  220.5 1.1 convolution_add_fusion.3
  223.9 1.6 constant_dynamic-slice_fusion.3
  225.4 1.8 fusion.138
  227.3 2.3 fusion.139
  229.6 1.1 convolution_add_fusion.3
  232.9 1.6 constant_dynamic-slice_fusion.3
  234.5 1.8 fusion.138
  236.3 2.6 fusion.139
  238.9 1.1 convolution_add_fusion.3
  242.2 1.6 constant_dynamic-slice_fusion.3
  243.8 1.8 fusion.138
  245.7 2.3 fusion.139
  248.0 1.1 convolution_add_fusion.3
  249.9 2.0 fusion.79
  251.9 3.2 %reduce-scatter.2.cloned.1.call-done = bf16[2,128,896]{2,1,0:T(8,128)(2,1)} async-done(((bf16[16,128,896]{2,1,0:T(8,128)(2,1)}), bf16[2,128,896]{2,1,0:T(8,128)(2,1)}) %reduce-scatter.2.cloned.1.call-update) | async-done | bytes 458768 | tf_op jit(solution)/shard_map/reduce_scatter | solution.py:171
  255.1 1.8 fusion.57
  258.2 1.4 convolution_convert_fusion.3
  259.6 3.1 %fusion.54 = f32[2,128,896]{2,1,0:T(8,128)} fusion(bf16[2,128,896]{1,2,0:T(8,128)(2,1)S(1)} %bitcast.151, bf16[896,896]{1,0:T(8,128)(2,1)} %param.25, bf16[2,128,896]{2,1,0:T(8,128)(2,1)S(1)} %copy-done.22), kind=kOutput, calls=%fused_computation.66 | convolution fusion | flops 411959296 | bytes 3440640 | tf_op jit(solution)/shard_map/transpose(jvp(vmap()))/dot_general | solution.py:19
  (187 shorter events, 31.0 us)
Async XLA Ops:
  7.2 14.8 %copy-start = (bf16[896,896]{1,0:T(8,128)(2,1)S(1)}, bf16[896,896]{1,0:T(8,128)(2,1)}, u32[]{:S(2)}) copy-start(bf16[896,896]{1,0:T(8,128)(2,1)} %param.28) | copy-start | bytes 4816900
  7.2 7.3 %copy-start.4 = (bf16[896,896]{1,0:T(8,128)(2,1)S(1)}, bf16[896,896]{1,0:T(8,128)(2,1)}, u32[]{:S(2)}) copy-start(bf16[896,896]{1,0:T(8,128)(2,1)} %param.25) | copy-start | bytes 4816900
  7.2 86.2 %all-gather.8.cloned.1.call-start = ((), (), s32[]{:S(2)}) async-start(), calls=%async_computation.3 | async-start | bytes 4128768 | tf_op jit(solution)/shard_map/all_gather | solution.py:122
  10.0 0.7 copy-start.17
  14.4 4.2 %copy-start.12 = (bf16[2,64,4,224]{3,2,1,0:T(4,128)(2,1)}, bf16[2,64,4,224]{3,2,1,0:T(4,128)(2,1)S(1)}, u32[]{:S(2)}) copy-start(bf16[2,64,4,224]{3,2,1,0:T(4,128)(2,1)S(1)} %reshape.243) | copy-start | bytes 688132
  17.0 2.4 copy-start.18
  18.6 3.3 %copy-start.11 = (f32[2,4,128,64]{2,3,1,0:T(8,128)}, f32[2,4,128,64]{2,3,1,0:T(8,128)S(1)}, u32[]{:S(2)}) copy-start(f32[2,4,128,64]{2,3,1,0:T(8,128)S(1)} %convolution_multiply_fusion.1) | copy-start | bytes 786436
  19.4 2.5 copy-start.21
  21.6 1.9 copy-start.7
  22.0 3.2 %copy-start.23 = (bf16[256,512]{1,0:T(8,128)(2,1)S(1)}, bf16[256,512]{1,0:T(8,128)(2,1)}, u32[]{:S(2)}) copy-start(bf16[256,512]{1,0:T(8,128)(2,1)} %param.19) | copy-start | bytes 786436
  23.5 4.1 %copy-start.24 = (bf16[256,512]{1,0:T(8,128)(2,1)S(1)}, bf16[256,512]{1,0:T(8,128)(2,1)}, u32[]{:S(2)}) copy-start(bf16[256,512]{1,0:T(8,128)(2,1)} %param.16) | copy-start | bytes 786436
  23.5 112.8 %all-gather.4.cloned.1.call-start = ((), (), s32[]{:S(2)}) async-start(), calls=%async_computation.1 | async-start | bytes 4456448 | tf_op jit(solution)/shard_map/all_gather | solution.py:63
  24.3 145.1 %all-gather.6.cloned.1.call-start = ((), (), s32[]{:S(2)}) async-start(), calls=%async_computation.2 | async-start | bytes 4456448 | tf_op jit(solution)/shard_map/all_gather | solution.py:67
  25.0 230.1 %reduce-scatter.2.cloned.1.call-start = ((), (), s32[]{:S(2)}) async-start(), calls=%async_computation.4 | async-start | bytes 4128768 | tf_op jit(solution)/shard_map/reduce_scatter | solution.py:171
  96.3 1.7 copy-start.14
  96.7 1.3 copy-start.3
  105.5 2.3 copy-start.6
  107.8 4.2 %copy-start.9 = (bf16[4,256,4,128]{3,2,1,0:T(4,128)(2,1)S(1)}, bf16[4,256,4,128]{3,2,1,0:T(4,128)(2,1)}, u32[]{:S(2)}) copy-start(bf16[4,256,4,128]{3,2,1,0:T(4,128)(2,1)} %reshape.245) | copy-start | bytes 3145732
  107.8 4.2 %copy-start.26 = (bf16[4,64,4,128]{3,2,1,0:T(4,128)(2,1)S(1)}, bf16[4,64,4,128]{3,2,1,0:T(4,128)(2,1)}, u32[]{:S(2)}) copy-start(bf16[4,64,4,128]{3,2,1,0:T(4,128)(2,1)} %reshape.249) | copy-start | bytes 786436
  108.3 1.0 copy-start.2
  120.4 2.1 copy-start.15
  122.6 1.3 copy-start.16
  129.8 2.7 copy-start.10
  143.2 33.1 %copy-start.19 = (f32[4,256,128]{2,1,0:T(8,128)S(1)}, f32[4,256,128]{2,1,0:T(8,128)}, u32[]{:S(2)}) copy-start(f32[4,256,128]{2,1,0:T(8,128)} %custom-call) | copy-start | bytes 1572868
  176.3 3.7 %copy-start.25 = (bf16[256,4,128]{2,0,1:T(8,128)(2,1)S(1)}, bf16[256,4,128]{2,0,1:T(8,128)(2,1)}, u32[]{:S(2)}) copy-start(bf16[256,4,128]{2,0,1:T(8,128)(2,1)} %get-tuple-element.243) | copy-start | bytes 786436 | tf_op jit(solution)/shard_map/while
  181.8 2.5 copy-start.1
  185.5 3.7 %copy-start.25 = (bf16[256,4,128]{2,0,1:T(8,128)(2,1)S(1)}, bf16[256,4,128]{2,0,1:T(8,128)(2,1)}, u32[]{:S(2)}) copy-start(bf16[256,4,128]{2,0,1:T(8,128)(2,1)} %get-tuple-element.243) | copy-start | bytes 786436 | tf_op jit(solution)/shard_map/while
  191.0 2.3 copy-start.1
  194.5 3.7 %copy-start.25 = (bf16[256,4,128]{2,0,1:T(8,128)(2,1)S(1)}, bf16[256,4,128]{2,0,1:T(8,128)(2,1)}, u32[]{:S(2)}) copy-start(bf16[256,4,128]{2,0,1:T(8,128)(2,1)} %get-tuple-element.243) | copy-start | bytes 786436 | tf_op jit(solution)/shard_map/while
  200.1 2.3 copy-start.1
  203.6 3.7 %copy-start.25 = (bf16[256,4,128]{2,0,1:T(8,128)(2,1)S(1)}, bf16[256,4,128]{2,0,1:T(8,128)(2,1)}, u32[]{:S(2)}) copy-start(bf16[256,4,128]{2,0,1:T(8,128)(2,1)} %get-tuple-element.243) | copy-start | bytes 786436 | tf_op jit(solution)/shard_map/while
  209.1 2.3 copy-start.1
  212.7 3.7 %copy-start.25 = (bf16[256,4,128]{2,0,1:T(8,128)(2,1)S(1)}, bf16[256,4,128]{2,0,1:T(8,128)(2,1)}, u32[]{:S(2)}) copy-start(bf16[256,4,128]{2,0,1:T(8,128)(2,1)} %get-tuple-element.243) | copy-start | bytes 786436 | tf_op jit(solution)/shard_map/while
  218.2 2.3 copy-start.1
  221.7 3.7 %copy-start.25 = (bf16[256,4,128]{2,0,1:T(8,128)(2,1)S(1)}, bf16[256,4,128]{2,0,1:T(8,128)(2,1)}, u32[]{:S(2)}) copy-start(bf16[256,4,128]{2,0,1:T(8,128)(2,1)} %get-tuple-element.243) | copy-start | bytes 786436 | tf_op jit(solution)/shard_map/while
  227.3 2.3 copy-start.1
  230.8 3.7 %copy-start.25 = (bf16[256,4,128]{2,0,1:T(8,128)(2,1)S(1)}, bf16[256,4,128]{2,0,1:T(8,128)(2,1)}, u32[]{:S(2)}) copy-start(bf16[256,4,128]{2,0,1:T(8,128)(2,1)} %get-tuple-element.243) | copy-start | bytes 786436 | tf_op jit(solution)/shard_map/while
  236.3 2.6 copy-start.1
  240.1 3.7 %copy-start.25 = (bf16[256,4,128]{2,0,1:T(8,128)(2,1)S(1)}, bf16[256,4,128]{2,0,1:T(8,128)(2,1)}, u32[]{:S(2)}) copy-start(bf16[256,4,128]{2,0,1:T(8,128)(2,1)} %get-tuple-element.243) | copy-start | bytes 786436 | tf_op jit(solution)/shard_map/while
  245.6 2.3 copy-start.1
  249.1 0.8 copy-start.20
  249.9 7.2 %copy-start.5 = (f32[2,4,128,64]{2,3,1,0:T(8,128)S(1)}, f32[2,4,128,64]{2,3,1,0:T(8,128)}, u32[]{:S(2)}) copy-start(f32[2,4,128,64]{2,3,1,0:T(8,128)} %get-tuple-element.141) | copy-start | bytes 786436
  249.9 7.2 %copy-start.8 = (bf16[2,64,4,224]{3,2,1,0:T(4,128)(2,1)S(1)}, bf16[2,64,4,224]{3,2,1,0:T(4,128)(2,1)}, u32[]{:S(2)}) copy-start(bf16[2,64,4,224]{3,2,1,0:T(4,128)(2,1)} %copy-done.7) | copy-start | bytes 688132
  251.9 6.2 %copy-start.13 = (bf16[2,64,4,224]{3,2,1,0:T(4,128)(2,1)S(1)}, bf16[2,64,4,224]{3,2,1,0:T(4,128)(2,1)}, u32[]{:S(2)}) copy-start(bf16[2,64,4,224]{3,2,1,0:T(4,128)(2,1)} %copy-done.12) | copy-start | bytes 688132
  257.2 2.5 copy-start.22
Sparse Core Ops, SparseCore 0:
  23.7 69.6 all-gather.7
  95.1 35.0 all-gather.3
  131.9 37.3 all-gather.5
  173.1 81.9 reduce-scatter.1
where the time goes:
time: 271 us; the launch traced here: 269 us
  waiting for transfers between devices  95.3 us (35%)
  matrix products  66.5 us (25%)
  local copies, waits for them, and re-layouts  55.1 us (20%)
  other arithmetic  37.3 us (14%)
  between operations  14.2 us (5%)
    all_gather x1, waiting for transfers between devices, local(): every_block = lax.all_gather(encoded, 'enc', axis=0, tiled=True)  64.6 us
    all_gather x1, waiting for transfers between devices, local(): lax.all_gather(self_v, 'ctx', axis=0, tiled=True)  26.1 us
    reduce_sum x8, other arithmetic, one_tile(): row_total = row_total * rescale + jnp.sum(weights, axis=-1)  18.7 us
    dynamic_slice x16, local copies, waits for them, and re-layouts, local(): lax.scan(one_tile, start_state, (key_partitions, value_tiles, tile_starts))  17.3 us
    dot_general x8, matrix products, one_tile(): jnp.einsum('qhd,khd->hqk', queries, key_tile, preferred_element_type=jnp....  14.6 us
    dot_general x8, matrix products, one_tile(): jnp.einsum('hqk,khd->hqd', weights.astype(jnp.bfloat16), value_tile, pref...  9.15 us
    reshape x1, local copies, waits for them, and re-layouts, local(): lax.all_gather(self_v, 'ctx', axis=0, tiled=True)  6.95 us
    reshape x1, local copies, waits for them, and re-layouts, local(): key_partitions = key_rows.reshape(count // block, block, heads_here, HSIZE)  6.92 us
  transfers between devices with their start and end apart: 4, of which 3 were waited for; matrix products, arithmetic and copies ran while one was open for 49% of the time, Pallas kernels for 0%

commit v1 on v0

v1 whole, which is shorter than its diff:
```python
import math

import jax
import jax.numpy as jnp
from jax import lax
from jax.experimental import pallas as pl
from jax.experimental.pallas import tpu as pltpu
from jax.sharding import Mesh
from jax.sharding import PartitionSpec as P

HSIZE = 128
EHEADS = 4
CL = 64
NL = 128
NX = 4
LOG2E = math.log2(math.e)
BF16 = jnp.bfloat16
F32 = jnp.float32

NT = (((1,), (1,)), ((), ()))
TN = (((0,), (0,)), ((), ()))


def mm(a, b):
    return jnp.dot(a, b, preferred_element_type=F32)


def mm_nt(a, b):
    return lax.dot_general(a, b, NT, preferred_element_type=F32)


def mm_tn(a, b):
    return lax.dot_general(a, b, TN, preferred_element_type=F32)


def call(kernel, mib=32, **kw):
    return pl.pallas_call(
        kernel,
        compiler_params=pltpu.CompilerParams(vmem_limit_bytes=mib * 1024 * 1024),
        **kw,
    )


def smem():
    return pl.BlockSpec(memory_space=pltpu.SMEM)


def vmem():
    return pl.BlockSpec(memory_space=pltpu.VMEM)


def hbm():
    return pl.BlockSpec(memory_space=pl.ANY)


def pack_kernel(q_ref, k_ref, v_ref, o0, o1, o2, o3, sems):
    x = lax.axis_index("x")
    copies = []
    for d, out in enumerate((o0, o1, o2, o3)):
        cols = pl.ds(pl.multiple_of(lax.rem(x + d, NX) * HSIZE, HSIZE), HSIZE)
        for i, src in enumerate((q_ref, k_ref, v_ref)):
            copies.append(pltpu.make_async_copy(src.at[:, cols], out.at[i], sems.at[d, i]))
    for c in copies:
        c.start()
    for c in copies:
        c.wait()


def attend_kernel(q0, q1, q2, q3, kv, o0, o1, o2, o3, acc, top, total):
    x = lax.axis_index("x")
    r = lax.axis_index("yl") * 2 + lax.axis_index("core")
    scale = LOG2E / math.sqrt(HSIZE)
    for d, (q_ref, o_ref) in enumerate(zip((q0, q1, q2, q3), (o0, o1, o2, o3))):
        xq = lax.rem(x - d + NX, NX)
        q = q_ref[0]
        rows = q.shape[0]
        acc[...] = jnp.zeros_like(acc)
        top[...] = jnp.full_like(top, -1e30)
        total[...] = jnp.zeros_like(total)

        def group(xk, masked):
            dk = lax.rem(x - xk + NX, NX)
            scores = [mm_nt(q, kv[i, dk, 0]) for i in range(4)]
            if masked:
                at = lax.broadcasted_iota(jnp.int32, (rows, rows), 1)
                upto = lax.broadcasted_iota(jnp.int32, (rows, rows), 0)
                scores = [
                    jnp.where(at + i * rows <= upto + r * rows, s, -1e30)
                    for i, s in enumerate(scores)
                ]
            best = jnp.maximum(
                jnp.maximum(scores[0], scores[1]), jnp.maximum(scores[2], scores[3])
            )
            old = top[...]
            new = jnp.maximum(old, jnp.max(best, axis=-1, keepdims=True))
            fade = jnp.exp2((old - new) * scale)
            weights = [jnp.exp2((s - new) * scale) for s in scores]
            added = (weights[0] + weights[1]) + (weights[2] + weights[3])
            total[...] = total[...] * fade + jnp.sum(added, axis=-1, keepdims=True)
            out = mm(weights[0].astype(BF16), kv[0, dk, 1])
            for i in range(1, 4):
                out = out + mm(weights[i].astype(BF16), kv[i, dk, 1])
            acc[...] = acc[...] * fade + out
            top[...] = new

        def step(xk, carry):
            group(xk, False)
            return carry

        lax.fori_loop(0, xq, step, 0)
        group(xq, True)
        o_ref[...] = (acc[...] / total[...]).astype(BF16)


def mix_kernel(s0, s1, s2, s3, cross, out):
    x = lax.axis_index("x")
    for d, piece in enumerate((s0, s1, s2, s3)):
        cols = pl.ds(pl.multiple_of(lax.rem(x + d, NX) * HSIZE, HSIZE), HSIZE)
        out[:, cols] = (piece[...].astype(F32) + cross[:, cols]).astype(BF16)


def head_rows(rows):
    width = rows.shape[1]
    each = width // EHEADS
    at = lax.broadcasted_iota(jnp.int32, (1, width), 1)
    parts = []
    for h in range(EHEADS):
        keep = jnp.where((at >= h * each) & (at < (h + 1) * each), 1.0, 0.0).astype(BF16)
        parts.append(rows * keep)
    return jnp.concatenate(parts, axis=0)


def encode_kernel(
    ids, nb, ctx, wq_h, wk_h, wv_h, wo_h, enc, wt, ek_out, ev_out, wq, wk, wv, wo, sems
):
    copies = [
        pltpu.make_async_copy(a, b, sems.at[i])
        for i, (a, b) in enumerate(((wq_h, wq), (wk_h, wk), (wv_h, wv), (wo_h, wo)))
    ]
    for c in copies:
        c.start()
    slots, rows, width = nb.shape
    each = width // EHEADS
    x = nb[...].reshape(slots * rows, width)
    contexts = []
    for t in range(slots):
        mine = (lax.axis_index("z") * 2 + lax.axis_index("yh")) * slots + t
        span = jnp.int32(0)
        for c in range(1, ids.shape[0]):
            span = jnp.where((ids[c, 0] == mine) | (ids[c, 1] == mine), c, span)
        contexts.append(ctx[pl.ds(pl.multiple_of(span * CL, CL), CL), :])
    m = jnp.concatenate(contexts, axis=0)
    copies[0].wait()
    eq = mm(x, wq[...]).astype(BF16)
    copies[1].wait()
    ek = mm(m, wk[...]).astype(BF16)
    copies[2].wait()
    ev = mm(m, wv[...]).astype(BF16)
    mixed = []
    for t in range(slots):
        ek_t = ek[t * CL : (t + 1) * CL]
        ev_t = ev[t * CL : (t + 1) * CL]
        ek_out[t] = ek_t
        ev_out[t] = ev_t
        s = mm_nt(head_rows(ek_t), eq[t * rows : (t + 1) * rows]) * (1.0 / math.sqrt(each))
        s = s.reshape(EHEADS, CL, rows)
        p = jnp.exp(s - jnp.max(s, axis=1, keepdims=True))
        w = (p / jnp.sum(p, axis=1, keepdims=True)).reshape(EHEADS * CL, rows)
        wt[t] = w
        mixed.append(mm_tn(w.astype(BF16), head_rows(ev_t)).astype(BF16))
    copies[3].wait()
    out = x.astype(F32) + mm(jnp.concatenate(mixed, axis=0), wo[...])
    enc[...] = out.astype(BF16).reshape(slots, rows, width)


def pullback_kernel(d0, d1, d2, d3, wt, ek, ev, wq_h, wo_h, out, wq, wo, sems):
    load_o = pltpu.make_async_copy(wo_h, wo, sems.at[0])
    load_q = pltpu.make_async_copy(wq_h, wq, sems.at[1])
    load_o.start()
    load_q.start()
    slots, rows, width = d0.shape
    each = width // EHEADS
    d = (d0[...].astype(F32) + d1[...].astype(F32)) + (d2[...].astype(F32) + d3[...].astype(F32))
    d = d.reshape(slots * rows, width)
    load_o.wait()
    de = mm(d.astype(BF16), wo[...]).astype(BF16)
    back = []
    for t in range(slots):
        w = wt[t]
        dw = mm_nt(head_rows(ev[t]), de[t * rows : (t + 1) * rows])
        dw = dw.astype(BF16).astype(F32).reshape(EHEADS, CL, rows)
        w = w.reshape(EHEADS, CL, rows)
        ds = w * (dw - jnp.sum(w * dw, axis=1, keepdims=True)) * (1.0 / math.sqrt(each))
        ds = ds.reshape(EHEADS * CL, rows).astype(BF16)
        back.append(mm_tn(ds, head_rows(ek[t])).astype(BF16))
    load_q.wait()
    out[...] = (d + mm(jnp.concatenate(back, axis=0), wq[...])).reshape(slots, rows, width)


def prep_kernel(kw, vw, wq, wo, q, g, kw_t, vw_t, wq_t, wo_t, qm_t, gm_t):
    kw_t[...] = kw[...].T
    vw_t[...] = vw[...].T
    wq_t[...] = wq[...].T
    wo_t[...] = wo[...].T
    for c in range(qm_t.shape[0]):
        qm_t[c] = head_blocks(q[c * CL : (c + 1) * CL]).T
        gm_t[c] = head_blocks(g[c * CL : (c + 1) * CL]).T


def head_blocks(rows):
    width = rows.shape[1]
    at = lax.broadcasted_iota(jnp.int32, (1, width), 1)
    parts = []
    for h in range(width // HSIZE):
        keep = jnp.where((at >= h * HSIZE) & (at < (h + 1) * HSIZE), 1.0, 0.0).astype(BF16)
        parts.append(rows * keep)
    return jnp.concatenate(parts, axis=0)


def cross_kernel(ids, e00, e01, e10, e11, e20, e21, e30, e31, *rest):
    blocks = (e00, e01, e10, e11, e20, e21, e30, e31)
    q, g, qm_t, gm_t, kw, vw, kw_t, vw_t, cross = rest[:9]
    outs, (table, held, sent, dk, dv, zero, in_sem, out_sem) = rest[9:17], rest[17:]
    z, yh = lax.axis_index("z"), lax.axis_index("yh")
    n_named = held.shape[0]
    spans = n_named // 2
    scale = 1.0 / math.sqrt(HSIZE)

    for i in range(16):
        table[i] = jnp.int32(-1)
    for n in range(n_named):
        slot = ids[n // 2, n % 2]
        dz = lax.rem(slot // 4 - z + NX, NX)
        dy = jnp.bitwise_xor(lax.rem(slot // 2, 2), yh)
        table[dz * 4 + dy * 2 + lax.rem(slot, 2)] = jnp.int32(n)
    zero[...] = jnp.zeros_like(zero)
    places = [4, 5, 0, 1, 2, 3, 6, 7]
    places = [(i, t) for i in places for t in range(2)]
    for i, t in places:
        n = table[2 * i + t]

        @pl.when(n >= 0)
        def _():
            pltpu.make_async_copy(blocks[i].at[t], held.at[n], in_sem.at[n]).start()

    for i, t in places:

        @pl.when(table[2 * i + t] < 0)
        def _():
            pltpu.make_async_copy(zero, outs[i].at[t], out_sem.at[2 * i + t]).start()

    heads = q.shape[1] // HSIZE
    for half in range(2):
        first = half * (n_named // 2)
        for n in range(first, first + n_named // 2):
            pltpu.make_async_copy(e00.at[0], held.at[n], in_sem.at[n]).wait()
        e = held[first : first + n_named // 2].reshape(n_named // 2 * NL, -1)
        ck_all = mm(e, kw[...]).astype(BF16)
        cv_all = mm(e, vw[...]).astype(BF16)
        for i in range(spans // 2):
            c = half * (spans // 2) + i
            ck = ck_all[i * 2 * NL : (i + 1) * 2 * NL]
            cv = cv_all[i * 2 * NL : (i + 1) * 2 * NL]
            qm = head_blocks(q[c * CL : (c + 1) * CL])
            gm = head_blocks(g[c * CL : (c + 1) * CL])
            s = mm(ck, qm_t[c]) * scale
            dp = mm(cv, gm_t[c])
            p = jnp.exp(s - jnp.max(s, axis=0, keepdims=True))
            p = p / jnp.sum(p, axis=0, keepdims=True)
            pb = p.astype(BF16)
            ds = p * (dp - jnp.sum(p * dp, axis=0, keepdims=True)) * scale
            dk[i * 2 * NL : (i + 1) * 2 * NL] = mm(ds.astype(BF16), qm).astype(BF16)
            dv[i * 2 * NL : (i + 1) * 2 * NL] = mm(pb, gm).astype(BF16)
            o = mm_tn(pb, cv)
            for h in range(heads):
                cross[c * CL : (c + 1) * CL, h * HSIZE : (h + 1) * HSIZE] = o[
                    h * CL : (h + 1) * CL, h * HSIZE : (h + 1) * HSIZE
                ]
        de = mm(dk[...], kw_t[...]) + mm(dv[...], vw_t[...])
        sent[first : first + n_named // 2] = de.astype(BF16).reshape(n_named // 2, NL, -1)
        for i, t in places:
            n = table[2 * i + t]

            @pl.when((n >= first) & (n < first + n_named // 2))
            def _():
                pltpu.make_async_copy(sent.at[n], outs[i].at[t], out_sem.at[2 * i + t]).start()

    for i, t in places:
        pltpu.make_async_copy(zero, outs[i].at[t], out_sem.at[2 * i + t]).wait()


def shift(n, by):
    return [(i, (i + by) % n) for i in range(n)]


def local(
    self_q,
    self_k,
    self_v,
    cross_q,
    cross_k_weight,
    cross_v_weight,
    span_ctx,
    neighbours,
    neighbour_ids,
    enc_q,
    enc_k,
    enc_v,
    enc_o,
    mixed_grad,
):
    rows, width = self_q.shape
    slots, nl, ew = neighbours.shape
    spans, per_span = neighbour_ids.shape
    n_named = spans * per_span
    struct = jax.ShapeDtypeStruct
    after = lax.optimization_barrier

    enc, wt, ek, ev = call(
        encode_kernel,
        mib=56,
        out_shape=[
            struct((slots, nl, ew), BF16),
            struct((slots, EHEADS * CL, nl), F32),
            struct((slots, CL, ew), BF16),
            struct((slots, CL, ew), BF16),
        ],
        in_specs=[smem(), vmem(), vmem()] + [hbm()] * 4,
        out_specs=[vmem()] * 4,
        scratch_shapes=[pltpu.VMEM((ew, ew), BF16)] * 4 + [pltpu.SemaphoreType.DMA((4,))],
    )(neighbour_ids, neighbours, span_ctx, enc_q, enc_k, enc_v, enc_o)

    e00 = enc
    e01 = lax.ppermute(e00, "yh", shift(2, 1))
    e30 = lax.ppermute(e00, "z", shift(NX, 1))
    e10 = lax.ppermute(e00, "z", shift(NX, -1))

    self_q, self_k, self_v, _ = after((self_q, self_k, self_v, wt))
    packed = call(
        pack_kernel,
        out_shape=[struct((3, rows, HSIZE), BF16)] * NX,
        in_specs=[hbm()] * 3,
        out_specs=[hbm()] * NX,
        scratch_shapes=[pltpu.SemaphoreType.DMA((NX, 3))],
    )(self_q, self_k, self_v)
    pieces = [packed[0]] + [lax.ppermute(packed[d], "x", shift(NX, d)) for d in range(1, NX)]

    own_kv = jnp.stack([p[1:] for p in pieces])
    e01, e30, e10, own_kv = after((e01, e30, e10, own_kv))
    e11 = lax.ppermute(e01, "z", shift(NX, -1))
    e31 = lax.ppermute(e01, "z", shift(NX, 1))
    e20 = lax.ppermute(e30, "z", shift(NX, 1))
    e21 = lax.ppermute(e11, "z", shift(NX, -1))

    kv = lax.all_gather(own_kv, ("yl", "core"), axis=0)

    kw_t, vw_t, wq_t, wo_t, qm_t, gm_t = call(
        prep_kernel,
        out_shape=[struct((width, ew), BF16)] * 2
        + [struct((ew, ew), BF16)] * 2
        + [struct((spans, width, width // HSIZE * CL), BF16)] * 2,
        in_specs=[vmem()] * 6,
        out_specs=[vmem()] * 6,
    )(*after((cross_k_weight, cross_v_weight, enc_q, enc_o, cross_q, mixed_grad, wt))[:6])

    kv, e21 = after((kv, e21))
    cross, *p = call(
        cross_kernel,
        out_shape=[struct((rows, width), F32)] + [struct((slots, nl, ew), BF16)] * 8,
        in_specs=[smem()] + [hbm()] * 8 + [vmem()] * 8,
        out_specs=[vmem()] + [hbm()] * 8,
        scratch_shapes=[
            pltpu.SMEM((16,), jnp.int32),
            pltpu.VMEM((n_named, nl, ew), BF16),
            pltpu.VMEM((n_named, nl, ew), BF16),
            pltpu.VMEM((n_named // 2 * nl, width), BF16),
            pltpu.VMEM((n_named // 2 * nl, width), BF16),
            pltpu.VMEM((nl, ew), BF16),
            pltpu.SemaphoreType.DMA((n_named,)),
            pltpu.SemaphoreType.DMA((16,)),
        ],
    )(
        neighbour_ids,
        e00,
        e01,
        e10,
        e11,
        e20,
        e21,
        e30,
        e31,
        cross_q,
        mixed_grad,
        qm_t,
        gm_t,
        cross_k_weight,
        cross_v_weight,
        kw_t,
        vw_t,
    )
    p00, p01, p10, p11, p20, p21, p30, p31 = p

    def add(a, b):
        return (a.astype(F32) + b.astype(F32)).astype(BF16)

    far1 = lax.ppermute(p21, "z", shift(NX, -1))
    far0 = lax.ppermute(p20, "z", shift(NX, 1))
    up1 = lax.ppermute(p11, "z", shift(NX, 1))
    down0 = lax.ppermute(p30, "z", shift(NX, -1))
    down1 = lax.ppermute(add(p31, far1), "z", shift(NX, -1))
    up0 = lax.ppermute(add(p10, far0), "z", shift(NX, 1))
    theirs = (p01.astype(F32) + up1.astype(F32) + down1.astype(F32)).astype(BF16)
    other = lax.ppermute(theirs, "yh", shift(2, 1))

    kv, _ = after((kv, cross))
    outs = call(
        attend_kernel,
        out_shape=[struct((rows, HSIZE), BF16)] * NX,
        in_specs=[vmem()] * 5,
        out_specs=[vmem()] * NX,
        scratch_shapes=[
            pltpu.VMEM((rows, HSIZE), F32),
            pltpu.VMEM((rows, 1), F32),
            pltpu.VMEM((rows, 1), F32),
        ],
    )(*pieces, kv)
    selfs = [outs[0]] + [lax.ppermute(outs[d], "x", shift(NX, -d)) for d in range(1, NX)]

    mixed = call(
        mix_kernel,
        out_shape=struct((rows, width), BF16),
        in_specs=[vmem()] * 5,
        out_specs=vmem(),
    )(*selfs, cross)

    grad = call(
        pullback_kernel,
        out_shape=struct((slots, nl, ew), F32),
        in_specs=[vmem()] * 7 + [hbm()] * 2,
        out_specs=vmem(),
        scratch_shapes=[pltpu.VMEM((ew, ew), BF16)] * 2 + [pltpu.SemaphoreType.DMA((2,))],
    )(p00, up0, down0, other, wt, ek, ev, wq_t, wo_t)
    return mixed, grad


def solution(mesh):
    fine = Mesh(mesh.devices.reshape(4, 2, 2, 4, 2), ("x", "yl", "core", "z", "yh"))
    ctx, enc = ("x", "yl", "core"), ("z", "yh")
    tokens = P(ctx, enc)
    return jax.shard_map(
        local,
        mesh=fine,
        in_specs=(
            tokens,
            tokens,
            tokens,
            tokens,
            P(None, enc),
            P(None, enc),
            P(ctx, None),
            P(ctx + enc, None, None),
            P(ctx, None),
            P(),
            P(),
            P(),
            P(),
            tokens,
        ),
        out_specs=(tokens, P(ctx + enc, None, None)),
        check_vma=False,
    )
```

time: 271 us -> 156 us (0.58)
  matrix products: 66.5 us -> 0 us
  waiting for transfers between devices: 95.3 us -> 42.8 us
  Pallas kernels: 0 us -> 37.2 us
  other arithmetic: 37.3 us -> 1.28 us
  starting transfers between devices: 0.16 us -> 34.2 us
  local copies, waits for them, and re-layouts: 55.1 us -> 25.6 us
    all_gather x3 -> x1, waiting for transfers between devices: 90.8 us -> 2.54 us  [local(): kv = lax.all_gather(own_kv, ('yl', 'core'), axis=0)]
    dot_general x37 -> x0, matrix products: 66.5 us -> none  [the longest x8 14.6 us: one_tile(): jnp.einsum('qhd,khd->hqk', queries, key_tile, preferred_element_type=jnp....]
    ppermute x0 -> x20, waiting for transfers between devices: none -> 40.2 us  [the longest x1 8.88 us: local(): up1 = lax.ppermute(p11, 'z', shift(NX, 1))]
    pallas_call x0 -> x7, Pallas kernels: none -> 37.2 us  [the longest x1 15 us: local(): call(cross_kernel, out_shape=[struct((rows, width), F32)] + [struct((slot...]
    ppermute x0 -> x20, starting transfers between devices: none -> 34.2 us  [the longest x3 6.83 us: local(): lax.ppermute(packed[d], 'x', shift(NX, d))]
    reshape x10 -> x0, local copies, waits for them, and re-layouts: 21.6 us -> none  [the longest x1 6.95 us: local(): lax.all_gather(self_v, 'ctx', axis=0, tiled=True)]
    unnamed x53 -> x85, local copies, waits for them, and re-layouts: 5.74 us -> 25.6 us
    reduce_sum x8 -> x0, other arithmetic: 18.7 us -> none  [one_tile(): row_total = row_total * rescale + jnp.sum(weights, axis=-1)]
  transfers between devices with their start and end apart: 4 -> 21, of which waited for: 3 -> 12; matrix products, arithmetic and copies ran while one was open for 49% -> 1% of each run, Pallas kernels for 0% -> 7%
where the time goes in v1:
time: 156 us; the launch traced here: 155 us
  waiting for transfers between devices  42.8 us (27%)
  Pallas kernels  37.2 us (24%)
  starting transfers between devices  34.2 us (22%)
  local copies, waits for them, and re-layouts  25.6 us (16%)
  between operations  14.4 us (9%)
    unnamed x85, local copies, waits for them, and re-layouts  25.6 us
    pallas_call x1, Pallas kernels, local(): call(cross_kernel, out_shape=[struct((rows, width), F32)] + [struct((slot...  15 us
    ppermute x1, waiting for transfers between devices, local(): up1 = lax.ppermute(p11, 'z', shift(NX, 1))  8.88 us
    pallas_call x1, Pallas kernels, local(): call(attend_kernel, out_shape=[struct((rows, HSIZE), BF16)] * NX, in_spec...  8.28 us
    ppermute x1, waiting for transfers between devices, local(): e11 = lax.ppermute(e01, 'z', shift(NX, -1))  7.66 us
    pallas_call x1, Pallas kernels, local(): call(encode_kernel, mib=56, out_shape=[struct((slots, nl, ew), BF16), str...  6.89 us
    ppermute x3, starting transfers between devices, local(): lax.ppermute(packed[d], 'x', shift(NX, d))  6.83 us
    ppermute x1, waiting for transfers between devices, local(): far1 = lax.ppermute(p21, 'z', shift(NX, -1))  6.59 us
  transfers between devices with their start and end apart: 21, of which 12 were waited for; matrix products, arithmetic and copies ran while one was open for 1% of the time, Pallas kernels for 7%

profile of v1, /device:TPU:0, one launch (start us, length us, event | category | flops | bytes accessed | tf_op | source)
XLA Modules:
  0.0 155.5 jit_solution(11281247559299205269)
XLA Ops:
  7.2 1.4 copy.18.ids
  8.6 6.9 %shard_map.149 = (bf16[2,128,896]{2,1,0:T(8,128)(2,1)}, f32[2,256,128]{2,1,0:T(8,128)}, bf16[2,64,896]{2,1,0:T(8,128)(2,1)}, bf16[2,64,896]{2,1,0:T(8,128)(2,1)}) custom-call(s32[4,2]{1,0:T(4,128)} %copy.18.ids, bf16[2,128,896]{2,1,0:T(8,128)(2,1)} %nb.1, bf16[256,896]{1,0:T(8,128)(2,1)} %ctx.1, bf16[896,896]{1,0:T(8,128)(2,1)} %wq, bf16[896,896]{1,0:T(8,128)(2,1)} %wk_h.1, ...), custom_call_target="tpu_custom_call" | custom-call | tf_op jit(solution)/shard_map/pallas_call | solution.py:319
  15.5 4.2 %collective-permute-start.5 = (bf16[2,128,896]{2,1,0:T(8,128)(2,1)}, bf16[2,128,896]{2,1,0:T(8,128)(2,1)}, u32[]{:S(2)}, u32[]{:S(2)}) collective-permute-start(bf16[2,128,896]{2,1,0:T(8,128)(2,1)} %get-tuple-element.53.e00), channel_id=1, source_target_pairs={{0,6},{2,0},{4,2},{6,4},{1,7},{3,1},{5,3},{7,5},{8,14},{10,8},{12,... | collective-permute-start | bytes 1376264 | tf_op jit(solution)/shard_map/ppermute | solution.py:336
  19.7 3.2 %collective-permute-start.3 = (bf16[2,128,896]{2,1,0:T(8,128)(2,1)}, bf16[2,128,896]{2,1,0:T(8,128)(2,1)}, u32[]{:S(2)}, u32[]{:S(2)}) collective-permute-start(bf16[2,128,896]{2,1,0:T(8,128)(2,1)} %get-tuple-element.53.e00), channel_id=1, source_target_pairs={{0,1},{1,0},{2,3},{3,2},{4,5},{5,4},{6,7},{7,6},{8,9},{9,8},{10,11... | collective-permute-start | bytes 1376264 | tf_op jit(solution)/shard_map/ppermute | solution.py:334
  22.9 0.3 shard_map.150
  23.2 1.6 %collective-permute-start = (bf16[3,256,128]{2,1,0:T(8,128)(2,1)S(1)}, bf16[3,256,128]{2,1,0:T(8,128)(2,1)S(1)}, u32[]{:S(2)}, u32[]{:S(2)}) collective-permute-start(bf16[3,256,128]{2,1,0:T(8,128)(2,1)S(1)} %get-tuple-element.50), channel_id=1, source_target_pairs={{0,32},{32,64},{64,96},{96,0},{1,33},{33,65},{65,97},{97,1},{2,34}... | collective-permute-start | bytes 589832 | tf_op jit(solution)/shard_map/ppermute | solution.py:346
  24.8 2.7 %collective-permute-start.1 = (bf16[3,256,128]{2,1,0:T(8,128)(2,1)S(1)}, bf16[3,256,128]{2,1,0:T(8,128)(2,1)S(1)}, u32[]{:S(2)}, u32[]{:S(2)}) collective-permute-start(bf16[3,256,128]{2,1,0:T(8,128)(2,1)S(1)} %get-tuple-element.51), channel_id=1, source_target_pairs={{0,64},{32,96},{64,0},{96,32},{1,65},{33,97},{65,1},{97,33},{2,66}... | collective-permute-start | bytes 589832 | tf_op jit(solution)/shard_map/ppermute | solution.py:346
  27.5 0.7 copy-done.22
  28.2 3.1 %collective-permute-done.q1 = bf16[3,256,128]{2,1,0:T(8,128)(2,1)S(1)} collective-permute-done((bf16[3,256,128]{2,1,0:T(8,128)(2,1)S(1)}, bf16[3,256,128]{2,1,0:T(8,128)(2,1)S(1)}, u32[]{:S(2)}, u32[]{:S(2)}) %collective-permute-start) | collective-permute-done | bytes 196640 | tf_op jit(solution)/shard_map/ppermute | solution.py:346
  31.3 2.5 %collective-permute-start.2 = (bf16[3,256,128]{2,1,0:T(8,128)(2,1)S(1)}, bf16[3,256,128]{2,1,0:T(8,128)(2,1)S(1)}, u32[]{:S(2)}, u32[]{:S(2)}) collective-permute-start(bf16[3,256,128]{2,1,0:T(8,128)(2,1)S(1)} %get-tuple-element.52), channel_id=1, source_target_pairs={{0,96},{32,0},{64,32},{96,64},{1,97},{33,1},{65,33},{97,65},{2,98}... | collective-permute-start | bytes 589832 | tf_op jit(solution)/shard_map/ppermute | solution.py:346
  33.9 0.7 copy-done.24
  34.5 1.2 collective-permute-done.1.q2
  35.8 0.7 copy-done.26
  36.4 0.6 collective-permute-done.2.q3
  37.1 0.7 copy-done.28
  37.7 0.9 pad_maximum_fusion
  38.7 3.3 %collective-permute-start.6 = (bf16[2,128,896]{2,1,0:T(8,128)(2,1)}, bf16[2,128,896]{2,1,0:T(8,128)(2,1)S(1)}, u32[]{:S(2)}, u32[]{:S(2)}) collective-permute-start(bf16[2,128,896]{2,1,0:T(8,128)(2,1)} %collective-permute-done.3.e01), channel_id=1, source_target_pairs={{0,6},{2,0},{4,2},{6,4},{1,7},{3,1},{5,3},{7,5},{8,14},{10,8},{12,... | collective-permute-start | bytes 1376264 | tf_op jit(solution)/shard_map/ppermute | solution.py:350
  42.0 7.7 %collective-permute-done.6.e11 = bf16[2,128,896]{2,1,0:T(8,128)(2,1)S(1)} collective-permute-done((bf16[2,128,896]{2,1,0:T(8,128)(2,1)}, bf16[2,128,896]{2,1,0:T(8,128)(2,1)S(1)}, u32[]{:S(2)}, u32[]{:S(2)}) %collective-permute-start.6) | collective-permute-done | bytes 458784 | tf_op jit(solution)/shard_map/ppermute | solution.py:350
  49.6 3.4 %collective-permute-start.7 = (bf16[2,128,896]{2,1,0:T(8,128)(2,1)S(1)}, bf16[2,128,896]{2,1,0:T(8,128)(2,1)S(1)}, u32[]{:S(2)}, u32[]{:S(2)}) collective-permute-start(bf16[2,128,896]{2,1,0:T(8,128)(2,1)S(1)} %collective-permute-done.6.e11), channel_id=1, source_target_pairs={{0,6},{2,0},{4,2},{6,4},{1,7},{3,1},{5,3},{7,5},{8,14},{10,8},{12,... | collective-permute-start | bytes 1376264 | tf_op jit(solution)/shard_map/ppermute | solution.py:353
  53.0 1.2 copy-done.2
  54.2 1.2 copy-done.4
  55.4 1.0 copy-done.12
  56.3 1.9 %shard_map.151 = (bf16[512,896]{1,0:T(8,128)(2,1)S(1)}, bf16[512,896]{1,0:T(8,128)(2,1)S(1)}, bf16[896,896]{1,0:T(8,128)(2,1)S(1)}, bf16[896,896]{1,0:T(8,128)(2...) custom-call(bf16[896,512]{1,0:T(8,128)(2,1)S(1)} %copy-done.2, ...), custom_call_target="tpu_custom_call" | custom-call | tf_op jit(solution)/shard_map/pallas_call | solution.py:357
  58.3 1.2 copy-done.7
  59.4 1.2 copy-done.9
  60.6 1.0 copy-done.14
  61.6 1.0 copy-done.16
  62.6 0.9 copy-done.18
  63.5 1.0 copy-done.20
  64.5 0.8 copy-done.33
  65.3 2.5 %all-gather.3.cloned.1.call-done = bf16[16,2,256,128]{3,2,1,0:T(8,128)(2,1)} async-done(((bf16[4,2,256,128]{3,2,1,0:T(8,128)(2,1)}), bf16[16,2,256,128]{3,2,1,0:T(8,128)(2,1)}) %all-gather.3.cloned.1.call-update) | async-done | bytes 2097168 | tf_op jit(solution)/shard_map/all_gather | solution.py:355
  67.8 4.9 %collective-permute-done.9.e31 = bf16[2,128,896]{2,1,0:T(8,128)(2,1)} collective-permute-done((bf16[2,128,896]{2,1,0:T(8,128)(2,1)}, bf16[2,128,896]{2,1,0:T(8,128)(2,1)}, u32[]{:S(2)}, u32[]{:S(2)}) %collective-permute-start.9) | collective-permute-done | bytes 458784 | tf_op jit(solution)/shard_map/ppermute | solution.py:351
  72.8 1.2 copy-done.3
  73.9 1.2 copy-done.5
  75.1 0.9 copy-done.13
  76.1 1.2 copy-done.15
  77.3 1.2 copy-done.17
  78.5 1.2 copy-done.19
  79.7 1.2 copy-done.21
  80.9 1.0 copy-done.30
  81.9 1.0 copy-done.32
  82.9 1.0 copy-done.34
  83.9 15.0 %shard_map.152 = (f32[256,512]{1,0:T(8,128)S(1)}, bf16[2,128,896]{2,1,0:T(8,128)(2,1)S(1)}, bf16[2,128,896]{2,1,0:T(8,128)(2,1)S(1)}, bf16[2,128,896]{2,1,0:T(8,...) custom-call(s32[4,2]{1,0:T(4,128)S(1)} %copy-done.41, ...), custom_call_target="tpu_custom_call" | custom-call | tf_op jit(solution)/shard_map/pallas_call | solution.py:367
  98.9 0.1 collective-permute-start.17
  99.0 2.0 %collective-permute-start.13 = (bf16[2,128,896]{2,1,0:T(8,128)(2,1)S(1)}, bf16[2,128,896]{2,1,0:T(8,128)(2,1)S(1)}, u32[]{:S(2)}, u32[]{:S(2)}) collective-permute-start(bf16[2,128,896]{2,1,0:T(8,128)(2,1)S(1)} %get-tuple-element.78), channel_id=1, source_target_pairs={{0,2},{2,4},{4,6},{6,0},{1,3},{3,5},{5,7},{7,1},{8,10},{10,12},{12... | collective-permute-start | bytes 1376264 | tf_op jit(solution)/shard_map/ppermute | solution.py:407
  101.1 6.6 %collective-permute-done.17 = bf16[2,128,896]{2,1,0:T(8,128)(2,1)S(1)} collective-permute-done((bf16[2,128,896]{2,1,0:T(8,128)(2,1)S(1)}, bf16[2,128,896]{2,1,0:T(8,128)(2,1)S(1)}, u32[]{:S(2)}, u32[]{:S(2)}) %collective-permute-start.17) | collective-permute-done | bytes 458784 | tf_op jit(solution)/shard_map/ppermute | solution.py:406
  107.7 0.1 add_convert_fusion.1
  107.8 3.8 %collective-permute-start.18 = (bf16[2,128,896]{2,1,0:T(8,128)(2,1)S(1)}, bf16[2,128,896]{2,1,0:T(8,128)(2,1)S(1)}, u32[]{:S(2)}, u32[]{:S(2)}) collective-permute-start(bf16[2,128,896]{2,1,0:T(8,128)(2,1)S(1)} %add_convert_fusion.1), channel_id=1, source_target_pairs={{0,6},{2,0},{4,2},{6,4},{1,7},{3,1},{5,3},{7,5},{8,14},{10,8},{12,... | collective-permute-start | bytes 1376264 | tf_op jit(solution)/shard_map/ppermute | solution.py:410
  111.6 0.1 collective-permute-start.15
  111.6 2.1 %collective-permute-done.13 = bf16[2,128,896]{2,1,0:T(8,128)(2,1)S(1)} collective-permute-done((bf16[2,128,896]{2,1,0:T(8,128)(2,1)S(1)}, bf16[2,128,896]{2,1,0:T(8,128)(2,1)S(1)}, u32[]{:S(2)}, u32[]{:S(2)}) %collective-permute-start.13) | collective-permute-done | bytes 458784 | tf_op jit(solution)/shard_map/ppermute | solution.py:407
  113.8 0.1 add_convert_fusion.2
  113.9 0.8 collective-permute-start.14
  114.7 8.9 %collective-permute-done.16 = bf16[2,128,896]{2,1,0:T(8,128)(2,1)S(1)} collective-permute-done((bf16[2,128,896]{2,1,0:T(8,128)(2,1)S(1)}, bf16[2,128,896]{2,1,0:T(8,128)(2,1)S(1)}, u32[]{:S(2)}, u32[]{:S(2)}) %collective-permute-start.16) | collective-permute-done | bytes 458784 | tf_op jit(solution)/shard_map/ppermute | solution.py:408
  123.6 0.2 add_convert_fusion
  123.8 0.8 collective-permute-start.19
  124.6 8.3 %shard_map.153 = (bf16[256,128]{1,0:T(8,128)(2,1)S(1)}, bf16[256,128]{1,0:T(8,128)(2,1)S(1)}, bf16[256,128]{1,0:T(8,128)(2,1)S(1)}, bf16[256,128]{1,0:T(8,128)(2,1)S(1)}) custom-call(bf16[3,256,128]{2,1,0:T(8,128)(2,1)S(1)} %copy-done.23, bf16[3,256,128]{2,1,0:T(8,128)(2,1)S(1)} %copy-done.25, bf16[3,256,128]{2,1,0:T(8,128)(2,1)S(1)} %copy-done.27, ...), custom_call_target="tpu_custom_call" | custom-call | tf_op jit(solution)/shard_map/pallas_call | solution.py:416
  132.9 3.1 %collective-permute-start.10 = (bf16[256,128]{1,0:T(8,128)(2,1)S(1)}, bf16[256,128]{1,0:T(8,128)(2,1)S(1)}, u32[]{:S(2)}, u32[]{:S(2)}) collective-permute-start(bf16[256,128]{1,0:T(8,128)(2,1)S(1)} %get-tuple-element.73), channel_id=1, source_target_pairs={{0,96},{32,0},{64,32},{96,64},{1,97},{33,1},{65,33},{97,65},{2,98}... | collective-permute-start | bytes 196616 | tf_op jit(solution)/shard_map/ppermute | solution.py:427
  136.0 1.2 collective-permute-start.11
  137.2 0.7 collective-permute-done.10.s1
  137.9 1.5 collective-permute-start.12
  139.4 2.4 %collective-permute-done.11.s2 = bf16[256,128]{1,0:T(8,128)(2,1)S(1)} collective-permute-done((bf16[256,128]{1,0:T(8,128)(2,1)S(1)}, bf16[256,128]{1,0:T(8,128)(2,1)S(1)}, u32[]{:S(2)}, u32[]{:S(2)}) %collective-permute-start.11) | collective-permute-done | bytes 65568 | tf_op jit(solution)/shard_map/ppermute | solution.py:427
  141.8 1.9 %collective-permute-done.12.s3 = bf16[256,128]{1,0:T(8,128)(2,1)S(1)} collective-permute-done((bf16[256,128]{1,0:T(8,128)(2,1)S(1)}, bf16[256,128]{1,0:T(8,128)(2,1)S(1)}, u32[]{:S(2)}, u32[]{:S(2)}) %collective-permute-start.12) | collective-permute-done | bytes 65568 | tf_op jit(solution)/shard_map/ppermute | solution.py:427
  143.7 0.8 shard_map.154
  144.6 4.0 %shard_map.155 = f32[2,128,896]{2,1,0:T(8,128)} custom-call(bf16[2,128,896]{2,1,0:T(8,128)(2,1)S(1)} %get-tuple-element.76.d0, bf16[2,128,896]{2,1,0:T(8,128)(2,1)S(1)} %collective-permute-done.14.d1, bf16[2,128,896]{2,1,0:T(8,128)(2,1)S(1)} %collective-permute-done.15.d2, bf16[2,128,896]{2,1,0:T(8,128)(2,1)S(1)} %collective-permute-done.19.d3, ...), custom_call_target="tpu_custom_call" | custom-call | tf_op jit(solution)/shard_map/pallas_call | solution.py:436
  (79 shorter events, 0.3 us)
Async XLA Ops:
  7.2 60.7 %all-gather.3.cloned.1.call-start = ((), (), s32[]{:S(2)}) async-start(), calls=%async_computation | async-start | bytes 2621440 | tf_op jit(solution)/shard_map/all_gather | solution.py:355
  8.6 14.3 %copy-start.35 = (bf16[256,512]{1,0:T(8,128)(2,1)S(1)}, bf16[256,512]{1,0:T(8,128)(2,1)}, u32[]{:S(2)}) copy-start(bf16[256,512]{1,0:T(8,128)(2,1)} %q_ref) | copy-start | bytes 786436
  8.6 14.3 %copy-start.36 = (bf16[256,512]{1,0:T(8,128)(2,1)S(1)}, bf16[256,512]{1,0:T(8,128)(2,1)}, u32[]{:S(2)}) copy-start(bf16[256,512]{1,0:T(8,128)(2,1)} %k_ref) | copy-start | bytes 786436
  8.6 14.3 %copy-start.37 = (bf16[256,512]{1,0:T(8,128)(2,1)S(1)}, bf16[256,512]{1,0:T(8,128)(2,1)}, u32[]{:S(2)}) copy-start(bf16[256,512]{1,0:T(8,128)(2,1)} %v_ref) | copy-start | bytes 786436
  8.6 44.4 %copy-start.11 = (bf16[256,512]{1,0:T(8,128)(2,1)S(1)}, bf16[256,512]{1,0:T(8,128)(2,1)}, u32[]{:S(2)}) copy-start(bf16[256,512]{1,0:T(8,128)(2,1)} %rest_0_.1) | copy-start | bytes 786436
  15.5 23.1 %collective-permute-start.5 = (bf16[2,128,896]{2,1,0:T(8,128)(2,1)}, bf16[2,128,896]{2,1,0:T(8,128)(2,1)}, u32[]{:S(2)}, u32[]{:S(2)}) collective-permute-start(bf16[2,128,896]{2,1,0:T(8,128)(2,1)} %get-tuple-element.53.e00), channel_id=1, source_target_pairs={{0,6},{2,0},{4,2},{6,4},{1,7},{3,1},{5,3},{7,5},{8,14},{10,8},{12,... | collective-permute-start | bytes 1376264 | tf_op jit(solution)/shard_map/ppermute | solution.py:336
  19.7 18.9 %collective-permute-start.4 = (bf16[2,128,896]{2,1,0:T(8,128)(2,1)}, bf16[2,128,896]{2,1,0:T(8,128)(2,1)}, u32[]{:S(2)}, u32[]{:S(2)}) collective-permute-start(bf16[2,128,896]{2,1,0:T(8,128)(2,1)} %get-tuple-element.53.e00), channel_id=1, source_target_pairs={{0,2},{2,4},{4,6},{6,0},{1,3},{3,5},{5,7},{7,1},{8,10},{10,12},{12... | collective-permute-start | bytes 1376264 | tf_op jit(solution)/shard_map/ppermute | solution.py:335
  19.7 18.9 %collective-permute-start.3 = (bf16[2,128,896]{2,1,0:T(8,128)(2,1)}, bf16[2,128,896]{2,1,0:T(8,128)(2,1)}, u32[]{:S(2)}, u32[]{:S(2)}) collective-permute-start(bf16[2,128,896]{2,1,0:T(8,128)(2,1)} %get-tuple-element.53.e00), channel_id=1, source_target_pairs={{0,1},{1,0},{2,3},{3,2},{4,5},{5,4},{6,7},{7,6},{8,9},{9,8},{10,11... | collective-permute-start | bytes 1376264 | tf_op jit(solution)/shard_map/ppermute | solution.py:334
  22.9 30.1 %copy-start = (bf16[896,896]{1,0:T(8,128)(2,1)S(1)}, bf16[896,896]{1,0:T(8,128)(2,1)}, u32[]{:S(2)}) copy-start(bf16[896,896]{1,0:T(8,128)(2,1)} %wq) | copy-start | bytes 4816900
  22.9 30.1 %copy-start.1 = (bf16[896,896]{1,0:T(8,128)(2,1)S(1)}, bf16[896,896]{1,0:T(8,128)(2,1)}, u32[]{:S(2)}) copy-start(bf16[896,896]{1,0:T(8,128)(2,1)} %wo) | copy-start | bytes 4816900
  23.2 8.1 %collective-permute-start = (bf16[3,256,128]{2,1,0:T(8,128)(2,1)S(1)}, bf16[3,256,128]{2,1,0:T(8,128)(2,1)S(1)}, u32[]{:S(2)}, u32[]{:S(2)}) collective-permute-start(bf16[3,256,128]{2,1,0:T(8,128)(2,1)S(1)} %get-tuple-element.50), channel_id=1, source_target_pairs={{0,32},{32,64},{64,96},{96,0},{1,33},{33,65},{65,97},{97,1},{2,34}... | collective-permute-start | bytes 589832 | tf_op jit(solution)/shard_map/ppermute | solution.py:346
  24.8 11.0 %collective-permute-start.1 = (bf16[3,256,128]{2,1,0:T(8,128)(2,1)S(1)}, bf16[3,256,128]{2,1,0:T(8,128)(2,1)S(1)}, u32[]{:S(2)}, u32[]{:S(2)}) collective-permute-start(bf16[3,256,128]{2,1,0:T(8,128)(2,1)S(1)} %get-tuple-element.51), channel_id=1, source_target_pairs={{0,64},{32,96},{64,0},{96,32},{1,65},{33,97},{65,1},{97,33},{2,66}... | collective-permute-start | bytes 589832 | tf_op jit(solution)/shard_map/ppermute | solution.py:346
  27.5 0.7 copy-start.22
  31.3 5.7 %collective-permute-start.2 = (bf16[3,256,128]{2,1,0:T(8,128)(2,1)S(1)}, bf16[3,256,128]{2,1,0:T(8,128)(2,1)S(1)}, u32[]{:S(2)}, u32[]{:S(2)}) collective-permute-start(bf16[3,256,128]{2,1,0:T(8,128)(2,1)S(1)} %get-tuple-element.52), channel_id=1, source_target_pairs={{0,96},{32,0},{64,32},{96,64},{1,97},{33,1},{65,33},{97,65},{2,98}... | collective-permute-start | bytes 589832 | tf_op jit(solution)/shard_map/ppermute | solution.py:346
  33.9 0.7 copy-start.24
  35.8 0.7 copy-start.26
  37.1 0.7 copy-start.28
  38.6 34.1 %copy-start.41 = (s32[4,2]{1,0:T(4,128)S(1)}, s32[4,2]{1,0:T(4,128)}, u32[]{:S(2)}) copy-start(s32[4,2]{1,0:T(4,128)} %copy.18.ids) | copy-start | bytes 100
  38.7 11.0 %collective-permute-start.6 = (bf16[2,128,896]{2,1,0:T(8,128)(2,1)}, bf16[2,128,896]{2,1,0:T(8,128)(2,1)S(1)}, u32[]{:S(2)}, u32[]{:S(2)}) collective-permute-start(bf16[2,128,896]{2,1,0:T(8,128)(2,1)} %collective-permute-done.3.e01), channel_id=1, source_target_pairs={{0,6},{2,0},{4,2},{6,4},{1,7},{3,1},{5,3},{7,5},{8,14},{10,8},{12,... | collective-permute-start | bytes 1376264 | tf_op jit(solution)/shard_map/ppermute | solution.py:350
  49.6 8.6 %copy-start.31 = (bf16[2,128,896]{2,1,0:T(8,128)(2,1)}, bf16[2,128,896]{2,1,0:T(8,128)(2,1)S(1)}, u32[]{:S(2)}) copy-start(bf16[2,128,896]{2,1,0:T(8,128)(2,1)S(1)} %collective-permute-done.6.e11) | copy-start | bytes 1376260
  49.6 14.9 %collective-permute-start.7 = (bf16[2,128,896]{2,1,0:T(8,128)(2,1)S(1)}, bf16[2,128,896]{2,1,0:T(8,128)(2,1)S(1)}, u32[]{:S(2)}, u32[]{:S(2)}) collective-permute-start(bf16[2,128,896]{2,1,0:T(8,128)(2,1)S(1)} %collective-permute-done.6.e11), channel_id=1, source_target_pairs={{0,6},{2,0},{4,2},{6,4},{1,7},{3,1},{5,3},{7,5},{8,14},{10,8},{12,... | collective-permute-start | bytes 1376264 | tf_op jit(solution)/shard_map/ppermute | solution.py:353
  53.0 14.9 %collective-permute-start.8 = (bf16[2,128,896]{2,1,0:T(8,128)(2,1)}, bf16[2,128,896]{2,1,0:T(8,128)(2,1)}, u32[]{:S(2)}, u32[]{:S(2)}) collective-permute-start(bf16[2,128,896]{2,1,0:T(8,128)(2,1)} %collective-permute-done.4.e30), channel_id=1, source_target_pairs={{0,2},{2,4},{4,6},{6,0},{1,3},{3,5},{5,7},{7,1},{8,10},{10,12},{12... | collective-permute-start | bytes 1376264 | tf_op jit(solution)/shard_map/ppermute | solution.py:352
  53.0 19.8 %collective-permute-start.9 = (bf16[2,128,896]{2,1,0:T(8,128)(2,1)}, bf16[2,128,896]{2,1,0:T(8,128)(2,1)}, u32[]{:S(2)}, u32[]{:S(2)}) collective-permute-start(bf16[2,128,896]{2,1,0:T(8,128)(2,1)} %collective-permute-done.3.e01), channel_id=1, source_target_pairs={{0,2},{2,4},{4,6},{6,0},{1,3},{3,5},{5,7},{7,1},{8,10},{10,12},{12... | collective-permute-start | bytes 1376264 | tf_op jit(solution)/shard_map/ppermute | solution.py:351
  53.0 1.2 copy-start.2
  54.2 1.2 copy-start.4
  55.4 1.0 copy-start.12
  58.2 1.2 copy-start.7
  59.4 1.2 copy-start.9
  60.6 1.0 copy-start.14
  61.6 1.0 copy-start.16
  62.6 0.9 copy-start.18
  63.5 1.0 copy-start.20
  64.5 0.8 copy-start.33
  72.8 1.2 copy-start.3
  73.9 1.2 copy-start.5
  75.1 0.9 copy-start.13
  76.1 1.2 copy-start.15
  77.3 1.2 copy-start.17
  78.5 1.2 copy-start.19
  79.7 1.2 copy-start.21
  80.9 1.0 copy-start.30
  81.9 1.0 copy-start.32
  82.9 1.0 copy-start.34
  98.9 8.7 %collective-permute-start.17 = (bf16[2,128,896]{2,1,0:T(8,128)(2,1)S(1)}, bf16[2,128,896]{2,1,0:T(8,128)(2,1)S(1)}, u32[]{:S(2)}, u32[]{:S(2)}) collective-permute-start(bf16[2,128,896]{2,1,0:T(8,128)(2,1)S(1)} %get-tuple-element.83), channel_id=1, source_target_pairs={{0,6},{2,0},{4,2},{6,4},{1,7},{3,1},{5,3},{7,5},{8,14},{10,8},{12,... | collective-permute-start | bytes 1376264 | tf_op jit(solution)/shard_map/ppermute | solution.py:406
  99.0 14.7 %collective-permute-start.13 = (bf16[2,128,896]{2,1,0:T(8,128)(2,1)S(1)}, bf16[2,128,896]{2,1,0:T(8,128)(2,1)S(1)}, u32[]{:S(2)}, u32[]{:S(2)}) collective-permute-start(bf16[2,128,896]{2,1,0:T(8,128)(2,1)S(1)} %get-tuple-element.78), channel_id=1, source_target_pairs={{0,2},{2,4},{4,6},{6,0},{1,3},{3,5},{5,7},{7,1},{8,10},{10,12},{12... | collective-permute-start | bytes 1376264 | tf_op jit(solution)/shard_map/ppermute | solution.py:407
  101.0 22.6 %collective-permute-start.16 = (bf16[2,128,896]{2,1,0:T(8,128)(2,1)S(1)}, bf16[2,128,896]{2,1,0:T(8,128)(2,1)S(1)}, u32[]{:S(2)}, u32[]{:S(2)}) collective-permute-start(bf16[2,128,896]{2,1,0:T(8,128)(2,1)S(1)} %get-tuple-element.81), channel_id=1, source_target_pairs={{0,2},{2,4},{4,6},{6,0},{1,3},{3,5},{5,7},{7,1},{8,10},{10,12},{12... | collective-permute-start | bytes 1376264 | tf_op jit(solution)/shard_map/ppermute | solution.py:408
  107.8 15.8 %collective-permute-start.18 = (bf16[2,128,896]{2,1,0:T(8,128)(2,1)S(1)}, bf16[2,128,896]{2,1,0:T(8,128)(2,1)S(1)}, u32[]{:S(2)}, u32[]{:S(2)}) collective-permute-start(bf16[2,128,896]{2,1,0:T(8,128)(2,1)S(1)} %add_convert_fusion.1), channel_id=1, source_target_pairs={{0,6},{2,0},{4,2},{6,4},{1,7},{3,1},{5,3},{7,5},{8,14},{10,8},{12,... | collective-permute-start | bytes 1376264 | tf_op jit(solution)/shard_map/ppermute | solution.py:410
  111.6 33.0 %collective-permute-start.15 = (bf16[2,128,896]{2,1,0:T(8,128)(2,1)S(1)}, bf16[2,128,896]{2,1,0:T(8,128)(2,1)S(1)}, u32[]{:S(2)}, u32[]{:S(2)}) collective-permute-start(bf16[2,128,896]{2,1,0:T(8,128)(2,1)S(1)} %get-tuple-element.79), channel_id=1, source_target_pairs={{0,6},{2,0},{4,2},{6,4},{1,7},{3,1},{5,3},{7,5},{8,14},{10,8},{12,... | collective-permute-start | bytes 1376264 | tf_op jit(solution)/shard_map/ppermute | solution.py:409
  113.8 10.8 %copy-start.6 = (bf16[16,2,256,128]{3,2,1,0:T(8,128)(2,1)S(1)}, bf16[16,2,256,128]{3,2,1,0:T(8,128)(2,1)}, u32[]{:S(2)}) copy-start(bf16[16,2,256,128]{3,2,1,0:T(8,128)(2,1)} %all-gather.3.cloned.1.call-done) | copy-start | bytes 6291460
  113.8 10.8 %copy-start.23 = (bf16[3,256,128]{2,1,0:T(8,128)(2,1)S(1)}, bf16[3,256,128]{2,1,0:T(8,128)(2,1)}, u32[]{:S(2)}) copy-start(bf16[3,256,128]{2,1,0:T(8,128)(2,1)} %copy-done.22) | copy-start | bytes 589828
  113.8 10.8 %copy-start.25 = (bf16[3,256,128]{2,1,0:T(8,128)(2,1)S(1)}, bf16[3,256,128]{2,1,0:T(8,128)(2,1)}, u32[]{:S(2)}) copy-start(bf16[3,256,128]{2,1,0:T(8,128)(2,1)} %copy-done.24) | copy-start | bytes 589828
  113.8 10.8 %copy-start.27 = (bf16[3,256,128]{2,1,0:T(8,128)(2,1)S(1)}, bf16[3,256,128]{2,1,0:T(8,128)(2,1)}, u32[]{:S(2)}) copy-start(bf16[3,256,128]{2,1,0:T(8,128)(2,1)} %copy-done.26) | copy-start | bytes 589828
  113.8 10.8 %copy-start.29 = (bf16[3,256,128]{2,1,0:T(8,128)(2,1)S(1)}, bf16[3,256,128]{2,1,0:T(8,128)(2,1)}, u32[]{:S(2)}) copy-start(bf16[3,256,128]{2,1,0:T(8,128)(2,1)} %copy-done.28) | copy-start | bytes 589828
  113.9 30.6 %collective-permute-start.14 = (bf16[2,128,896]{2,1,0:T(8,128)(2,1)S(1)}, bf16[2,128,896]{2,1,0:T(8,128)(2,1)S(1)}, u32[]{:S(2)}, u32[]{:S(2)}) collective-permute-start(bf16[2,128,896]{2,1,0:T(8,128)(2,1)S(1)} %add_convert_fusion.2), channel_id=1, source_target_pairs={{0,2},{2,4},{4,6},{6,0},{1,3},{3,5},{5,7},{7,1},{8,10},{10,12},{12... | collective-permute-start | bytes 1376264 | tf_op jit(solution)/shard_map/ppermute | solution.py:411
  123.8 20.8 %collective-permute-start.19 = (bf16[2,128,896]{2,1,0:T(8,128)(2,1)S(1)}, bf16[2,128,896]{2,1,0:T(8,128)(2,1)S(1)}, u32[]{:S(2)}, u32[]{:S(2)}) collective-permute-start(bf16[2,128,896]{2,1,0:T(8,128)(2,1)S(1)} %add_convert_fusion), channel_id=1, source_target_pairs={{0,1},{1,0},{2,3},{3,2},{4,5},{5,4},{6,7},{7,6},{8,9},{9,8},{10,11... | collective-permute-start | bytes 1376264 | tf_op jit(solution)/shard_map/ppermute | solution.py:413
  124.6 19.9 %copy-start.8 = (bf16[896,896]{1,0:T(8,128)(2,1)S(1)}, bf16[896,896]{1,0:T(8,128)(2,1)}, u32[]{:S(2)}) copy-start(bf16[896,896]{1,0:T(8,128)(2,1)} %copy-done.7) | copy-start | bytes 4816900
  124.6 19.9 %copy-start.10 = (bf16[896,896]{1,0:T(8,128)(2,1)S(1)}, bf16[896,896]{1,0:T(8,128)(2,1)}, u32[]{:S(2)}) copy-start(bf16[896,896]{1,0:T(8,128)(2,1)} %copy-done.9) | copy-start | bytes 4816900
  124.6 19.9 %copy-start.38 = (f32[2,256,128]{2,1,0:T(8,128)S(1)}, f32[2,256,128]{2,1,0:T(8,128)}, u32[]{:S(2)}) copy-start(f32[2,256,128]{2,1,0:T(8,128)} %get-tuple-element.45.wt) | copy-start | bytes 786436
  124.6 19.9 %copy-start.39 = (bf16[2,64,896]{2,1,0:T(8,128)(2,1)S(1)}, bf16[2,64,896]{2,1,0:T(8,128)(2,1)}, u32[]{:S(2)}) copy-start(bf16[2,64,896]{2,1,0:T(8,128)(2,1)} %get-tuple-element.84.ek) | copy-start | bytes 688132
  124.6 19.9 %copy-start.40 = (bf16[2,64,896]{2,1,0:T(8,128)(2,1)S(1)}, bf16[2,64,896]{2,1,0:T(8,128)(2,1)}, u32[]{:S(2)}) copy-start(bf16[2,64,896]{2,1,0:T(8,128)(2,1)} %get-tuple-element.85.ev) | copy-start | bytes 688132
  132.9 5.0 %collective-permute-start.10 = (bf16[256,128]{1,0:T(8,128)(2,1)S(1)}, bf16[256,128]{1,0:T(8,128)(2,1)S(1)}, u32[]{:S(2)}, u32[]{:S(2)}) collective-permute-start(bf16[256,128]{1,0:T(8,128)(2,1)S(1)} %get-tuple-element.73), channel_id=1, source_target_pairs={{0,96},{32,0},{64,32},{96,64},{1,97},{33,1},{65,33},{97,65},{2,98}... | collective-permute-start | bytes 196616 | tf_op jit(solution)/shard_map/ppermute | solution.py:427
  136.0 5.8 %collective-permute-start.11 = (bf16[256,128]{1,0:T(8,128)(2,1)S(1)}, bf16[256,128]{1,0:T(8,128)(2,1)S(1)}, u32[]{:S(2)}, u32[]{:S(2)}) collective-permute-start(bf16[256,128]{1,0:T(8,128)(2,1)S(1)} %get-tuple-element.74), channel_id=1, source_target_pairs={{0,64},{32,96},{64,0},{96,32},{1,65},{33,97},{65,1},{97,33},{2,66}... | collective-permute-start | bytes 196616 | tf_op jit(solution)/shard_map/ppermute | solution.py:427
  137.9 5.8 %collective-permute-start.12 = (bf16[256,128]{1,0:T(8,128)(2,1)S(1)}, bf16[256,128]{1,0:T(8,128)(2,1)S(1)}, u32[]{:S(2)}, u32[]{:S(2)}) collective-permute-start(bf16[256,128]{1,0:T(8,128)(2,1)S(1)} %get-tuple-element.75), channel_id=1, source_target_pairs={{0,32},{32,64},{64,96},{96,0},{1,33},{33,65},{65,97},{97,1},{2,34}... | collective-permute-start | bytes 196616 | tf_op jit(solution)/shard_map/ppermute | solution.py:427
Sparse Core Ops, SparseCore 0:
  38.8 29.0 all-gather.2

commit v2 on v1

--- a/solution.py
+++ b/solution.py
@@ -33,7 +33,7 @@
     return lax.dot_general(a, b, TN, preferred_element_type=F32)
 
 
-def call(kernel, mib=32, **kw):
+def call(kernel, mib=58, **kw):
     return pl.pallas_call(
         kernel,
         compiler_params=pltpu.CompilerParams(vmem_limit_bytes=mib * 1024 * 1024),
@@ -53,34 +53,25 @@
     return pl.BlockSpec(memory_space=pl.ANY)
 
 
-def pack_kernel(q_ref, k_ref, v_ref, o0, o1, o2, o3, sems):
-    x = lax.axis_index("x")
-    copies = []
-    for d, out in enumerate((o0, o1, o2, o3)):
-        cols = pl.ds(pl.multiple_of(lax.rem(x + d, NX) * HSIZE, HSIZE), HSIZE)
+def pack_kernel(q_ref, k_ref, v_ref, out):
+    for h in range(NX):
+        cols = slice(h * HSIZE, (h + 1) * HSIZE)
         for i, src in enumerate((q_ref, k_ref, v_ref)):
-            copies.append(pltpu.make_async_copy(src.at[:, cols], out.at[i], sems.at[d, i]))
-    for c in copies:
-        c.start()
-    for c in copies:
-        c.wait()
-
-
-def attend_kernel(q0, q1, q2, q3, kv, o0, o1, o2, o3, acc, top, total):
-    x = lax.axis_index("x")
+            out[h, i] = src[:, cols]
+
+
+def attend_kernel(pieces, kv, out, acc, top, total):
     r = lax.axis_index("yl") * 2 + lax.axis_index("core")
     scale = LOG2E / math.sqrt(HSIZE)
-    for d, (q_ref, o_ref) in enumerate(zip((q0, q1, q2, q3), (o0, o1, o2, o3))):
-        xq = lax.rem(x - d + NX, NX)
-        q = q_ref[0]
+    for xq in range(NX):
+        q = pieces[xq, 0]
         rows = q.shape[0]
         acc[...] = jnp.zeros_like(acc)
         top[...] = jnp.full_like(top, -1e30)
         total[...] = jnp.zeros_like(total)
 
         def group(xk, masked):
-            dk = lax.rem(x - xk + NX, NX)
-            scores = [mm_nt(q, kv[i, dk, 0]) for i in range(4)]
+            scores = [mm_nt(q, kv[i, xk, 0]) for i in range(4)]
             if masked:
                 at = lax.broadcasted_iota(jnp.int32, (rows, rows), 1)
                 upto = lax.broadcasted_iota(jnp.int32, (rows, rows), 0)
@@ -97,26 +88,22 @@
             weights = [jnp.exp2((s - new) * scale) for s in scores]
             added = (weights[0] + weights[1]) + (weights[2] + weights[3])
             total[...] = total[...] * fade + jnp.sum(added, axis=-1, keepdims=True)
-            out = mm(weights[0].astype(BF16), kv[0, dk, 1])
+            out = mm(weights[0].astype(BF16), kv[0, xk, 1])
             for i in range(1, 4):
-                out = out + mm(weights[i].astype(BF16), kv[i, dk, 1])
+                out = out + mm(weights[i].astype(BF16), kv[i, xk, 1])
             acc[...] = acc[...] * fade + out
             top[...] = new
 
-        def step(xk, carry):
+        for xk in range(xq):
             group(xk, False)
-            return carry
-
-        lax.fori_loop(0, xq, step, 0)
         group(xq, True)
-        o_ref[...] = (acc[...] / total[...]).astype(BF16)
-
-
-def mix_kernel(s0, s1, s2, s3, cross, out):
-    x = lax.axis_index("x")
-    for d, piece in enumerate((s0, s1, s2, s3)):
-        cols = pl.ds(pl.multiple_of(lax.rem(x + d, NX) * HSIZE, HSIZE), HSIZE)
-        out[:, cols] = (piece[...].astype(F32) + cross[:, cols]).astype(BF16)
+        out[xq] = (acc[...] / total[...]).astype(BF16)
+
+
+def mix_kernel(pieces, cross, out):
+    for h in range(NX):
+        cols = slice(h * HSIZE, (h + 1) * HSIZE)
+        out[:, cols] = (pieces[h].astype(F32) + cross[:, cols]).astype(BF16)
 
 
 def head_rows(rows):
@@ -131,30 +118,31 @@
 
 
 def encode_kernel(
-    ids, nb, ctx, wq_h, wk_h, wv_h, wo_h, enc, wt, ek_out, ev_out, wq, wk, wv, wo, sems
+    ids, nb_h, ctx_h, wq_h, wk_h, wv_h, wo_h, enc, wt, ek_out, ev_out, *scratch
 ):
-    copies = [
-        pltpu.make_async_copy(a, b, sems.at[i])
-        for i, (a, b) in enumerate(((wq_h, wq), (wk_h, wk), (wv_h, wv), (wo_h, wo)))
-    ]
+    nb, ctx, wq, wk, wv, wo, sems = scratch
+    both = ((nb_h, nb), (wq_h, wq), (ctx_h, ctx), (wk_h, wk), (wv_h, wv), (wo_h, wo))
+    copies = [pltpu.make_async_copy(a, b, sems.at[i]) for i, (a, b) in enumerate(both)]
     for c in copies:
         c.start()
     slots, rows, width = nb.shape
     each = width // EHEADS
+    copies[0].wait()
     x = nb[...].reshape(slots * rows, width)
+    copies[1].wait()
+    eq = mm(x, wq[...]).astype(BF16)
+    copies[2].wait()
     contexts = []
     for t in range(slots):
         mine = (lax.axis_index("z") * 2 + lax.axis_index("yh")) * slots + t
         span = jnp.int32(0)
-        for c in range(1, ids.shape[0]):
-            span = jnp.where((ids[c, 0] == mine) | (ids[c, 1] == mine), c, span)
+        for c in range(1, ids.shape[1]):
+            span = jnp.where((ids[0, c] == mine) | (ids[1, c] == mine), c, span)
         contexts.append(ctx[pl.ds(pl.multiple_of(span * CL, CL), CL), :])
     m = jnp.concatenate(contexts, axis=0)
-    copies[0].wait()
-    eq = mm(x, wq[...]).astype(BF16)
-    copies[1].wait()
+    copies[3].wait()
     ek = mm(m, wk[...]).astype(BF16)
-    copies[2].wait()
+    copies[4].wait()
     ev = mm(m, wv[...]).astype(BF16)
     mixed = []
     for t in range(slots):
@@ -168,7 +156,7 @@
         w = (p / jnp.sum(p, axis=1, keepdims=True)).reshape(EHEADS * CL, rows)
         wt[t] = w
         mixed.append(mm_tn(w.astype(BF16), head_rows(ev_t)).astype(BF16))
-    copies[3].wait()
+    copies[5].wait()
     out = x.astype(F32) + mm(jnp.concatenate(mixed, axis=0), wo[...])
     enc[...] = out.astype(BF16).reshape(slots, rows, width)
 
@@ -219,8 +207,15 @@
 
 def cross_kernel(ids, e00, e01, e10, e11, e20, e21, e30, e31, *rest):
     blocks = (e00, e01, e10, e11, e20, e21, e30, e31)
-    q, g, qm_t, gm_t, kw, vw, kw_t, vw_t, cross = rest[:9]
-    outs, (table, held, sent, dk, dv, zero, in_sem, out_sem) = rest[9:17], rest[17:]
+    given, cross, outs = rest[:8], rest[8], rest[9:17]
+    table, held, sent, dk, dv, zero, in_sem, out_sem, given_sem = rest[17:26]
+    here = rest[26:]
+    kw, vw, qm_t, gm_t, q, g, kw_t, vw_t = here
+    loads = [
+        pltpu.make_async_copy(a, b, given_sem.at[i]) for i, (a, b) in enumerate(zip(given, here))
+    ]
+    loads[0].start()
+    loads[1].start()
     z, yh = lax.axis_index("z"), lax.axis_index("yh")
     n_named = held.shape[0]
     spans = n_named // 2
@@ -229,7 +224,7 @@
     for i in range(16):
         table[i] = jnp.int32(-1)
     for n in range(n_named):
-        slot = ids[n // 2, n % 2]
+        slot = ids[n % 2, n // 2]
         dz = lax.rem(slot // 4 - z + NX, NX)
         dy = jnp.bitwise_xor(lax.rem(slot // 2, 2), yh)
         table[dz * 4 + dy * 2 + lax.rem(slot, 2)] = jnp.int32(n)
@@ -243,6 +238,8 @@
         def _():
             pltpu.make_async_copy(blocks[i].at[t], held.at[n], in_sem.at[n]).start()
 
+    for c in loads[2:]:
+        c.start()
     for i, t in places:
 
         @pl.when(table[2 * i + t] < 0)
@@ -255,8 +252,15 @@
         for n in range(first, first + n_named // 2):
             pltpu.make_async_copy(e00.at[0], held.at[n], in_sem.at[n]).wait()
         e = held[first : first + n_named // 2].reshape(n_named // 2 * NL, -1)
+        if half == 0:
+            loads[0].wait()
         ck_all = mm(e, kw[...]).astype(BF16)
+        if half == 0:
+            loads[1].wait()
         cv_all = mm(e, vw[...]).astype(BF16)
+        if half == 0:
+            for c in loads[2:6]:
+                c.wait()
         for i in range(spans // 2):
             c = half * (spans // 2) + i
             ck = ck_all[i * 2 * NL : (i + 1) * 2 * NL]
@@ -276,6 +280,9 @@
                 cross[c * CL : (c + 1) * CL, h * HSIZE : (h + 1) * HSIZE] = o[
                     h * CL : (h + 1) * CL, h * HSIZE : (h + 1) * HSIZE
                 ]
+        if half == 0:
+            loads[6].wait()
+            loads[7].wait()
         de = mm(dk[...], kw_t[...]) + mm(dv[...], vw_t[...])
         sent[first : first + n_named // 2] = de.astype(BF16).reshape(n_named // 2, NL, -1)
         for i, t in places:
@@ -316,19 +323,22 @@
     struct = jax.ShapeDtypeStruct
     after = lax.optimization_barrier
 
+    ids = neighbour_ids.T
+
     enc, wt, ek, ev = call(
         encode_kernel,
-        mib=56,
         out_shape=[
             struct((slots, nl, ew), BF16),
             struct((slots, EHEADS * CL, nl), F32),
             struct((slots, CL, ew), BF16),
             struct((slots, CL, ew), BF16),
         ],
-        in_specs=[smem(), vmem(), vmem()] + [hbm()] * 4,
+        in_specs=[smem()] + [hbm()] * 6,
         out_specs=[vmem()] * 4,
-        scratch_shapes=[pltpu.VMEM((ew, ew), BF16)] * 4 + [pltpu.SemaphoreType.DMA((4,))],
-    )(neighbour_ids, neighbours, span_ctx, enc_q, enc_k, enc_v, enc_o)
+        scratch_shapes=[pltpu.VMEM(neighbours.shape, BF16), pltpu.VMEM(span_ctx.shape, BF16)]
+        + [pltpu.VMEM((ew, ew), BF16)] * 4
+        + [pltpu.SemaphoreType.DMA((6,))],
+    )(ids, neighbours, span_ctx, enc_q, enc_k, enc_v, enc_o)
 
     e00 = enc
     e01 = lax.ppermute(e00, "yh", shift(2, 1))
@@ -338,36 +348,37 @@
     self_q, self_k, self_v, _ = after((self_q, self_k, self_v, wt))
     packed = call(
         pack_kernel,
-        out_shape=[struct((3, rows, HSIZE), BF16)] * NX,
-        in_specs=[hbm()] * 3,
-        out_specs=[hbm()] * NX,
-        scratch_shapes=[pltpu.SemaphoreType.DMA((NX, 3))],
+        out_shape=struct((NX, 3, rows, HSIZE), BF16),
+        in_specs=[vmem()] * 3,
+        out_specs=vmem(),
     )(self_q, self_k, self_v)
-    pieces = [packed[0]] + [lax.ppermute(packed[d], "x", shift(NX, d)) for d in range(1, NX)]
-
-    own_kv = jnp.stack([p[1:] for p in pieces])
-    e01, e30, e10, own_kv = after((e01, e30, e10, own_kv))
+    pieces = lax.all_to_all(packed, "x", 0, 0)
+    own_kv = pieces[:, 1:]
+
+    e01, e30, e10, packed = after((e01, e30, e10, packed))
     e11 = lax.ppermute(e01, "z", shift(NX, -1))
     e31 = lax.ppermute(e01, "z", shift(NX, 1))
-    e20 = lax.ppermute(e30, "z", shift(NX, 1))
-    e21 = lax.ppermute(e11, "z", shift(NX, -1))
-
-    kv = lax.all_gather(own_kv, ("yl", "core"), axis=0)
-
-    kw_t, vw_t, wq_t, wo_t, qm_t, gm_t = call(
+
+    weights = after((cross_k_weight, cross_v_weight, enc_q, enc_o, cross_q, mixed_grad, e01))[:6]
+    prepared = call(
         prep_kernel,
         out_shape=[struct((width, ew), BF16)] * 2
         + [struct((ew, ew), BF16)] * 2
         + [struct((spans, width, width // HSIZE * CL), BF16)] * 2,
         in_specs=[vmem()] * 6,
         out_specs=[vmem()] * 6,
-    )(*after((cross_k_weight, cross_v_weight, enc_q, enc_o, cross_q, mixed_grad, wt))[:6])
-
-    kv, e21 = after((kv, e21))
+    )(*weights)
+
+    e11, e31, e30, own_kv, *prepared = after((e11, e31, e30, own_kv, *prepared))
+    kw_t, vw_t, wq_t, wo_t, qm_t, gm_t = prepared
+    e20 = lax.ppermute(e30, "z", shift(NX, 1))
+    e21 = lax.ppermute(e11, "z", shift(NX, -1))
+    kv = lax.all_gather(own_kv, ("yl", "core"), axis=0)
+
     cross, *p = call(
         cross_kernel,
         out_shape=[struct((rows, width), F32)] + [struct((slots, nl, ew), BF16)] * 8,
-        in_specs=[smem()] + [hbm()] * 8 + [vmem()] * 8,
+        in_specs=[smem()] + [hbm()] * 16,
         out_specs=[vmem()] + [hbm()] * 8,
         scratch_shapes=[
             pltpu.SMEM((16,), jnp.int32),
@@ -378,9 +389,14 @@
             pltpu.VMEM((nl, ew), BF16),
             pltpu.SemaphoreType.DMA((n_named,)),
             pltpu.SemaphoreType.DMA((16,)),
-        ],
+            pltpu.SemaphoreType.DMA((8,)),
+        ]
+        + [pltpu.VMEM((ew, width), BF16)] * 2
+        + [pltpu.VMEM((spans, width, width // HSIZE * CL), BF16)] * 2
+        + [pltpu.VMEM((rows, width), BF16)] * 2
+        + [pltpu.VMEM((width, ew), BF16)] * 2,
     )(
-        neighbour_ids,
+        ids,
         e00,
         e01,
         e10,
@@ -389,12 +405,12 @@
         e21,
         e30,
         e31,
+        cross_k_weight,
+        cross_v_weight,
+        qm_t,
+        gm_t,
         cross_q,
         mixed_grad,
-        qm_t,
-        gm_t,
-        cross_k_weight,
-        cross_v_weight,
         kw_t,
         vw_t,
     )
@@ -405,41 +421,46 @@
 
     far1 = lax.ppermute(p21, "z", shift(NX, -1))
     far0 = lax.ppermute(p20, "z", shift(NX, 1))
-    up1 = lax.ppermute(p11, "z", shift(NX, 1))
-    down0 = lax.ppermute(p30, "z", shift(NX, -1))
-    down1 = lax.ppermute(add(p31, far1), "z", shift(NX, -1))
-    up0 = lax.ppermute(add(p10, far0), "z", shift(NX, 1))
-    theirs = (p01.astype(F32) + up1.astype(F32) + down1.astype(F32)).astype(BF16)
-    other = lax.ppermute(theirs, "yh", shift(2, 1))
-
     kv, _ = after((kv, cross))
     outs = call(
         attend_kernel,
-        out_shape=[struct((rows, HSIZE), BF16)] * NX,
-        in_specs=[vmem()] * 5,
-        out_specs=[vmem()] * NX,
+        mib=20,
+        out_shape=struct((NX, rows, HSIZE), BF16),
+        in_specs=[vmem()] * 2,
+        out_specs=vmem(),
         scratch_shapes=[
             pltpu.VMEM((rows, HSIZE), F32),
             pltpu.VMEM((rows, 1), F32),
             pltpu.VMEM((rows, 1), F32),
         ],
-    )(*pieces, kv)
-    selfs = [outs[0]] + [lax.ppermute(outs[d], "x", shift(NX, -d)) for d in range(1, NX)]
-
-    mixed = call(
-        mix_kernel,
-        out_shape=struct((rows, width), BF16),
-        in_specs=[vmem()] * 5,
-        out_specs=vmem(),
-    )(*selfs, cross)
+    )(pieces, kv)
+    far1, far0, p11, outs = after((far1, far0, p11, outs))
+    selfs = lax.all_to_all(outs, "x", 0, 0)
+    down1 = lax.ppermute(add(p31, far1), "z", shift(NX, -1))
+    up1 = lax.ppermute(p11, "z", shift(NX, 1))
+    near0 = add(p10, far0)
+    down1, up1, near0, p30, selfs = after((down1, up1, near0, p30, selfs))
+    theirs = (p01.astype(F32) + up1.astype(F32) + down1.astype(F32)).astype(BF16)
+    other = lax.ppermute(theirs, "yh", shift(2, 1))
+    up0 = lax.ppermute(near0, "z", shift(NX, 1))
+    down0 = lax.ppermute(p30, "z", shift(NX, -1))
 
     grad = call(
         pullback_kernel,
+        mib=20,
         out_shape=struct((slots, nl, ew), F32),
         in_specs=[vmem()] * 7 + [hbm()] * 2,
         out_specs=vmem(),
         scratch_shapes=[pltpu.VMEM((ew, ew), BF16)] * 2 + [pltpu.SemaphoreType.DMA((2,))],
     )(p00, up0, down0, other, wt, ek, ev, wq_t, wo_t)
+
+    mixed = call(
+        mix_kernel,
+        mib=20,
+        out_shape=struct((rows, width), BF16),
+        in_specs=[vmem()] * 2,
+        out_specs=vmem(),
+    )(selfs, cross)
     return mixed, grad
 
 

time: 156 us -> 130 us (0.83)
  local copies, waits for them, and re-layouts: 25.6 us -> 8.86 us
  waiting for transfers between devices: 42.8 us -> 31.3 us
  Pallas kernels: 37.2 us -> 40.3 us
  starting transfers between devices: 34.2 us -> 31.6 us
  other arithmetic: 1.28 us -> 3.22 us
    unnamed x85 -> x34, local copies, waits for them, and re-layouts: 25.6 us -> 8.04 us
    ppermute x7 -> x1, starting transfers between devices: 13.4 us -> 0.01 us  [local(): up0 = lax.ppermute(near0, 'z', shift(NX, 1))]
    ppermute x1, waiting for transfers between devices: 8.88 us -> 0.01 us  [local(): up1 = lax.ppermute(p11, 'z', shift(NX, 1))]
    all_to_all x0 -> x2, starting transfers between devices: none -> 8.14 us  [the longest x1 4.29 us: local(): pieces = lax.all_to_all(packed, 'x', 0, 0)]
    ppermute x1, waiting for transfers between devices: 0.01 us -> 7.85 us  [local(): e20 = lax.ppermute(e30, 'z', shift(NX, 1))]
    ppermute x7 -> x1, waiting for transfers between devices: 10 us -> 2.88 us  [local(): up0 = lax.ppermute(near0, 'z', shift(NX, 1))]
    ppermute x1, waiting for transfers between devices: 6.59 us -> 0.01 us  [local(): far1 = lax.ppermute(p21, 'z', shift(NX, -1))]
    ppermute x1, waiting for transfers between devices: 7.66 us -> 1.72 us  [local(): e11 = lax.ppermute(e01, 'z', shift(NX, -1))]
  transfers between devices with their start and end apart: 21 -> 17, of which waited for: 12 -> 9; matrix products, arithmetic and copies ran while one was open for 1% -> 1% of each run, Pallas kernels for 7% -> 23%
where the time goes in v2:
time: 130 us; the launch traced here: 129 us
  Pallas kernels  40.3 us (31%)
  starting transfers between devices  31.6 us (24%)
  waiting for transfers between devices  31.3 us (24%)
  between operations  14.1 us (11%)
  local copies, waits for them, and re-layouts  8.86 us (7%)
  other arithmetic  3.22 us (2%)
    pallas_call x1, Pallas kernels, local(): call(cross_kernel, out_shape=[struct((rows, width), F32)] + [struct((slot...  14 us
    unnamed x34, local copies, waits for them, and re-layouts  8.04 us
    ppermute x1, waiting for transfers between devices, local(): e20 = lax.ppermute(e30, 'z', shift(NX, 1))  7.85 us
    pallas_call x1, Pallas kernels, local(): call(attend_kernel, mib=20, out_shape=struct((NX, rows, HSIZE), BF16), in...  6.88 us
    pallas_call x1, Pallas kernels, local(): call(encode_kernel, out_shape=[struct((slots, nl, ew), BF16), struct((slo...  6.55 us
    pallas_call x1, Pallas kernels, local(): call(prep_kernel, out_shape=[struct((width, ew), BF16)] * 2 + [struct((ew...  6.03 us
    all_to_all x1, waiting for transfers between devices, local(): selfs = lax.all_to_all(outs, 'x', 0, 0)  5.8 us
    all_to_all x1, starting transfers between devices, local(): pieces = lax.all_to_all(packed, 'x', 0, 0)  4.29 us
  transfers between devices with their start and end apart: 17, of which 9 were waited for; matrix products, arithmetic and copies ran while one was open for 1% of the time, Pallas kernels for 23%

profile of v2, /device:TPU:0, one launch (start us, length us, event | category | flops | bytes accessed | tf_op | source)
XLA Modules:
  0.0 129.5 jit_solution(11191325880096847986)
XLA Ops:
  7.2 6.5 %shard_map.149 = (bf16[2,128,896]{2,1,0:T(8,128)(2,1)}, f32[2,256,128]{2,1,0:T(8,128)}, bf16[2,64,896]{2,1,0:T(8,128)(2,1)}, bf16[2,64,896]{2,1,0:T(8,128)(2,1)}) custom-call(s32[2,4]{1,0:T(2,128)} %bitcast.3, bf16[2,128,896]{2,1,0:T(8,128)(2,1)} %nb_h.1, bf16[256,896]{1,0:T(8,128)(2,1)} %ctx_h.1, bf16[896,896]{1,0:T(8,128)(2,1)} %wq, ...), custom_call_target="tpu_custom_call" | custom-call | tf_op jit(solution)/shard_map/pallas_call | solution.py:328
  13.7 3.4 %collective-permute-start = (bf16[2,128,896]{2,1,0:T(8,128)(2,1)}, bf16[2,128,896]{2,1,0:T(8,128)(2,1)S(1)}, u32[]{:S(2)}, u32[]{:S(2)}) collective-permute-start(bf16[2,128,896]{2,1,0:T(8,128)(2,1)} %get-tuple-element.53.e00), channel_id=1, source_target_pairs={{0,1},{1,0},{2,3},{3,2},{4,5},{5,4},{6,7},{7,6},{8,9},{9,8},{10,11... | collective-permute-start | bytes 1376264 | tf_op jit(solution)/shard_map/ppermute | solution.py:344
  17.1 1.9 %collective-permute-start.1 = (bf16[2,128,896]{2,1,0:T(8,128)(2,1)}, bf16[2,128,896]{2,1,0:T(8,128)(2,1)S(1)}, u32[]{:S(2)}, u32[]{:S(2)}) collective-permute-start(bf16[2,128,896]{2,1,0:T(8,128)(2,1)} %get-tuple-element.53.e00), channel_id=1, source_target_pairs={{0,2},{2,4},{4,6},{6,0},{1,3},{3,5},{5,7},{7,1},{8,10},{10,12},{12... | collective-permute-start | bytes 1376264 | tf_op jit(solution)/shard_map/ppermute | solution.py:345
  19.0 2.1 %collective-permute-start.2 = (bf16[2,128,896]{2,1,0:T(8,128)(2,1)}, bf16[2,128,896]{2,1,0:T(8,128)(2,1)S(1)}, u32[]{:S(2)}, u32[]{:S(2)}) collective-permute-start(bf16[2,128,896]{2,1,0:T(8,128)(2,1)} %get-tuple-element.53.e00), channel_id=1, source_target_pairs={{0,6},{2,0},{4,2},{6,4},{1,7},{3,1},{5,3},{7,5},{8,14},{10,8},{12,... | collective-permute-start | bytes 1376264 | tf_op jit(solution)/shard_map/ppermute | solution.py:346
  21.1 2.1 %shard_map.150 = bf16[4,3,256,128]{3,2,1,0:T(8,128)(2,1)} custom-call(bf16[256,512]{1,0:T(8,128)(2,1)} %q_ref, bf16[256,512]{1,0:T(8,128)(2,1)} %k_ref, bf16[256,512]{1,0:T(8,128)(2,1)} %v_ref), custom_call_target="tpu_custom_call" | custom-call | tf_op jit(solution)/shard_map/pallas_call | solution.py:349
  23.3 4.3 %all-to-all-start = ((bf16[4,3,256,128]{3,2,1,0:T(8,128)(2,1)}), bf16[4,3,256,128]{3,2,1,0:T(8,128)(2,1)S(1)}, u32[]{:S(2)}, u32[]{:S(2)}) async-start(bf16[4,3,256,128]{3,2,1,0:T(8,128)(2,1)} %shard_map.150), calls=%async_computation | async-start | bytes 1572864 | tf_op jit(solution)/shard_map/all_to_all | solution.py:355
  27.5 0.0 all-gather.3.cloned.1.call-start
  27.5 0.3 collective-permute-done.e01
  27.8 0.0 copy-start.8
  27.8 3.8 %collective-permute-done.1.e30 = bf16[2,128,896]{2,1,0:T(8,128)(2,1)S(1)} collective-permute-done((bf16[2,128,896]{2,1,0:T(8,128)(2,1)}, bf16[2,128,896]{2,1,0:T(8,128)(2,1)S(1)}, u32[]{:S(2)}, u32[]{:S(2)}) %collective-permute-start.1) | collective-permute-done | bytes 458784 | tf_op jit(solution)/shard_map/ppermute | solution.py:345
  31.6 0.0 collective-permute-done.2.e10
  31.6 2.9 %collective-permute-start.3 = (bf16[2,128,896]{2,1,0:T(8,128)(2,1)S(1)}, bf16[2,128,896]{2,1,0:T(8,128)(2,1)S(1)}, u32[]{:S(2)}, u32[]{:S(2)}) collective-permute-start(bf16[2,128,896]{2,1,0:T(8,128)(2,1)S(1)} %collective-permute-done.e01), channel_id=1, source_target_pairs={{0,6},{2,0},{4,2},{6,4},{1,7},{3,1},{5,3},{7,5},{8,14},{10,8},{12,... | collective-permute-start | bytes 1376264 | tf_op jit(solution)/shard_map/ppermute | solution.py:359
  34.5 0.0 collective-permute-start.4
  34.5 6.0 %shard_map.151 = (bf16[512,896]{1,0:T(8,128)(2,1)}, bf16[512,896]{1,0:T(8,128)(2,1)}, bf16[896,896]{1,0:T(8,128)(2,1)}, bf16[896,896]{1,0:T(8,128)(2,1)}, bf16[4...) custom-call(bf16[896,512]{1,0:T(8,128)(2,1)} %rest_0_.1, bf16[896,512]{1,0:T(8,128)(2,1)} %rest_1_.1, ...), custom_call_target="tpu_custom_call" | custom-call | tf_op jit(solution)/shard_map/pallas_call | solution.py:363
  40.6 0.0 copy-done.8
  40.6 0.0 copy-done.10
  40.6 0.0 all-to-all-done.pieces
  40.6 0.8 slice.4
  41.4 1.7 %collective-permute-done.3.e11 = bf16[2,128,896]{2,1,0:T(8,128)(2,1)S(1)} collective-permute-done((bf16[2,128,896]{2,1,0:T(8,128)(2,1)S(1)}, bf16[2,128,896]{2,1,0:T(8,128)(2,1)S(1)}, u32[]{:S(2)}, u32[]{:S(2)}) %collective-permute-start.3) | collective-permute-done | bytes 458784 | tf_op jit(solution)/shard_map/ppermute | solution.py:359
  43.1 3.4 %collective-permute-done.4.e31 = bf16[2,128,896]{2,1,0:T(8,128)(2,1)S(1)} collective-permute-done((bf16[2,128,896]{2,1,0:T(8,128)(2,1)S(1)}, bf16[2,128,896]{2,1,0:T(8,128)(2,1)S(1)}, u32[]{:S(2)}, u32[]{:S(2)}) %collective-permute-start.4) | collective-permute-done | bytes 458784 | tf_op jit(solution)/shard_map/ppermute | solution.py:360
  46.5 0.0 all-gather.3.cloned.1.call-update
  46.6 0.0 copy-done.9
  46.6 0.1 collective-permute-start.5
  46.7 3.2 %collective-permute-start.6 = (bf16[2,128,896]{2,1,0:T(8,128)(2,1)S(1)}, bf16[2,128,896]{2,1,0:T(8,128)(2,1)S(1)}, u32[]{:S(2)}, u32[]{:S(2)}) collective-permute-start(bf16[2,128,896]{2,1,0:T(8,128)(2,1)S(1)} %collective-permute-done.3.e11), channel_id=1, source_target_pairs={{0,6},{2,0},{4,2},{6,4},{1,7},{3,1},{5,3},{7,5},{8,14},{10,8},{12,... | collective-permute-start | bytes 1376264 | tf_op jit(solution)/shard_map/ppermute | solution.py:375
  49.9 7.8 %collective-permute-done.5.e20 = bf16[2,128,896]{2,1,0:T(8,128)(2,1)S(1)} collective-permute-done((bf16[2,128,896]{2,1,0:T(8,128)(2,1)S(1)}, bf16[2,128,896]{2,1,0:T(8,128)(2,1)S(1)}, u32[]{:S(2)}, u32[]{:S(2)}) %collective-permute-start.5) | collective-permute-done | bytes 458784 | tf_op jit(solution)/shard_map/ppermute | solution.py:374
  57.7 0.0 collective-permute-done.6.e21
  57.7 0.0 copy-done.11
  57.7 0.0 copy-done.13
  57.7 0.8 copy-done.15
  58.5 0.8 copy-done.16
  59.3 14.0 %shard_map.152 = (f32[256,512]{1,0:T(8,128)}, bf16[2,128,896]{2,1,0:T(8,128)(2,1)}, bf16[2,128,896]{2,1,0:T(8,128)(2,1)}, bf16[2,128,896]{2,1,0:T(8,128)(2,1)}, ...) custom-call(s32[2,4]{1,0:T(2,128)} %bitcast.4, ...), custom_call_target="tpu_custom_call" | custom-call | tf_op jit(solution)/shard_map/pallas_call | solution.py:378
  73.3 1.1 collective-permute-start.7
  74.4 1.0 collective-permute-start.8
  75.4 1.6 %copy-done = bf16[16,2,256,128]{3,2,1,0:T(8,128)(2,1)S(1)} copy-done((bf16[16,2,256,128]{3,2,1,0:T(8,128)(2,1)S(1)}, bf16[16,2,256,128]{3,2,1,0:T(8,128)(2,1)}, u32[]{:S(2)}) %copy-start) | copy-done | bytes 2097176
  77.0 6.9 %shard_map.153 = bf16[4,256,128]{2,1,0:T(8,128)(2,1)} custom-call(bf16[4,3,256,128]{3,2,1,0:T(8,128)(2,1)S(1)} %all-to-all-done.pieces, bf16[4,4,2,256,128]{4,3,2,1,0:T(8,128)(2,1)S(1)} %bitcast.2), custom_call_target="tpu_custom_call" | custom-call | tf_op jit(solution)/shard_map/pallas_call | solution.py:425
  83.8 0.0 collective-permute-done.7
  83.8 1.8 %collective-permute-done.8 = bf16[2,128,896]{2,1,0:T(8,128)(2,1)S(1)} collective-permute-done((bf16[2,128,896]{2,1,0:T(8,128)(2,1)}, bf16[2,128,896]{2,1,0:T(8,128)(2,1)S(1)}, u32[]{:S(2)}, u32[]{:S(2)}) %collective-permute-start.8) | collective-permute-done | bytes 458784 | tf_op jit(solution)/shard_map/ppermute | solution.py:423
  85.6 0.0 copy-done.14
  85.6 0.9 add_convert_fusion.2
  86.5 0.4 collective-permute-start.9
  87.0 1.6 %collective-permute-start.10 = (bf16[2,128,896]{2,1,0:T(8,128)(2,1)}, bf16[2,128,896]{2,1,0:T(8,128)(2,1)}, u32[]{:S(2)}, u32[]{:S(2)}) collective-permute-start(bf16[2,128,896]{2,1,0:T(8,128)(2,1)} %get-tuple-element.88), channel_id=1, source_target_pairs={{0,2},{2,4},{4,6},{6,0},{1,3},{3,5},{5,7},{7,1},{8,10},{10,12},{12... | collective-permute-start | bytes 1376264 | tf_op jit(solution)/shard_map/ppermute | solution.py:440
  88.5 3.9 %all-to-all-start.1 = ((bf16[4,256,128]{2,1,0:T(8,128)(2,1)}), bf16[4,256,128]{2,1,0:T(8,128)(2,1)S(1)}, u32[]{:S(2)}, u32[]{:S(2)}) async-start(bf16[4,256,128]{2,1,0:T(8,128)(2,1)} %shard_map.153), calls=%async_computation.1 | async-start | bytes 524288 | tf_op jit(solution)/shard_map/all_to_all | solution.py:438
  92.4 0.0 copy-done.12
  92.4 0.9 add_convert_fusion.1
  93.3 5.8 %all-to-all-done.1.pieces = bf16[4,256,128]{2,1,0:T(8,128)(2,1)S(1)} async-done(((bf16[4,256,128]{2,1,0:T(8,128)(2,1)}), bf16[4,256,128]{2,1,0:T(8,128)(2,1)S(1)}, u32[]{:S(2)}, u32[]{:S(2)}) %all-to-all-start.1) | async-done | bytes 262176 | tf_op jit(solution)/shard_map/all_to_all | solution.py:438
  99.1 0.0 collective-permute-done.9
  99.1 0.0 collective-permute-done.10
  99.1 1.5 %add_convert_fusion = bf16[2,128,896]{2,1,0:T(8,128)(2,1)S(1)} fusion(bf16[2,128,896]{2,1,0:T(8,128)(2,1)} %collective-permute-done.9, bf16[2,128,896]{2,1,0:T(8,128)(2,1)} %collective-permute-done.10, bf16[2,128,896]{2,1,0:T(8,128)(2,1)} %get-tuple-element.97), kind=kLoop, calls=%fused_computation | loop fusion | flops 1376256 | bytes 1835008 | tf_op jit(solution)/shard_map/convert_element_type | solution.py:443
  100.5 2.5 %collective-permute-start.13 = (bf16[2,128,896]{2,1,0:T(8,128)(2,1)S(1)}, bf16[2,128,896]{2,1,0:T(8,128)(2,1)S(1)}, u32[]{:S(2)}, u32[]{:S(2)}) collective-permute-start(bf16[2,128,896]{2,1,0:T(8,128)(2,1)S(1)} %add_convert_fusion), channel_id=1, source_target_pairs={{0,1},{1,0},{2,3},{3,2},{4,5},{5,4},{6,7},{7,6},{8,9},{9,8},{10,11... | collective-permute-start | bytes 1376264 | tf_op jit(solution)/shard_map/ppermute | solution.py:444
  103.1 0.0 collective-permute-start.11
  103.1 3.2 %collective-permute-start.12 = (bf16[2,128,896]{2,1,0:T(8,128)(2,1)}, bf16[2,128,896]{2,1,0:T(8,128)(2,1)S(1)}, u32[]{:S(2)}, u32[]{:S(2)}) collective-permute-start(bf16[2,128,896]{2,1,0:T(8,128)(2,1)} %get-tuple-element.96), channel_id=1, source_target_pairs={{0,6},{2,0},{4,2},{6,4},{1,7},{3,1},{5,3},{7,5},{8,14},{10,8},{12,... | collective-permute-start | bytes 1376264 | tf_op jit(solution)/shard_map/ppermute | solution.py:446
  106.3 1.0 copy-done.3
  107.4 0.8 shard_map.154
  108.1 3.7 %collective-permute-done.13.d3 = bf16[2,128,896]{2,1,0:T(8,128)(2,1)S(1)} collective-permute-done((bf16[2,128,896]{2,1,0:T(8,128)(2,1)S(1)}, bf16[2,128,896]{2,1,0:T(8,128)(2,1)S(1)}, u32[]{:S(2)}, u32[]{:S(2)}) %collective-permute-start.13) | collective-permute-done | bytes 458784 | tf_op jit(solution)/shard_map/ppermute | solution.py:444
  111.9 2.9 %collective-permute-done.11.d1 = bf16[2,128,896]{2,1,0:T(8,128)(2,1)S(1)} collective-permute-done((bf16[2,128,896]{2,1,0:T(8,128)(2,1)}, bf16[2,128,896]{2,1,0:T(8,128)(2,1)S(1)}, u32[]{:S(2)}, u32[]{:S(2)}) %collective-permute-start.11) | collective-permute-done | bytes 458784 | tf_op jit(solution)/shard_map/ppermute | solution.py:445
  114.7 0.0 collective-permute-done.12.d2
  114.7 0.0 copy-done.2
  114.7 0.0 copy-done.1
  114.8 0.0 copy-start.4
  114.8 1.0 copy-done.4
  115.8 0.9 copy-done.5
  116.7 0.9 copy-done.6
  117.7 0.9 copy-done.7
  118.6 4.0 %shard_map.155 = f32[2,128,896]{2,1,0:T(8,128)} custom-call(bf16[2,128,896]{2,1,0:T(8,128)(2,1)S(1)} %copy-done.4, bf16[2,128,896]{2,1,0:T(8,128)(2,1)S(1)} %collective-permute-done.11.d1, bf16[2,128,896]{2,1,0:T(8,128)(2,1)S(1)} %collective-permute-done.12.d2, bf16[2,128,896]{2,1,0:T(8,128)(2,1)S(1)} %collective-permute-done.13.d3, ...), custom_call_target="tpu_custom_call" | custom-call | tf_op jit(solution)/shard_map/pallas_call | solution.py:448
  (16 shorter events, 0.0 us)
Async XLA Ops:
  13.7 14.1 %collective-permute-start = (bf16[2,128,896]{2,1,0:T(8,128)(2,1)}, bf16[2,128,896]{2,1,0:T(8,128)(2,1)S(1)}, u32[]{:S(2)}, u32[]{:S(2)}) collective-permute-start(bf16[2,128,896]{2,1,0:T(8,128)(2,1)} %get-tuple-element.53.e00), channel_id=1, source_target_pairs={{0,1},{1,0},{2,3},{3,2},{4,5},{5,4},{6,7},{7,6},{8,9},{9,8},{10,11... | collective-permute-start | bytes 1376264 | tf_op jit(solution)/shard_map/ppermute | solution.py:344
  17.1 14.5 %collective-permute-start.1 = (bf16[2,128,896]{2,1,0:T(8,128)(2,1)}, bf16[2,128,896]{2,1,0:T(8,128)(2,1)S(1)}, u32[]{:S(2)}, u32[]{:S(2)}) collective-permute-start(bf16[2,128,896]{2,1,0:T(8,128)(2,1)} %get-tuple-element.53.e00), channel_id=1, source_target_pairs={{0,2},{2,4},{4,6},{6,0},{1,3},{3,5},{5,7},{7,1},{8,10},{10,12},{12... | collective-permute-start | bytes 1376264 | tf_op jit(solution)/shard_map/ppermute | solution.py:345
  19.0 12.6 %collective-permute-start.2 = (bf16[2,128,896]{2,1,0:T(8,128)(2,1)}, bf16[2,128,896]{2,1,0:T(8,128)(2,1)S(1)}, u32[]{:S(2)}, u32[]{:S(2)}) collective-permute-start(bf16[2,128,896]{2,1,0:T(8,128)(2,1)} %get-tuple-element.53.e00), channel_id=1, source_target_pairs={{0,6},{2,0},{4,2},{6,4},{1,7},{3,1},{5,3},{7,5},{8,14},{10,8},{12,... | collective-permute-start | bytes 1376264 | tf_op jit(solution)/shard_map/ppermute | solution.py:346
  23.3 17.3 %all-to-all-start = ((bf16[4,3,256,128]{3,2,1,0:T(8,128)(2,1)}), bf16[4,3,256,128]{3,2,1,0:T(8,128)(2,1)S(1)}, u32[]{:S(2)}, u32[]{:S(2)}) async-start(bf16[4,3,256,128]{3,2,1,0:T(8,128)(2,1)} %shard_map.150), calls=%async_computation | async-start | bytes 1572864 | tf_op jit(solution)/shard_map/all_to_all | solution.py:355
  27.5 47.8 %all-gather.3.cloned.1.call-start = ((), (), s32[]{:S(2)}) async-start(), calls=%async_computation.2 | async-start | bytes 2621440 | tf_op jit(solution)/shard_map/all_gather | solution.py:376
  27.8 12.8 %copy-start.8 = (bf16[2,128,896]{2,1,0:T(8,128)(2,1)}, bf16[2,128,896]{2,1,0:T(8,128)(2,1)S(1)}, u32[]{:S(2)}) copy-start(bf16[2,128,896]{2,1,0:T(8,128)(2,1)S(1)} %collective-permute-done.e01) | copy-start | bytes 1376260
  31.6 15.0 %copy-start.9 = (bf16[2,128,896]{2,1,0:T(8,128)(2,1)}, bf16[2,128,896]{2,1,0:T(8,128)(2,1)S(1)}, u32[]{:S(2)}) copy-start(bf16[2,128,896]{2,1,0:T(8,128)(2,1)S(1)} %collective-permute-done.1.e30) | copy-start | bytes 1376260
  31.6 9.0 %copy-start.10 = (bf16[2,128,896]{2,1,0:T(8,128)(2,1)}, bf16[2,128,896]{2,1,0:T(8,128)(2,1)S(1)}, u32[]{:S(2)}) copy-start(bf16[2,128,896]{2,1,0:T(8,128)(2,1)S(1)} %collective-permute-done.2.e10) | copy-start | bytes 1376260
  31.6 11.5 %collective-permute-start.3 = (bf16[2,128,896]{2,1,0:T(8,128)(2,1)S(1)}, bf16[2,128,896]{2,1,0:T(8,128)(2,1)S(1)}, u32[]{:S(2)}, u32[]{:S(2)}) collective-permute-start(bf16[2,128,896]{2,1,0:T(8,128)(2,1)S(1)} %collective-permute-done.e01), channel_id=1, source_target_pairs={{0,6},{2,0},{4,2},{6,4},{1,7},{3,1},{5,3},{7,5},{8,14},{10,8},{12,... | collective-permute-start | bytes 1376264 | tf_op jit(solution)/shard_map/ppermute | solution.py:359
  34.5 12.0 %collective-permute-start.4 = (bf16[2,128,896]{2,1,0:T(8,128)(2,1)S(1)}, bf16[2,128,896]{2,1,0:T(8,128)(2,1)S(1)}, u32[]{:S(2)}, u32[]{:S(2)}) collective-permute-start(bf16[2,128,896]{2,1,0:T(8,128)(2,1)S(1)} %collective-permute-done.e01), channel_id=1, source_target_pairs={{0,2},{2,4},{4,6},{6,0},{1,3},{3,5},{5,7},{7,1},{8,10},{10,12},{12... | collective-permute-start | bytes 1376264 | tf_op jit(solution)/shard_map/ppermute | solution.py:360
  43.1 14.6 %copy-start.11 = (bf16[2,128,896]{2,1,0:T(8,128)(2,1)}, bf16[2,128,896]{2,1,0:T(8,128)(2,1)S(1)}, u32[]{:S(2)}) copy-start(bf16[2,128,896]{2,1,0:T(8,128)(2,1)S(1)} %collective-permute-done.3.e11) | copy-start | bytes 1376260
  46.5 11.2 %copy-start.13 = (bf16[2,128,896]{2,1,0:T(8,128)(2,1)}, bf16[2,128,896]{2,1,0:T(8,128)(2,1)S(1)}, u32[]{:S(2)}) copy-start(bf16[2,128,896]{2,1,0:T(8,128)(2,1)S(1)} %collective-permute-done.4.e31) | copy-start | bytes 1376260
  46.6 11.2 %collective-permute-start.5 = (bf16[2,128,896]{2,1,0:T(8,128)(2,1)S(1)}, bf16[2,128,896]{2,1,0:T(8,128)(2,1)S(1)}, u32[]{:S(2)}, u32[]{:S(2)}) collective-permute-start(bf16[2,128,896]{2,1,0:T(8,128)(2,1)S(1)} %collective-permute-done.1.e30), channel_id=1, source_target_pairs={{0,2},{2,4},{4,6},{6,0},{1,3},{3,5},{5,7},{7,1},{8,10},{10,12},{12... | collective-permute-start | bytes 1376264 | tf_op jit(solution)/shard_map/ppermute | solution.py:374
  46.7 11.1 %collective-permute-start.6 = (bf16[2,128,896]{2,1,0:T(8,128)(2,1)S(1)}, bf16[2,128,896]{2,1,0:T(8,128)(2,1)S(1)}, u32[]{:S(2)}, u32[]{:S(2)}) collective-permute-start(bf16[2,128,896]{2,1,0:T(8,128)(2,1)S(1)} %collective-permute-done.3.e11), channel_id=1, source_target_pairs={{0,6},{2,0},{4,2},{6,4},{1,7},{3,1},{5,3},{7,5},{8,14},{10,8},{12,... | collective-permute-start | bytes 1376264 | tf_op jit(solution)/shard_map/ppermute | solution.py:375
  57.7 0.8 copy-start.15
  58.5 0.8 copy-start.16
  73.3 10.6 %collective-permute-start.7 = (bf16[2,128,896]{2,1,0:T(8,128)(2,1)}, bf16[2,128,896]{2,1,0:T(8,128)(2,1)S(1)}, u32[]{:S(2)}, u32[]{:S(2)}) collective-permute-start(bf16[2,128,896]{2,1,0:T(8,128)(2,1)} %get-tuple-element.81), channel_id=1, source_target_pairs={{0,6},{2,0},{4,2},{6,4},{1,7},{3,1},{5,3},{7,5},{8,14},{10,8},{12,... | collective-permute-start | bytes 1376264 | tf_op jit(solution)/shard_map/ppermute | solution.py:422
  74.4 11.3 %collective-permute-start.8 = (bf16[2,128,896]{2,1,0:T(8,128)(2,1)}, bf16[2,128,896]{2,1,0:T(8,128)(2,1)S(1)}, u32[]{:S(2)}, u32[]{:S(2)}) collective-permute-start(bf16[2,128,896]{2,1,0:T(8,128)(2,1)} %get-tuple-element.82), channel_id=1, source_target_pairs={{0,2},{2,4},{4,6},{6,0},{1,3},{3,5},{5,7},{7,1},{8,10},{10,12},{12... | collective-permute-start | bytes 1376264 | tf_op jit(solution)/shard_map/ppermute | solution.py:423
  75.4 1.6 %copy-start = (bf16[16,2,256,128]{3,2,1,0:T(8,128)(2,1)S(1)}, bf16[16,2,256,128]{3,2,1,0:T(8,128)(2,1)}, u32[]{:S(2)}) copy-start(bf16[16,2,256,128]{3,2,1,0:T(8,128)(2,1)} %all-gather.3.cloned.1.call-done) | copy-start | bytes 6291460
  76.9 8.7 %copy-start.14 = (bf16[2,128,896]{2,1,0:T(8,128)(2,1)S(1)}, bf16[2,128,896]{2,1,0:T(8,128)(2,1)}, u32[]{:S(2)}) copy-start(bf16[2,128,896]{2,1,0:T(8,128)(2,1)} %get-tuple-element.80) | copy-start | bytes 1376260
  83.8 8.6 %copy-start.12 = (bf16[2,128,896]{2,1,0:T(8,128)(2,1)S(1)}, bf16[2,128,896]{2,1,0:T(8,128)(2,1)}, u32[]{:S(2)}) copy-start(bf16[2,128,896]{2,1,0:T(8,128)(2,1)} %get-tuple-element.89) | copy-start | bytes 1376260
  86.5 12.6 %collective-permute-start.9 = (bf16[2,128,896]{2,1,0:T(8,128)(2,1)}, bf16[2,128,896]{2,1,0:T(8,128)(2,1)}, u32[]{:S(2)}, u32[]{:S(2)}) collective-permute-start(bf16[2,128,896]{2,1,0:T(8,128)(2,1)} %add_convert_fusion.2), channel_id=1, source_target_pairs={{0,6},{2,0},{4,2},{6,4},{1,7},{3,1},{5,3},{7,5},{8,14},{10,8},{12,... | collective-permute-start | bytes 1376264 | tf_op jit(solution)/shard_map/ppermute | solution.py:439
  87.0 12.1 %collective-permute-start.10 = (bf16[2,128,896]{2,1,0:T(8,128)(2,1)}, bf16[2,128,896]{2,1,0:T(8,128)(2,1)}, u32[]{:S(2)}, u32[]{:S(2)}) collective-permute-start(bf16[2,128,896]{2,1,0:T(8,128)(2,1)} %get-tuple-element.88), channel_id=1, source_target_pairs={{0,2},{2,4},{4,6},{6,0},{1,3},{3,5},{5,7},{7,1},{8,10},{10,12},{12... | collective-permute-start | bytes 1376264 | tf_op jit(solution)/shard_map/ppermute | solution.py:440
  88.5 10.5 %all-to-all-start.1 = ((bf16[4,256,128]{2,1,0:T(8,128)(2,1)}), bf16[4,256,128]{2,1,0:T(8,128)(2,1)S(1)}, u32[]{:S(2)}, u32[]{:S(2)}) async-start(bf16[4,256,128]{2,1,0:T(8,128)(2,1)} %shard_map.153), calls=%async_computation.1 | async-start | bytes 524288 | tf_op jit(solution)/shard_map/all_to_all | solution.py:438
  92.4 22.3 %copy-start.2 = (bf16[896,896]{1,0:T(8,128)(2,1)S(1)}, bf16[896,896]{1,0:T(8,128)(2,1)}, u32[]{:S(2)}) copy-start(bf16[896,896]{1,0:T(8,128)(2,1)} %get-tuple-element.103.wo_h) | copy-start | bytes 4816900
  93.3 21.5 %copy-start.1 = (bf16[896,896]{1,0:T(8,128)(2,1)S(1)}, bf16[896,896]{1,0:T(8,128)(2,1)}, u32[]{:S(2)}) copy-start(bf16[896,896]{1,0:T(8,128)(2,1)} %get-tuple-element.102.wq_h) | copy-start | bytes 4816900
  100.5 11.3 %collective-permute-start.13 = (bf16[2,128,896]{2,1,0:T(8,128)(2,1)S(1)}, bf16[2,128,896]{2,1,0:T(8,128)(2,1)S(1)}, u32[]{:S(2)}, u32[]{:S(2)}) collective-permute-start(bf16[2,128,896]{2,1,0:T(8,128)(2,1)S(1)} %add_convert_fusion), channel_id=1, source_target_pairs={{0,1},{1,0},{2,3},{3,2},{4,5},{5,4},{6,7},{7,6},{8,9},{9,8},{10,11... | collective-permute-start | bytes 1376264 | tf_op jit(solution)/shard_map/ppermute | solution.py:444
  103.1 11.7 %collective-permute-start.11 = (bf16[2,128,896]{2,1,0:T(8,128)(2,1)}, bf16[2,128,896]{2,1,0:T(8,128)(2,1)S(1)}, u32[]{:S(2)}, u32[]{:S(2)}) collective-permute-start(bf16[2,128,896]{2,1,0:T(8,128)(2,1)} %add_convert_fusion.1), channel_id=1, source_target_pairs={{0,2},{2,4},{4,6},{6,0},{1,3},{3,5},{5,7},{7,1},{8,10},{10,12},{12... | collective-permute-start | bytes 1376264 | tf_op jit(solution)/shard_map/ppermute | solution.py:445
  103.1 11.7 %collective-permute-start.12 = (bf16[2,128,896]{2,1,0:T(8,128)(2,1)}, bf16[2,128,896]{2,1,0:T(8,128)(2,1)S(1)}, u32[]{:S(2)}, u32[]{:S(2)}) collective-permute-start(bf16[2,128,896]{2,1,0:T(8,128)(2,1)} %get-tuple-element.96), channel_id=1, source_target_pairs={{0,6},{2,0},{4,2},{6,4},{1,7},{3,1},{5,3},{7,5},{8,14},{10,8},{12,... | collective-permute-start | bytes 1376264 | tf_op jit(solution)/shard_map/ppermute | solution.py:446
  106.3 1.0 copy-start.3
  114.8 1.0 copy-start.4
  115.8 0.9 copy-start.5
  116.7 0.9 copy-start.6
  117.7 0.9 copy-start.7
Sparse Core Ops, SparseCore 0:
  46.7 25.6 all-gather.2

commit v3 on v2

--- a/solution.py
+++ b/solution.py
@@ -1,3 +1,4 @@
+import functools
 import math
 
 import jax
@@ -117,10 +118,8 @@
     return jnp.concatenate(parts, axis=0)
 
 
-def encode_kernel(
-    ids, nb_h, ctx_h, wq_h, wk_h, wv_h, wo_h, enc, wt, ek_out, ev_out, *scratch
-):
-    nb, ctx, wq, wk, wv, wo, sems = scratch
+def encode_kernel(other, ids, nb_h, ctx_h, wq_h, wk_h, wv_h, wo_h, enc, *rest):
+    kept, (nb, ctx, wq, wk, wv, wo, sems) = rest[:-7], rest[-7:]
     both = ((nb_h, nb), (wq_h, wq), (ctx_h, ctx), (wk_h, wk), (wv_h, wv), (wo_h, wo))
     copies = [pltpu.make_async_copy(a, b, sems.at[i]) for i, (a, b) in enumerate(both)]
     for c in copies:
@@ -134,7 +133,8 @@
     copies[2].wait()
     contexts = []
     for t in range(slots):
-        mine = (lax.axis_index("z") * 2 + lax.axis_index("yh")) * slots + t
+        pair = jnp.bitwise_xor(lax.axis_index("yh"), other)
+        mine = (lax.axis_index("z") * 2 + pair) * slots + t
         span = jnp.int32(0)
         for c in range(1, ids.shape[1]):
             span = jnp.where((ids[0, c] == mine) | (ids[1, c] == mine), c, span)
@@ -148,30 +148,34 @@
     for t in range(slots):
         ek_t = ek[t * CL : (t + 1) * CL]
         ev_t = ev[t * CL : (t + 1) * CL]
-        ek_out[t] = ek_t
-        ev_out[t] = ev_t
         s = mm_nt(head_rows(ek_t), eq[t * rows : (t + 1) * rows]) * (1.0 / math.sqrt(each))
         s = s.reshape(EHEADS, CL, rows)
         p = jnp.exp(s - jnp.max(s, axis=1, keepdims=True))
-        w = (p / jnp.sum(p, axis=1, keepdims=True)).reshape(EHEADS * CL, rows)
-        wt[t] = w
+        w = (p * (1.0 / jnp.sum(p, axis=1, keepdims=True))).reshape(EHEADS * CL, rows)
+        for ref, value in zip(kept, (w, ek_t, ev_t)):
+            ref[t] = value
         mixed.append(mm_tn(w.astype(BF16), head_rows(ev_t)).astype(BF16))
     copies[5].wait()
     out = x.astype(F32) + mm(jnp.concatenate(mixed, axis=0), wo[...])
     enc[...] = out.astype(BF16).reshape(slots, rows, width)
 
 
-def pullback_kernel(d0, d1, d2, d3, wt, ek, ev, wq_h, wo_h, out, wq, wo, sems):
-    load_o = pltpu.make_async_copy(wo_h, wo, sems.at[0])
-    load_q = pltpu.make_async_copy(wq_h, wq, sems.at[1])
-    load_o.start()
-    load_q.start()
+def pullback_kernel(*refs):
+    given, out, here, sems = refs[:9], refs[9], refs[10:19], refs[19]
+    d0, d1, d2, d3, wo, ev, wt, ek, wq = here
+    loads = [pltpu.make_async_copy(a, b, sems.at[i]) for i, (a, b) in enumerate(zip(given, here))]
+    for c in loads:
+        c.start()
     slots, rows, width = d0.shape
     each = width // EHEADS
+    for c in loads[:4]:
+        c.wait()
     d = (d0[...].astype(F32) + d1[...].astype(F32)) + (d2[...].astype(F32) + d3[...].astype(F32))
     d = d.reshape(slots * rows, width)
-    load_o.wait()
+    loads[4].wait()
     de = mm(d.astype(BF16), wo[...]).astype(BF16)
+    for c in loads[5:8]:
+        c.wait()
     back = []
     for t in range(slots):
         w = wt[t]
@@ -181,15 +185,18 @@
         ds = w * (dw - jnp.sum(w * dw, axis=1, keepdims=True)) * (1.0 / math.sqrt(each))
         ds = ds.reshape(EHEADS * CL, rows).astype(BF16)
         back.append(mm_tn(ds, head_rows(ek[t])).astype(BF16))
-    load_q.wait()
+    loads[8].wait()
     out[...] = (d + mm(jnp.concatenate(back, axis=0), wq[...])).reshape(slots, rows, width)
 
 
-def prep_kernel(kw, vw, wq, wo, q, g, kw_t, vw_t, wq_t, wo_t, qm_t, gm_t):
+def turn_kernel(kw, vw, wq, wo, kw_t, vw_t, wq_t, wo_t):
     kw_t[...] = kw[...].T
     vw_t[...] = vw[...].T
     wq_t[...] = wq[...].T
     wo_t[...] = wo[...].T
+
+
+def blocks_kernel(q, g, qm_t, gm_t):
     for c in range(qm_t.shape[0]):
         qm_t[c] = head_blocks(q[c * CL : (c + 1) * CL]).T
         gm_t[c] = head_blocks(g[c * CL : (c + 1) * CL]).T
@@ -208,8 +215,8 @@
 def cross_kernel(ids, e00, e01, e10, e11, e20, e21, e30, e31, *rest):
     blocks = (e00, e01, e10, e11, e20, e21, e30, e31)
     given, cross, outs = rest[:8], rest[8], rest[9:17]
-    table, held, sent, dk, dv, zero, in_sem, out_sem, given_sem = rest[17:26]
-    here = rest[26:]
+    table, held, sent, ck, cv, dk, dv, zero, in_sem, out_sem, given_sem = rest[17:28]
+    here = rest[28:]
     kw, vw, qm_t, gm_t, q, g, kw_t, vw_t = here
     loads = [
         pltpu.make_async_copy(a, b, given_sem.at[i]) for i, (a, b) in enumerate(zip(given, here))
@@ -247,50 +254,63 @@
             pltpu.make_async_copy(zero, outs[i].at[t], out_sem.at[2 * i + t]).start()
 
     heads = q.shape[1] // HSIZE
+    pair = 2 * NL
     for half in range(2):
         first = half * (n_named // 2)
         for n in range(first, first + n_named // 2):
             pltpu.make_async_copy(e00.at[0], held.at[n], in_sem.at[n]).wait()
         e = held[first : first + n_named // 2].reshape(n_named // 2 * NL, -1)
+        at = slice(first * NL, (first + n_named // 2) * NL)
         if half == 0:
             loads[0].wait()
-        ck_all = mm(e, kw[...]).astype(BF16)
+        ck[at] = mm(e, kw[...]).astype(BF16)
         if half == 0:
             loads[1].wait()
-        cv_all = mm(e, vw[...]).astype(BF16)
-        if half == 0:
-            for c in loads[2:6]:
-                c.wait()
-        for i in range(spans // 2):
-            c = half * (spans // 2) + i
-            ck = ck_all[i * 2 * NL : (i + 1) * 2 * NL]
-            cv = cv_all[i * 2 * NL : (i + 1) * 2 * NL]
-            qm = head_blocks(q[c * CL : (c + 1) * CL])
-            gm = head_blocks(g[c * CL : (c + 1) * CL])
-            s = mm(ck, qm_t[c]) * scale
-            dp = mm(cv, gm_t[c])
-            p = jnp.exp(s - jnp.max(s, axis=0, keepdims=True))
-            p = p / jnp.sum(p, axis=0, keepdims=True)
-            pb = p.astype(BF16)
-            ds = p * (dp - jnp.sum(p * dp, axis=0, keepdims=True)) * scale
-            dk[i * 2 * NL : (i + 1) * 2 * NL] = mm(ds.astype(BF16), qm).astype(BF16)
-            dv[i * 2 * NL : (i + 1) * 2 * NL] = mm(pb, gm).astype(BF16)
-            o = mm_tn(pb, cv)
-            for h in range(heads):
-                cross[c * CL : (c + 1) * CL, h * HSIZE : (h + 1) * HSIZE] = o[
-                    h * CL : (h + 1) * CL, h * HSIZE : (h + 1) * HSIZE
-                ]
-        if half == 0:
-            loads[6].wait()
-            loads[7].wait()
-        de = mm(dk[...], kw_t[...]) + mm(dv[...], vw_t[...])
-        sent[first : first + n_named // 2] = de.astype(BF16).reshape(n_named // 2, NL, -1)
-        for i, t in places:
-            n = table[2 * i + t]
-
-            @pl.when((n >= first) & (n < first + n_named // 2))
-            def _():
-                pltpu.make_async_copy(sent.at[n], outs[i].at[t], out_sem.at[2 * i + t]).start()
+        cv[at] = mm(e, vw[...]).astype(BF16)
+    for c in loads[2:]:
+        c.wait()
+
+    def scores(c):
+        at = slice(c * pair, (c + 1) * pair)
+        return mm(ck[at], qm_t[c]) * scale, mm(cv[at], gm_t[c])
+
+    def soften(s, dp):
+        p = jnp.exp(s - jnp.max(s, axis=0, keepdims=True))
+        p = p * (1.0 / jnp.sum(p, axis=0, keepdims=True))
+        ds = p * (dp - jnp.sum(p * dp, axis=0, keepdims=True)) * scale
+        return p.astype(BF16), ds.astype(BF16)
+
+    def products(c, pb, ds):
+        at = slice(c * pair, (c + 1) * pair)
+        dk[at] = mm(ds, head_blocks(q[c * CL : (c + 1) * CL])).astype(BF16)
+        dv[at] = mm(pb, head_blocks(g[c * CL : (c + 1) * CL])).astype(BF16)
+        o = mm_tn(pb, cv[at])
+        for h in range(heads):
+            cross[c * CL : (c + 1) * CL, h * HSIZE : (h + 1) * HSIZE] = o[
+                h * CL : (h + 1) * CL, h * HSIZE : (h + 1) * HSIZE
+            ]
+
+    def back(c):
+        at = slice(c * pair, (c + 1) * pair)
+        de = mm(dk[at], kw_t[...]) + mm(dv[at], vw_t[...])
+        sent[2 * c : 2 * c + 2] = de.astype(BF16).reshape(2, NL, -1)
+
+    ahead = scores(0)
+    for c in range(spans):
+        now = ahead
+        if c + 1 < spans:
+            ahead = scores(c + 1)
+        soft = soften(*now)
+        if c >= 1:
+            back(c - 1)
+        products(c, *soft)
+    back(spans - 1)
+    for i, t in places:
+        n = table[2 * i + t]
+
+        @pl.when(n >= 0)
+        def _():
+            pltpu.make_async_copy(sent.at[n], outs[i].at[t], out_sem.at[2 * i + t]).start()
 
     for i, t in places:
         pltpu.make_async_copy(zero, outs[i].at[t], out_sem.at[2 * i + t]).wait()
@@ -325,23 +345,29 @@
 
     ids = neighbour_ids.T
 
-    enc, wt, ek, ev = call(
-        encode_kernel,
-        out_shape=[
-            struct((slots, nl, ew), BF16),
+    raw = lax.ppermute(neighbours, "yh", shift(2, 1))
+
+    def encode(other, blocks, kept):
+        return call(
+            functools.partial(encode_kernel, other),
+            out_shape=[struct((slots, nl, ew), BF16)] + kept,
+            in_specs=[smem()] + [hbm()] * 6,
+            out_specs=[vmem()] * (1 + len(kept)),
+            scratch_shapes=[pltpu.VMEM(neighbours.shape, BF16), pltpu.VMEM(span_ctx.shape, BF16)]
+            + [pltpu.VMEM((ew, ew), BF16)] * 4
+            + [pltpu.SemaphoreType.DMA((6,))],
+        )(ids, blocks, span_ctx, enc_q, enc_k, enc_v, enc_o)
+
+    e00, wt, ek, ev = encode(
+        0,
+        neighbours,
+        [
             struct((slots, EHEADS * CL, nl), F32),
             struct((slots, CL, ew), BF16),
             struct((slots, CL, ew), BF16),
         ],
-        in_specs=[smem()] + [hbm()] * 6,
-        out_specs=[vmem()] * 4,
-        scratch_shapes=[pltpu.VMEM(neighbours.shape, BF16), pltpu.VMEM(span_ctx.shape, BF16)]
-        + [pltpu.VMEM((ew, ew), BF16)] * 4
-        + [pltpu.SemaphoreType.DMA((6,))],
-    )(ids, neighbours, span_ctx, enc_q, enc_k, enc_v, enc_o)
-
-    e00 = enc
-    e01 = lax.ppermute(e00, "yh", shift(2, 1))
+    )
+
     e30 = lax.ppermute(e00, "z", shift(NX, 1))
     e10 = lax.ppermute(e00, "z", shift(NX, -1))
 
@@ -352,28 +378,34 @@
         in_specs=[vmem()] * 3,
         out_specs=vmem(),
     )(self_q, self_k, self_v)
-    pieces = lax.all_to_all(packed, "x", 0, 0)
-    own_kv = pieces[:, 1:]
-
+    raw, _ = after((raw, wt))
+    (e01,) = encode(1, raw, [])
     e01, e30, e10, packed = after((e01, e30, e10, packed))
     e11 = lax.ppermute(e01, "z", shift(NX, -1))
     e31 = lax.ppermute(e01, "z", shift(NX, 1))
-
-    weights = after((cross_k_weight, cross_v_weight, enc_q, enc_o, cross_q, mixed_grad, e01))[:6]
-    prepared = call(
-        prep_kernel,
-        out_shape=[struct((width, ew), BF16)] * 2
-        + [struct((ew, ew), BF16)] * 2
-        + [struct((spans, width, width // HSIZE * CL), BF16)] * 2,
-        in_specs=[vmem()] * 6,
-        out_specs=[vmem()] * 6,
+    pieces = lax.all_to_all(packed, "x", 0, 0)
+
+    weights = after((cross_k_weight, cross_v_weight, enc_q, enc_o, e01))[:4]
+    turned = call(
+        turn_kernel,
+        out_shape=[struct((width, ew), BF16)] * 2 + [struct((ew, ew), BF16)] * 2,
+        in_specs=[vmem()] * 4,
+        out_specs=[vmem()] * 4,
     )(*weights)
 
-    e11, e31, e30, own_kv, *prepared = after((e11, e31, e30, own_kv, *prepared))
-    kw_t, vw_t, wq_t, wo_t, qm_t, gm_t = prepared
+    e30, e11, e31, *turned = after((e30, e11, e31, *turned))
+    kw_t, vw_t, wq_t, wo_t = turned
     e20 = lax.ppermute(e30, "z", shift(NX, 1))
     e21 = lax.ppermute(e11, "z", shift(NX, -1))
-    kv = lax.all_gather(own_kv, ("yl", "core"), axis=0)
+    kv = lax.all_gather(pieces[:, 1:], ("yl", "core"), axis=0)
+
+    queries, grads, _ = after((cross_q, mixed_grad, e11))
+    qm_t, gm_t = call(
+        blocks_kernel,
+        out_shape=[struct((spans, width, width // HSIZE * CL), BF16)] * 2,
+        in_specs=[vmem()] * 2,
+        out_specs=[vmem()] * 2,
+    )(queries, grads)
 
     cross, *p = call(
         cross_kernel,
@@ -384,8 +416,10 @@
             pltpu.SMEM((16,), jnp.int32),
             pltpu.VMEM((n_named, nl, ew), BF16),
             pltpu.VMEM((n_named, nl, ew), BF16),
-            pltpu.VMEM((n_named // 2 * nl, width), BF16),
-            pltpu.VMEM((n_named // 2 * nl, width), BF16),
+            pltpu.VMEM((n_named * nl, width), BF16),
+            pltpu.VMEM((n_named * nl, width), BF16),
+            pltpu.VMEM((n_named * nl, width), BF16),
+            pltpu.VMEM((n_named * nl, width), BF16),
             pltpu.VMEM((nl, ew), BF16),
             pltpu.SemaphoreType.DMA((n_named,)),
             pltpu.SemaphoreType.DMA((16,)),
@@ -421,10 +455,13 @@
 
     far1 = lax.ppermute(p21, "z", shift(NX, -1))
     far0 = lax.ppermute(p20, "z", shift(NX, 1))
-    kv, _ = after((kv, cross))
+    far1, far0, p11 = after((far1, far0, p11))
+    down1 = lax.ppermute(add(p31, far1), "z", shift(NX, -1))
+    up1 = lax.ppermute(p11, "z", shift(NX, 1))
+    near0 = add(p10, far0)
+    kv, _ = after((kv, far1))
     outs = call(
         attend_kernel,
-        mib=20,
         out_shape=struct((NX, rows, HSIZE), BF16),
         in_specs=[vmem()] * 2,
         out_specs=vmem(),
@@ -434,12 +471,8 @@
             pltpu.VMEM((rows, 1), F32),
         ],
     )(pieces, kv)
-    far1, far0, p11, outs = after((far1, far0, p11, outs))
+    down1, up1, near0, p30, outs = after((down1, up1, near0, p30, outs))
     selfs = lax.all_to_all(outs, "x", 0, 0)
-    down1 = lax.ppermute(add(p31, far1), "z", shift(NX, -1))
-    up1 = lax.ppermute(p11, "z", shift(NX, 1))
-    near0 = add(p10, far0)
-    down1, up1, near0, p30, selfs = after((down1, up1, near0, p30, selfs))
     theirs = (p01.astype(F32) + up1.astype(F32) + down1.astype(F32)).astype(BF16)
     other = lax.ppermute(theirs, "yh", shift(2, 1))
     up0 = lax.ppermute(near0, "z", shift(NX, 1))
@@ -447,16 +480,22 @@
 
     grad = call(
         pullback_kernel,
-        mib=20,
         out_shape=struct((slots, nl, ew), F32),
-        in_specs=[vmem()] * 7 + [hbm()] * 2,
+        in_specs=[hbm()] * 9,
         out_specs=vmem(),
-        scratch_shapes=[pltpu.VMEM((ew, ew), BF16)] * 2 + [pltpu.SemaphoreType.DMA((2,))],
-    )(p00, up0, down0, other, wt, ek, ev, wq_t, wo_t)
+        scratch_shapes=[pltpu.VMEM((slots, nl, ew), BF16)] * 4
+        + [
+            pltpu.VMEM((ew, ew), BF16),
+            pltpu.VMEM(ev.shape, BF16),
+            pltpu.VMEM(wt.shape, F32),
+            pltpu.VMEM(ek.shape, BF16),
+            pltpu.VMEM((ew, ew), BF16),
+            pltpu.SemaphoreType.DMA((9,)),
+        ],
+    )(p00, up0, down0, other, wo_t, ev, wt, ek, wq_t)
 
     mixed = call(
         mix_kernel,
-        mib=20,
         out_shape=struct((rows, width), BF16),
         in_specs=[vmem()] * 2,
         out_specs=vmem(),

time: 130 us -> 144 us (1.11)
  blocking collectives: 0 us -> 25.3 us
  Pallas kernels: 40.3 us -> 52.6 us
  starting transfers between devices: 31.6 us -> 23.1 us
  waiting for transfers between devices: 31.3 us -> 23.8 us
  local copies, waits for them, and re-layouts: 8.86 us -> 3.68 us
  other arithmetic: 3.22 us -> 1.41 us
    all_to_all x0 -> x2, blocking collectives: none -> 25.3 us  [the longest x1 15.5 us: local(): pieces = lax.all_to_all(packed, 'x', 0, 0)]
    pallas_call x5 -> x7, Pallas kernels: 24.2 us -> 37.2 us  [the longest x2 13 us: encode(): call(functools.partial(encode_kernel, other), out_shape=[struct((slots, n...]
    ppermute x1, waiting for transfers between devices: 0.01 us -> 8.77 us  [local(): far1 = lax.ppermute(p21, 'z', shift(NX, -1))]
    all_to_all x2 -> x0, starting transfers between devices: 8.14 us -> none  [the longest x1 4.29 us: local(): pieces = lax.all_to_all(packed, 'x', 0, 0)]
    all_to_all x2 -> x0, waiting for transfers between devices: 5.8 us -> none  [the longest x1 5.8 us: local(): selfs = lax.all_to_all(outs, 'x', 0, 0)]
    unnamed x34, local copies, waits for them, and re-layouts: 8.04 us -> 2.79 us
    ppermute x1, waiting for transfers between devices: 7.85 us -> 3.57 us  [local(): e20 = lax.ppermute(e30, 'z', shift(NX, 1))]
    ppermute x1, waiting for transfers between devices: 3.74 us -> 0.01 us  [local(): other = lax.ppermute(theirs, 'yh', shift(2, 1))]
  transfers between devices with their start and end apart: 17 -> 15, of which waited for: 9 -> 7; matrix products, arithmetic and copies ran while one was open for 1% -> 1% of each run, Pallas kernels for 23% -> 33%
where the time goes in v3:
time: 144 us
  Pallas kernels  52.6 us (37%)
  blocking collectives  25.3 us (18%)
  waiting for transfers between devices  23.8 us (17%)
  starting transfers between devices  23.1 us (16%)
  between operations  14.2 us (10%)
  local copies, waits for them, and re-layouts  3.68 us (3%)
    all_to_all x1, blocking collectives, local(): pieces = lax.all_to_all(packed, 'x', 0, 0)  15.5 us
    pallas_call x1, Pallas kernels, local(): call(cross_kernel, out_shape=[struct((rows, width), F32)] + [struct((slot...  13.2 us
    pallas_call x2, Pallas kernels, encode(): call(functools.partial(encode_kernel, other), out_shape=[struct((slots, n...  13 us
    all_to_all x1, blocking collectives, local(): selfs = lax.all_to_all(outs, 'x', 0, 0)  9.72 us
    ppermute x1, waiting for transfers between devices, local(): far1 = lax.ppermute(p21, 'z', shift(NX, -1))  8.77 us
    pallas_call x1, Pallas kernels, local(): call(attend_kernel, out_shape=struct((NX, rows, HSIZE), BF16), in_specs=[...  8.74 us
    pallas_call x1, Pallas kernels, local(): call(pullback_kernel, out_shape=struct((slots, nl, ew), F32), in_specs=[h...  5.59 us
    pallas_call x1, Pallas kernels, local(): call(turn_kernel, out_shape=[struct((width, ew), BF16)] * 2 + [struct((ew...  5.13 us
  transfers between devices with their start and end apart: 15, of which 7 were waited for; matrix products, arithmetic and copies ran while one was open for 1% of the time, Pallas kernels for 33%

profile of v3, /device:TPU:0, one launch (start us, length us, event | category | flops | bytes accessed | tf_op | source)
XLA Modules:
  0.0 144.1 jit_solution(16167886508242471264)
XLA Ops:
  7.2 0.0 all-gather.3.cloned.1.call-start
  7.2 3.4 %collective-permute-start = (bf16[2,128,896]{2,1,0:T(8,128)(2,1)}, bf16[2,128,896]{2,1,0:T(8,128)(2,1)S(1)}, u32[]{:S(2)}, u32[]{:S(2)}) collective-permute-start(bf16[2,128,896]{2,1,0:T(8,128)(2,1)} %nb_h.1), channel_id=1, source_target_pairs={{0,1},{1,0},{2,3},{3,2},{4,5},{5,4},{6,7},{7,6},{8,9},{9,8},{10,11... | collective-permute-start | bytes 1376264 | tf_op jit(solution)/shard_map/ppermute | solution.py:348
  10.6 6.5 %shard_map.149 = (bf16[2,128,896]{2,1,0:T(8,128)(2,1)}, f32[2,256,128]{2,1,0:T(8,128)}, bf16[2,64,896]{2,1,0:T(8,128)(2,1)}, bf16[2,64,896]{2,1,0:T(8,128)(2,1)}) custom-call(s32[2,4]{1,0:T(2,128)} %bitcast.3, bf16[2,128,896]{2,1,0:T(8,128)(2,1)} %nb_h.1, bf16[256,896]{1,0:T(8,128)(2,1)} %ctx_h.3, bf16[896,896]{1,0:T(8,128)(2,1)} %wq, ...), custom_call_target="tpu_custom_call" | custom-call | tf_op jit(solution)/shard_map/pallas_call | solution.py:351
  17.1 2.0 %collective-permute-start.1 = (bf16[2,128,896]{2,1,0:T(8,128)(2,1)}, bf16[2,128,896]{2,1,0:T(8,128)(2,1)S(1)}, u32[]{:S(2)}, u32[]{:S(2)}) collective-permute-start(bf16[2,128,896]{2,1,0:T(8,128)(2,1)} %get-tuple-element.51.e00), channel_id=1, source_target_pairs={{0,2},{2,4},{4,6},{6,0},{1,3},{3,5},{5,7},{7,1},{8,10},{10,12},{12... | collective-permute-start | bytes 1376264 | tf_op jit(solution)/shard_map/ppermute | solution.py:371
  19.1 2.2 %collective-permute-start.2 = (bf16[2,128,896]{2,1,0:T(8,128)(2,1)}, bf16[2,128,896]{2,1,0:T(8,128)(2,1)S(1)}, u32[]{:S(2)}, u32[]{:S(2)}) collective-permute-start(bf16[2,128,896]{2,1,0:T(8,128)(2,1)} %get-tuple-element.51.e00), channel_id=1, source_target_pairs={{0,6},{2,0},{4,2},{6,4},{1,7},{3,1},{5,3},{7,5},{8,14},{10,8},{12,... | collective-permute-start | bytes 1376264 | tf_op jit(solution)/shard_map/ppermute | solution.py:372
  21.3 2.1 %shard_map.151 = bf16[4,3,256,128]{3,2,1,0:T(8,128)(2,1)} custom-call(bf16[256,512]{1,0:T(8,128)(2,1)} %q_ref, bf16[256,512]{1,0:T(8,128)(2,1)} %k_ref, bf16[256,512]{1,0:T(8,128)(2,1)} %v_ref), custom_call_target="tpu_custom_call" | custom-call | tf_op jit(solution)/shard_map/pallas_call | solution.py:375
  23.4 0.0 collective-permute-done.nb_h
  23.4 0.8 copy-done.15
  24.2 6.5 %shard_map.150.e01 = bf16[2,128,896]{2,1,0:T(8,128)(2,1)} custom-call(s32[2,4]{1,0:T(2,128)} %bitcast.4, bf16[2,128,896]{2,1,0:T(8,128)(2,1)} %copy-done.15, bf16[256,896]{1,0:T(8,128)(2,1)} %ctx_h.3, bf16[896,896]{1,0:T(8,128)(2,1)} %wq, bf16[896,896]{1,0:T(8,128)(2,1)} %wk_h.3, bf16[896,896]{1,0:T(8,128)(2,1)} %wv_h.3, bf16[896,896]{1,0:T(8,128)(2,1)} %wo), custom_call_target="tpu_custom_call" | custom-call | tf_op jit(solution)/shard_map/pallas_call | solution.py:351
  30.7 0.0 copy-start.2
  30.7 0.9 collective-permute-done.1.e30
  31.6 0.0 collective-permute-done.2.e10
  31.6 0.0 copy-done.1
  31.6 0.0 copy-start.9
  31.7 15.5 %all_to_all.10.pieces = bf16[4,3,256,128]{3,2,1,0:T(8,128)(2,1)S(1)} all-to-all(bf16[4,3,256,128]{3,2,1,0:T(8,128)(2,1)S(1)} %copy-done.1), channel_id=1, replica_groups=mesh['x'=4,'yl'=2,'core'=2,'z'=4,'yh'=2] {'x'}, dimensions={0} | all-to-all | bytes 1572864 | tf_op jit(solution)/shard_map/all_to_all | solution.py:386
  47.2 0.9 slice.4
  48.1 0.0 all-gather.3.cloned.1.call-update
  48.1 0.0 copy-done.2
  48.1 2.8 %collective-permute-start.3 = (bf16[2,128,896]{2,1,0:T(8,128)(2,1)S(1)}, bf16[2,128,896]{2,1,0:T(8,128)(2,1)S(1)}, u32[]{:S(2)}, u32[]{:S(2)}) collective-permute-start(bf16[2,128,896]{2,1,0:T(8,128)(2,1)S(1)} %copy-done.2), channel_id=1, source_target_pairs={{0,6},{2,0},{4,2},{6,4},{1,7},{3,1},{5,3},{7,5},{8,14},{10,8},{12,... | collective-permute-start | bytes 1376264 | tf_op jit(solution)/shard_map/ppermute | solution.py:384
  50.9 0.0 collective-permute-start.4
  50.9 5.1 %shard_map.152 = (bf16[512,896]{1,0:T(8,128)(2,1)}, bf16[512,896]{1,0:T(8,128)(2,1)}, bf16[896,896]{1,0:T(8,128)(2,1)}, bf16[896,896]{1,0:T(8,128)(2,1)}) custom-call(bf16[896,512]{1,0:T(8,128)(2,1)} %rest_0_.1, bf16[896,512]{1,0:T(8,128)(2,1)} %rest_1_.1, bf16[896,896]{1,0:T(8,128)(2,1)} %wq, bf16[896,896]{1,0:T(8,128)(2,1)} %wo), custom_call_target="tpu_custom_call" | custom-call | tf_op jit(solution)/shard_map/pallas_call | solution.py:389
  56.0 0.0 copy-done.9
  56.0 0.0 copy-done
  56.0 2.4 %collective-permute-done.3.e11 = bf16[2,128,896]{2,1,0:T(8,128)(2,1)S(1)} collective-permute-done((bf16[2,128,896]{2,1,0:T(8,128)(2,1)S(1)}, bf16[2,128,896]{2,1,0:T(8,128)(2,1)S(1)}, u32[]{:S(2)}, u32[]{:S(2)}) %collective-permute-start.3) | collective-permute-done | bytes 458784 | tf_op jit(solution)/shard_map/ppermute | solution.py:384
  58.4 3.2 %collective-permute-done.4.e31 = bf16[2,128,896]{2,1,0:T(8,128)(2,1)S(1)} collective-permute-done((bf16[2,128,896]{2,1,0:T(8,128)(2,1)S(1)}, bf16[2,128,896]{2,1,0:T(8,128)(2,1)S(1)}, u32[]{:S(2)}, u32[]{:S(2)}) %collective-permute-start.4) | collective-permute-done | bytes 458784 | tf_op jit(solution)/shard_map/ppermute | solution.py:385
  61.6 0.0 copy-done.8
  61.6 0.0 collective-permute-start.5
  61.6 3.2 %collective-permute-start.6 = (bf16[2,128,896]{2,1,0:T(8,128)(2,1)S(1)}, bf16[2,128,896]{2,1,0:T(8,128)(2,1)S(1)}, u32[]{:S(2)}, u32[]{:S(2)}) collective-permute-start(bf16[2,128,896]{2,1,0:T(8,128)(2,1)S(1)} %collective-permute-done.3.e11), channel_id=1, source_target_pairs={{0,6},{2,0},{4,2},{6,4},{1,7},{3,1},{5,3},{7,5},{8,14},{10,8},{12,... | collective-permute-start | bytes 1376264 | tf_op jit(solution)/shard_map/ppermute | solution.py:399
  64.8 2.9 %shard_map.153 = (bf16[4,512,256]{2,1,0:T(8,128)(2,1)}, bf16[4,512,256]{2,1,0:T(8,128)(2,1)}) custom-call(bf16[256,512]{1,0:T(8,128)(2,1)} %rest_4_.1, bf16[256,512]{1,0:T(8,128)(2,1)} %rest_5_.1), custom_call_target="tpu_custom_call" | custom-call | tf_op jit(solution)/shard_map/pallas_call | solution.py:403
  67.7 3.6 %collective-permute-done.5.e20 = bf16[2,128,896]{2,1,0:T(8,128)(2,1)S(1)} collective-permute-done((bf16[2,128,896]{2,1,0:T(8,128)(2,1)S(1)}, bf16[2,128,896]{2,1,0:T(8,128)(2,1)S(1)}, u32[]{:S(2)}, u32[]{:S(2)}) %collective-permute-start.5) | collective-permute-done | bytes 458784 | tf_op jit(solution)/shard_map/ppermute | solution.py:398
  71.3 0.0 collective-permute-done.6.e21
  71.3 0.0 copy-done.10
  71.3 0.0 copy-done.12
  71.3 0.8 copy-done.13
  72.0 0.2 copy-done.14
  72.2 13.2 %shard_map.154 = (f32[256,512]{1,0:T(8,128)}, bf16[2,128,896]{2,1,0:T(8,128)(2,1)}, bf16[2,128,896]{2,1,0:T(8,128)(2,1)}, bf16[2,128,896]{2,1,0:T(8,128)(2,1)}, ...) custom-call(s32[2,4]{1,0:T(2,128)} %bitcast.5, ...), custom_call_target="tpu_custom_call" | custom-call | tf_op jit(solution)/shard_map/pallas_call | solution.py:410
  85.4 3.1 %collective-permute-start.7 = (bf16[2,128,896]{2,1,0:T(8,128)(2,1)}, bf16[2,128,896]{2,1,0:T(8,128)(2,1)S(1)}, u32[]{:S(2)}, u32[]{:S(2)}) collective-permute-start(bf16[2,128,896]{2,1,0:T(8,128)(2,1)} %get-tuple-element.78), channel_id=1, source_target_pairs={{0,6},{2,0},{4,2},{6,4},{1,7},{3,1},{5,3},{7,5},{8,14},{10,8},{12,... | collective-permute-start | bytes 1376264 | tf_op jit(solution)/shard_map/ppermute | solution.py:456
  88.6 0.0 collective-permute-start.8
  88.6 8.8 %collective-permute-done.7 = bf16[2,128,896]{2,1,0:T(8,128)(2,1)S(1)} collective-permute-done((bf16[2,128,896]{2,1,0:T(8,128)(2,1)}, bf16[2,128,896]{2,1,0:T(8,128)(2,1)S(1)}, u32[]{:S(2)}, u32[]{:S(2)}) %collective-permute-start.7) | collective-permute-done | bytes 458784 | tf_op jit(solution)/shard_map/ppermute | solution.py:456
  97.4 3.4 %collective-permute-done.8 = bf16[2,128,896]{2,1,0:T(8,128)(2,1)S(1)} collective-permute-done((bf16[2,128,896]{2,1,0:T(8,128)(2,1)}, bf16[2,128,896]{2,1,0:T(8,128)(2,1)S(1)}, u32[]{:S(2)}, u32[]{:S(2)}) %collective-permute-start.8) | collective-permute-done | bytes 458784 | tf_op jit(solution)/shard_map/ppermute | solution.py:457
  100.7 1.1 add_convert_fusion.2
  101.8 0.3 collective-permute-start.9
  102.1 1.8 %collective-permute-start.10 = (bf16[2,128,896]{2,1,0:T(8,128)(2,1)}, bf16[2,128,896]{2,1,0:T(8,128)(2,1)S(1)}, u32[]{:S(2)}, u32[]{:S(2)}) collective-permute-start(bf16[2,128,896]{2,1,0:T(8,128)(2,1)} %get-tuple-element.82), channel_id=1, source_target_pairs={{0,2},{2,4},{4,6},{6,0},{1,3},{3,5},{5,7},{7,1},{8,10},{10,12},{12... | collective-permute-start | bytes 1376264 | tf_op jit(solution)/shard_map/ppermute | solution.py:460
  103.9 0.0 copy-done.11
  103.9 0.1 add_convert_fusion.1
  104.1 0.0 copy-start.7
  104.1 0.0 all-gather.3.cloned.1.call-done
  104.1 8.7 %shard_map.155 = bf16[4,256,128]{2,1,0:T(8,128)(2,1)} custom-call(bf16[4,3,256,128]{3,2,1,0:T(8,128)(2,1)} %copy-done, bf16[4,4,2,256,128]{4,3,2,1,0:T(8,128)(2,1)} %bitcast.2), custom_call_target="tpu_custom_call" | custom-call | tf_op jit(solution)/shard_map/pallas_call | solution.py:463
  112.8 0.0 collective-permute-done.9
  112.8 1.6 %collective-permute-done.10 = bf16[2,128,896]{2,1,0:T(8,128)(2,1)S(1)} collective-permute-done((bf16[2,128,896]{2,1,0:T(8,128)(2,1)}, bf16[2,128,896]{2,1,0:T(8,128)(2,1)S(1)}, u32[]{:S(2)}, u32[]{:S(2)}) %collective-permute-start.10) | collective-permute-done | bytes 458784 | tf_op jit(solution)/shard_map/ppermute | solution.py:460
  114.4 0.2 add_convert_fusion
  114.6 1.1 collective-permute-start.13
  115.7 2.0 %collective-permute-start.11 = (bf16[2,128,896]{2,1,0:T(8,128)(2,1)S(1)}, bf16[2,128,896]{2,1,0:T(8,128)(2,1)S(1)}, u32[]{:S(2)}, u32[]{:S(2)}) collective-permute-start(bf16[2,128,896]{2,1,0:T(8,128)(2,1)S(1)} %add_convert_fusion.1), channel_id=1, source_target_pairs={{0,2},{2,4},{4,6},{6,0},{1,3},{3,5},{5,7},{7,1},{8,10},{10,12},{12... | collective-permute-start | bytes 1376264 | tf_op jit(solution)/shard_map/ppermute | solution.py:478
  117.7 0.0 copy-done.16
  117.7 1.2 collective-permute-start.12
  118.9 9.7 %all_to_all.11.pieces = bf16[4,256,128]{2,1,0:T(8,128)(2,1)} all-to-all(bf16[4,256,128]{2,1,0:T(8,128)(2,1)S(1)} %copy-done.3), channel_id=1, replica_groups=mesh['x'=4,'yl'=2,'core'=2,'z'=4,'yh'=2] {'x'}, dimensions={0} | all-to-all | bytes 524288 | tf_op jit(solution)/shard_map/all_to_all | solution.py:475
  128.7 1.9 %shard_map.156 = bf16[256,512]{1,0:T(8,128)(2,1)} custom-call(bf16[4,256,128]{2,1,0:T(8,128)(2,1)} %all_to_all.11.pieces, f32[256,512]{1,0:T(8,128)} %get-tuple-element.89.cross), custom_call_target="tpu_custom_call" | custom-call | tf_op jit(solution)/shard_map/pallas_call | solution.py:497
  130.5 0.0 collective-permute-done.13.refs_3_
  130.6 0.0 collective-permute-done.11.refs_1_
  130.6 0.0 collective-permute-done.12.refs_2_
  130.6 0.7 copy-done.4
  131.3 0.1 copy-done.5
  131.5 0.2 copy-done.6
  131.6 5.6 %shard_map.157 = f32[2,128,896]{2,1,0:T(8,128)} custom-call(bf16[2,128,896]{2,1,0:T(8,128)(2,1)} %get-tuple-element.90.refs_0_, bf16[2,128,896]{2,1,0:T(8,128)(2,1)} %copy-done.5, bf16[2,128,896]{2,1,0:T(8,128)(2,1)} %copy-done.6, bf16[2,128,896]{2,1,0:T(8,128)(2,1)} %copy-done.4, bf16[896,896]{1,0:T(8,128)(2,1)} %get-tuple-element.96.refs_4_, ...), custom_call_target="tpu_custom_call" | custom-call | tf_op jit(solution)/shard_map/pallas_call | solution.py:481
  (16 shorter events, 0.0 us)
Async XLA Ops:
  7.2 96.9 %all-gather.3.cloned.1.call-start = ((), (), s32[]{:S(2)}) async-start(), calls=%async_computation.2 | async-start | bytes 2621440 | tf_op jit(solution)/shard_map/all_gather | solution.py:400
  7.2 16.2 %collective-permute-start = (bf16[2,128,896]{2,1,0:T(8,128)(2,1)}, bf16[2,128,896]{2,1,0:T(8,128)(2,1)S(1)}, u32[]{:S(2)}, u32[]{:S(2)}) collective-permute-start(bf16[2,128,896]{2,1,0:T(8,128)(2,1)} %nb_h.1), channel_id=1, source_target_pairs={{0,1},{1,0},{2,3},{3,2},{4,5},{5,4},{6,7},{7,6},{8,9},{9,8},{10,11... | collective-permute-start | bytes 1376264 | tf_op jit(solution)/shard_map/ppermute | solution.py:348
  17.1 14.5 %collective-permute-start.1 = (bf16[2,128,896]{2,1,0:T(8,128)(2,1)}, bf16[2,128,896]{2,1,0:T(8,128)(2,1)S(1)}, u32[]{:S(2)}, u32[]{:S(2)}) collective-permute-start(bf16[2,128,896]{2,1,0:T(8,128)(2,1)} %get-tuple-element.51.e00), channel_id=1, source_target_pairs={{0,2},{2,4},{4,6},{6,0},{1,3},{3,5},{5,7},{7,1},{8,10},{10,12},{12... | collective-permute-start | bytes 1376264 | tf_op jit(solution)/shard_map/ppermute | solution.py:371
  19.1 12.6 %collective-permute-start.2 = (bf16[2,128,896]{2,1,0:T(8,128)(2,1)}, bf16[2,128,896]{2,1,0:T(8,128)(2,1)S(1)}, u32[]{:S(2)}, u32[]{:S(2)}) collective-permute-start(bf16[2,128,896]{2,1,0:T(8,128)(2,1)} %get-tuple-element.51.e00), channel_id=1, source_target_pairs={{0,6},{2,0},{4,2},{6,4},{1,7},{3,1},{5,3},{7,5},{8,14},{10,8},{12,... | collective-permute-start | bytes 1376264 | tf_op jit(solution)/shard_map/ppermute | solution.py:372
  23.4 8.2 %copy-start.1 = (bf16[4,3,256,128]{3,2,1,0:T(8,128)(2,1)S(1)}, bf16[4,3,256,128]{3,2,1,0:T(8,128)(2,1)}, u32[]{:S(2)}) copy-start(bf16[4,3,256,128]{3,2,1,0:T(8,128)(2,1)} %shard_map.151) | copy-start | bytes 2359300
  23.4 0.8 copy-start.15
  30.7 17.4 %copy-start.2 = (bf16[2,128,896]{2,1,0:T(8,128)(2,1)S(1)}, bf16[2,128,896]{2,1,0:T(8,128)(2,1)}, u32[]{:S(2)}) copy-start(bf16[2,128,896]{2,1,0:T(8,128)(2,1)} %shard_map.150.e01) | copy-start | bytes 1376260
  31.6 29.9 %copy-start.8 = (bf16[2,128,896]{2,1,0:T(8,128)(2,1)}, bf16[2,128,896]{2,1,0:T(8,128)(2,1)S(1)}, u32[]{:S(2)}) copy-start(bf16[2,128,896]{2,1,0:T(8,128)(2,1)S(1)} %collective-permute-done.1.e30) | copy-start | bytes 1376260
  31.6 24.4 %copy-start.9 = (bf16[2,128,896]{2,1,0:T(8,128)(2,1)}, bf16[2,128,896]{2,1,0:T(8,128)(2,1)S(1)}, u32[]{:S(2)}) copy-start(bf16[2,128,896]{2,1,0:T(8,128)(2,1)S(1)} %collective-permute-done.2.e10) | copy-start | bytes 1376260
  47.2 8.8 %copy-start = (bf16[4,3,256,128]{3,2,1,0:T(8,128)(2,1)}, bf16[4,3,256,128]{3,2,1,0:T(8,128)(2,1)S(1)}, u32[]{:S(2)}) copy-start(bf16[4,3,256,128]{3,2,1,0:T(8,128)(2,1)S(1)} %all_to_all.10.pieces) | copy-start | bytes 2359300
  48.1 10.3 %collective-permute-start.3 = (bf16[2,128,896]{2,1,0:T(8,128)(2,1)S(1)}, bf16[2,128,896]{2,1,0:T(8,128)(2,1)S(1)}, u32[]{:S(2)}, u32[]{:S(2)}) collective-permute-start(bf16[2,128,896]{2,1,0:T(8,128)(2,1)S(1)} %copy-done.2), channel_id=1, source_target_pairs={{0,6},{2,0},{4,2},{6,4},{1,7},{3,1},{5,3},{7,5},{8,14},{10,8},{12,... | collective-permute-start | bytes 1376264 | tf_op jit(solution)/shard_map/ppermute | solution.py:384
  50.9 10.7 %collective-permute-start.4 = (bf16[2,128,896]{2,1,0:T(8,128)(2,1)S(1)}, bf16[2,128,896]{2,1,0:T(8,128)(2,1)S(1)}, u32[]{:S(2)}, u32[]{:S(2)}) collective-permute-start(bf16[2,128,896]{2,1,0:T(8,128)(2,1)S(1)} %copy-done.2), channel_id=1, source_target_pairs={{0,2},{2,4},{4,6},{6,0},{1,3},{3,5},{5,7},{7,1},{8,10},{10,12},{12... | collective-permute-start | bytes 1376264 | tf_op jit(solution)/shard_map/ppermute | solution.py:385
  58.4 12.9 %copy-start.10 = (bf16[2,128,896]{2,1,0:T(8,128)(2,1)}, bf16[2,128,896]{2,1,0:T(8,128)(2,1)S(1)}, u32[]{:S(2)}) copy-start(bf16[2,128,896]{2,1,0:T(8,128)(2,1)S(1)} %collective-permute-done.3.e11) | copy-start | bytes 1376260
  61.6 9.7 %copy-start.12 = (bf16[2,128,896]{2,1,0:T(8,128)(2,1)}, bf16[2,128,896]{2,1,0:T(8,128)(2,1)S(1)}, u32[]{:S(2)}) copy-start(bf16[2,128,896]{2,1,0:T(8,128)(2,1)S(1)} %collective-permute-done.4.e31) | copy-start | bytes 1376260
  61.6 9.7 %collective-permute-start.5 = (bf16[2,128,896]{2,1,0:T(8,128)(2,1)S(1)}, bf16[2,128,896]{2,1,0:T(8,128)(2,1)S(1)}, u32[]{:S(2)}, u32[]{:S(2)}) collective-permute-start(bf16[2,128,896]{2,1,0:T(8,128)(2,1)S(1)} %collective-permute-done.1.e30), channel_id=1, source_target_pairs={{0,2},{2,4},{4,6},{6,0},{1,3},{3,5},{5,7},{7,1},{8,10},{10,12},{12... | collective-permute-start | bytes 1376264 | tf_op jit(solution)/shard_map/ppermute | solution.py:398
  61.6 9.7 %collective-permute-start.6 = (bf16[2,128,896]{2,1,0:T(8,128)(2,1)S(1)}, bf16[2,128,896]{2,1,0:T(8,128)(2,1)S(1)}, u32[]{:S(2)}, u32[]{:S(2)}) collective-permute-start(bf16[2,128,896]{2,1,0:T(8,128)(2,1)S(1)} %collective-permute-done.3.e11), channel_id=1, source_target_pairs={{0,6},{2,0},{4,2},{6,4},{1,7},{3,1},{5,3},{7,5},{8,14},{10,8},{12,... | collective-permute-start | bytes 1376264 | tf_op jit(solution)/shard_map/ppermute | solution.py:399
  71.3 0.8 copy-start.13
  71.3 1.0 copy-start.14
  85.4 18.5 %copy-start.11 = (bf16[2,128,896]{2,1,0:T(8,128)(2,1)S(1)}, bf16[2,128,896]{2,1,0:T(8,128)(2,1)}, u32[]{:S(2)}) copy-start(bf16[2,128,896]{2,1,0:T(8,128)(2,1)} %get-tuple-element.83) | copy-start | bytes 1376260
  85.4 11.9 %collective-permute-start.7 = (bf16[2,128,896]{2,1,0:T(8,128)(2,1)}, bf16[2,128,896]{2,1,0:T(8,128)(2,1)S(1)}, u32[]{:S(2)}, u32[]{:S(2)}) collective-permute-start(bf16[2,128,896]{2,1,0:T(8,128)(2,1)} %get-tuple-element.78), channel_id=1, source_target_pairs={{0,6},{2,0},{4,2},{6,4},{1,7},{3,1},{5,3},{7,5},{8,14},{10,8},{12,... | collective-permute-start | bytes 1376264 | tf_op jit(solution)/shard_map/ppermute | solution.py:456
  88.6 12.1 %collective-permute-start.8 = (bf16[2,128,896]{2,1,0:T(8,128)(2,1)}, bf16[2,128,896]{2,1,0:T(8,128)(2,1)S(1)}, u32[]{:S(2)}, u32[]{:S(2)}) collective-permute-start(bf16[2,128,896]{2,1,0:T(8,128)(2,1)} %get-tuple-element.79), channel_id=1, source_target_pairs={{0,2},{2,4},{4,6},{6,0},{1,3},{3,5},{5,7},{7,1},{8,10},{10,12},{12... | collective-permute-start | bytes 1376264 | tf_op jit(solution)/shard_map/ppermute | solution.py:457
  101.8 11.0 %collective-permute-start.9 = (bf16[2,128,896]{2,1,0:T(8,128)(2,1)S(1)}, bf16[2,128,896]{2,1,0:T(8,128)(2,1)S(1)}, u32[]{:S(2)}, u32[]{:S(2)}) collective-permute-start(bf16[2,128,896]{2,1,0:T(8,128)(2,1)S(1)} %add_convert_fusion.2), channel_id=1, source_target_pairs={{0,6},{2,0},{4,2},{6,4},{1,7},{3,1},{5,3},{7,5},{8,14},{10,8},{12,... | collective-permute-start | bytes 1376264 | tf_op jit(solution)/shard_map/ppermute | solution.py:459
  102.1 12.3 %collective-permute-start.10 = (bf16[2,128,896]{2,1,0:T(8,128)(2,1)}, bf16[2,128,896]{2,1,0:T(8,128)(2,1)S(1)}, u32[]{:S(2)}, u32[]{:S(2)}) collective-permute-start(bf16[2,128,896]{2,1,0:T(8,128)(2,1)} %get-tuple-element.82), channel_id=1, source_target_pairs={{0,2},{2,4},{4,6},{6,0},{1,3},{3,5},{5,7},{7,1},{8,10},{10,12},{12... | collective-permute-start | bytes 1376264 | tf_op jit(solution)/shard_map/ppermute | solution.py:460
  104.1 10.4 %copy-start.7 = (bf16[2,128,896]{2,1,0:T(8,128)(2,1)S(1)}, bf16[2,128,896]{2,1,0:T(8,128)(2,1)}, u32[]{:S(2)}) copy-start(bf16[2,128,896]{2,1,0:T(8,128)(2,1)} %get-tuple-element.93) | copy-start | bytes 1376260
  112.8 4.9 %copy-start.16 = (bf16[2,128,896]{2,1,0:T(8,128)(2,1)S(1)}, bf16[2,128,896]{2,1,0:T(8,128)(2,1)}, u32[]{:S(2)}) copy-start(bf16[2,128,896]{2,1,0:T(8,128)(2,1)} %get-tuple-element.92) | copy-start | bytes 1376260
  112.8 6.1 %copy-start.3 = (bf16[4,256,128]{2,1,0:T(8,128)(2,1)S(1)}, bf16[4,256,128]{2,1,0:T(8,128)(2,1)}, u32[]{:S(2)}) copy-start(bf16[4,256,128]{2,1,0:T(8,128)(2,1)} %shard_map.155) | copy-start | bytes 786436
  114.6 15.9 %collective-permute-start.13 = (bf16[2,128,896]{2,1,0:T(8,128)(2,1)S(1)}, bf16[2,128,896]{2,1,0:T(8,128)(2,1)S(1)}, u32[]{:S(2)}, u32[]{:S(2)}) collective-permute-start(bf16[2,128,896]{2,1,0:T(8,128)(2,1)S(1)} %add_convert_fusion), channel_id=1, source_target_pairs={{0,1},{1,0},{2,3},{3,2},{4,5},{5,4},{6,7},{7,6},{8,9},{9,8},{10,11... | collective-permute-start | bytes 1376264 | tf_op jit(solution)/shard_map/ppermute | solution.py:477
  115.7 14.9 %collective-permute-start.11 = (bf16[2,128,896]{2,1,0:T(8,128)(2,1)S(1)}, bf16[2,128,896]{2,1,0:T(8,128)(2,1)S(1)}, u32[]{:S(2)}, u32[]{:S(2)}) collective-permute-start(bf16[2,128,896]{2,1,0:T(8,128)(2,1)S(1)} %add_convert_fusion.1), channel_id=1, source_target_pairs={{0,2},{2,4},{4,6},{6,0},{1,3},{3,5},{5,7},{7,1},{8,10},{10,12},{12... | collective-permute-start | bytes 1376264 | tf_op jit(solution)/shard_map/ppermute | solution.py:478
  117.7 12.8 %collective-permute-start.12 = (bf16[2,128,896]{2,1,0:T(8,128)(2,1)S(1)}, bf16[2,128,896]{2,1,0:T(8,128)(2,1)S(1)}, u32[]{:S(2)}, u32[]{:S(2)}) collective-permute-start(bf16[2,128,896]{2,1,0:T(8,128)(2,1)S(1)} %copy-done.16), channel_id=1, source_target_pairs={{0,6},{2,0},{4,2},{6,4},{1,7},{3,1},{5,3},{7,5},{8,14},{10,8},{12,... | collective-permute-start | bytes 1376264 | tf_op jit(solution)/shard_map/ppermute | solution.py:479
  130.5 0.8 copy-start.4
  130.6 0.9 copy-start.5
  130.6 1.0 copy-start.6
Sparse Core Ops, SparseCore 0:
  48.2 26.5 all-gather.2

commit v4 on v3

--- a/solution.py
+++ b/solution.py
@@ -1,4 +1,3 @@
-import functools
 import math
 
 import jax
@@ -118,23 +117,26 @@
     return jnp.concatenate(parts, axis=0)
 
 
-def encode_kernel(other, ids, nb_h, ctx_h, wq_h, wk_h, wv_h, wo_h, enc, *rest):
-    kept, (nb, ctx, wq, wk, wv, wo, sems) = rest[:-7], rest[-7:]
+def encode_kernel(
+    ids, nb_h, ctx_h, wq_h, wk_h, wv_h, wo_h, enc, wt, ek_out, ev_out, *scratch
+):
+    nb, ctx, wq, wk, wv, wo, sems = scratch
     both = ((nb_h, nb), (wq_h, wq), (ctx_h, ctx), (wk_h, wk), (wv_h, wv), (wo_h, wo))
     copies = [pltpu.make_async_copy(a, b, sems.at[i]) for i, (a, b) in enumerate(both)]
-    for c in copies:
+    for c in copies[:3]:
         c.start()
     slots, rows, width = nb.shape
     each = width // EHEADS
     copies[0].wait()
     x = nb[...].reshape(slots * rows, width)
     copies[1].wait()
+    for c in copies[3:]:
+        c.start()
     eq = mm(x, wq[...]).astype(BF16)
     copies[2].wait()
     contexts = []
     for t in range(slots):
-        pair = jnp.bitwise_xor(lax.axis_index("yh"), other)
-        mine = (lax.axis_index("z") * 2 + pair) * slots + t
+        mine = (lax.axis_index("z") * 2 + lax.axis_index("yh")) * slots + t
         span = jnp.int32(0)
         for c in range(1, ids.shape[1]):
             span = jnp.where((ids[0, c] == mine) | (ids[1, c] == mine), c, span)
@@ -152,8 +154,9 @@
         s = s.reshape(EHEADS, CL, rows)
         p = jnp.exp(s - jnp.max(s, axis=1, keepdims=True))
         w = (p * (1.0 / jnp.sum(p, axis=1, keepdims=True))).reshape(EHEADS * CL, rows)
-        for ref, value in zip(kept, (w, ek_t, ev_t)):
-            ref[t] = value
+        wt[t] = w
+        ek_out[t] = ek_t
+        ev_out[t] = ev_t
         mixed.append(mm_tn(w.astype(BF16), head_rows(ev_t)).astype(BF16))
     copies[5].wait()
     out = x.astype(F32) + mm(jnp.concatenate(mixed, axis=0), wo[...])
@@ -164,12 +167,14 @@
     given, out, here, sems = refs[:9], refs[9], refs[10:19], refs[19]
     d0, d1, d2, d3, wo, ev, wt, ek, wq = here
     loads = [pltpu.make_async_copy(a, b, sems.at[i]) for i, (a, b) in enumerate(zip(given, here))]
-    for c in loads:
+    for c in loads[:5]:
         c.start()
     slots, rows, width = d0.shape
     each = width // EHEADS
     for c in loads[:4]:
         c.wait()
+    for c in loads[5:]:
+        c.start()
     d = (d0[...].astype(F32) + d1[...].astype(F32)) + (d2[...].astype(F32) + d3[...].astype(F32))
     d = d.reshape(slots * rows, width)
     loads[4].wait()
@@ -189,9 +194,10 @@
     out[...] = (d + mm(jnp.concatenate(back, axis=0), wq[...])).reshape(slots, rows, width)
 
 
-def turn_kernel(kw, vw, wq, wo, kw_t, vw_t, wq_t, wo_t):
-    kw_t[...] = kw[...].T
-    vw_t[...] = vw[...].T
+def turn_kernel(kw, vw, wq, wo, kv_t, wq_t, wo_t):
+    width = kw.shape[1]
+    kv_t[:width] = kw[...].T
+    kv_t[width:] = vw[...].T
     wq_t[...] = wq[...].T
     wo_t[...] = wo[...].T
 
@@ -214,10 +220,11 @@
 
 def cross_kernel(ids, e00, e01, e10, e11, e20, e21, e30, e31, *rest):
     blocks = (e00, e01, e10, e11, e20, e21, e30, e31)
-    given, cross, outs = rest[:8], rest[8], rest[9:17]
-    table, held, sent, ck, cv, dk, dv, zero, in_sem, out_sem, given_sem = rest[17:28]
-    here = rest[28:]
-    kw, vw, qm_t, gm_t, q, g, kw_t, vw_t = here
+    given, cross, outs = rest[:7], rest[7], rest[8:16]
+    table, held, sent, ckv, dkv, zero, in_sem, out_sem, given_sem = rest[16:25]
+    kvw, qm_t, gm_t, q, g, kv_t = rest[25:]
+    width = q.shape[1]
+    here = (kvw.at[:, :width], kvw.at[:, width:], qm_t, gm_t, q, g, kv_t)
     loads = [
         pltpu.make_async_copy(a, b, given_sem.at[i]) for i, (a, b) in enumerate(zip(given, here))
     ]
@@ -245,55 +252,60 @@
         def _():
             pltpu.make_async_copy(blocks[i].at[t], held.at[n], in_sem.at[n]).start()
 
-    for c in loads[2:]:
-        c.start()
     for i, t in places:
 
         @pl.when(table[2 * i + t] < 0)
         def _():
             pltpu.make_async_copy(zero, outs[i].at[t], out_sem.at[2 * i + t]).start()
 
-    heads = q.shape[1] // HSIZE
+    heads = width // HSIZE
     pair = 2 * NL
     for half in range(2):
         first = half * (n_named // 2)
         for n in range(first, first + n_named // 2):
             pltpu.make_async_copy(e00.at[0], held.at[n], in_sem.at[n]).wait()
         e = held[first : first + n_named // 2].reshape(n_named // 2 * NL, -1)
-        at = slice(first * NL, (first + n_named // 2) * NL)
         if half == 0:
             loads[0].wait()
-        ck[at] = mm(e, kw[...]).astype(BF16)
-        if half == 0:
             loads[1].wait()
-        cv[at] = mm(e, vw[...]).astype(BF16)
+            for c in loads[2:]:
+                c.start()
+        ckv[first * NL : (first + n_named // 2) * NL] = mm(e, kvw[...]).astype(BF16)
     for c in loads[2:]:
         c.wait()
 
     def scores(c):
         at = slice(c * pair, (c + 1) * pair)
-        return mm(ck[at], qm_t[c]) * scale, mm(cv[at], gm_t[c])
+        return mm(ckv[at, :width], qm_t[c]), mm(ckv[at, width:], gm_t[c])
 
     def soften(s, dp):
-        p = jnp.exp(s - jnp.max(s, axis=0, keepdims=True))
+        p = jnp.exp2((s - jnp.max(s, axis=0, keepdims=True)) * (scale * LOG2E))
         p = p * (1.0 / jnp.sum(p, axis=0, keepdims=True))
-        ds = p * (dp - jnp.sum(p * dp, axis=0, keepdims=True)) * scale
+        ds = p * ((dp - jnp.sum(p * dp, axis=0, keepdims=True)) * scale)
         return p.astype(BF16), ds.astype(BF16)
 
     def products(c, pb, ds):
         at = slice(c * pair, (c + 1) * pair)
-        dk[at] = mm(ds, head_blocks(q[c * CL : (c + 1) * CL])).astype(BF16)
-        dv[at] = mm(pb, head_blocks(g[c * CL : (c + 1) * CL])).astype(BF16)
-        o = mm_tn(pb, cv[at])
+        dkv[at, :width] = mm(ds, head_blocks(q[c * CL : (c + 1) * CL])).astype(BF16)
+        dkv[at, width:] = mm(pb, head_blocks(g[c * CL : (c + 1) * CL])).astype(BF16)
+        pt = pb.T
         for h in range(heads):
-            cross[c * CL : (c + 1) * CL, h * HSIZE : (h + 1) * HSIZE] = o[
-                h * CL : (h + 1) * CL, h * HSIZE : (h + 1) * HSIZE
-            ]
+            cols = slice(h * HSIZE, (h + 1) * HSIZE)
+            cross[c * CL : (c + 1) * CL, cols] = mm(
+                pt[h * CL : (h + 1) * CL], ckv[at, width + h * HSIZE : width + (h + 1) * HSIZE]
+            )
 
     def back(c):
         at = slice(c * pair, (c + 1) * pair)
-        de = mm(dk[at], kw_t[...]) + mm(dv[at], vw_t[...])
-        sent[2 * c : 2 * c + 2] = de.astype(BF16).reshape(2, NL, -1)
+        sent[2 * c : 2 * c + 2] = mm(dkv[at], kv_t[...]).astype(BF16).reshape(2, NL, -1)
+
+    def send(low, high):
+        for i, t in places:
+            n = table[2 * i + t]
+
+            @pl.when((n >= low) & (n < high))
+            def _():
+                pltpu.make_async_copy(sent.at[n], outs[i].at[t], out_sem.at[2 * i + t]).start()
 
     ahead = scores(0)
     for c in range(spans):
@@ -304,14 +316,9 @@
         if c >= 1:
             back(c - 1)
         products(c, *soft)
+    send(0, n_named - 2)
     back(spans - 1)
-    for i, t in places:
-        n = table[2 * i + t]
-
-        @pl.when(n >= 0)
-        def _():
-            pltpu.make_async_copy(sent.at[n], outs[i].at[t], out_sem.at[2 * i + t]).start()
-
+    send(n_named - 2, n_named)
     for i, t in places:
         pltpu.make_async_copy(zero, outs[i].at[t], out_sem.at[2 * i + t]).wait()
 
@@ -345,29 +352,22 @@
 
     ids = neighbour_ids.T
 
-    raw = lax.ppermute(neighbours, "yh", shift(2, 1))
-
-    def encode(other, blocks, kept):
-        return call(
-            functools.partial(encode_kernel, other),
-            out_shape=[struct((slots, nl, ew), BF16)] + kept,
-            in_specs=[smem()] + [hbm()] * 6,
-            out_specs=[vmem()] * (1 + len(kept)),
-            scratch_shapes=[pltpu.VMEM(neighbours.shape, BF16), pltpu.VMEM(span_ctx.shape, BF16)]
-            + [pltpu.VMEM((ew, ew), BF16)] * 4
-            + [pltpu.SemaphoreType.DMA((6,))],
-        )(ids, blocks, span_ctx, enc_q, enc_k, enc_v, enc_o)
-
-    e00, wt, ek, ev = encode(
-        0,
-        neighbours,
-        [
+    e00, wt, ek, ev = call(
+        encode_kernel,
+        out_shape=[
+            struct((slots, nl, ew), BF16),
             struct((slots, EHEADS * CL, nl), F32),
             struct((slots, CL, ew), BF16),
             struct((slots, CL, ew), BF16),
         ],
-    )
-
+        in_specs=[smem()] + [hbm()] * 6,
+        out_specs=[vmem()] * 4,
+        scratch_shapes=[pltpu.VMEM(neighbours.shape, BF16), pltpu.VMEM(span_ctx.shape, BF16)]
+        + [pltpu.VMEM((ew, ew), BF16)] * 4
+        + [pltpu.SemaphoreType.DMA((6,))],
+    )(ids, neighbours, span_ctx, enc_q, enc_k, enc_v, enc_o)
+
+    e01 = lax.ppermute(e00, "yh", shift(2, 1))
     e30 = lax.ppermute(e00, "z", shift(NX, 1))
     e10 = lax.ppermute(e00, "z", shift(NX, -1))
 
@@ -378,26 +378,26 @@
         in_specs=[vmem()] * 3,
         out_specs=vmem(),
     )(self_q, self_k, self_v)
-    raw, _ = after((raw, wt))
-    (e01,) = encode(1, raw, [])
+    pieces = lax.all_to_all(packed, "x", 0, 0)
+    own_kv = pieces[:, 1:]
+
     e01, e30, e10, packed = after((e01, e30, e10, packed))
     e11 = lax.ppermute(e01, "z", shift(NX, -1))
     e31 = lax.ppermute(e01, "z", shift(NX, 1))
-    pieces = lax.all_to_all(packed, "x", 0, 0)
 
     weights = after((cross_k_weight, cross_v_weight, enc_q, enc_o, e01))[:4]
     turned = call(
         turn_kernel,
-        out_shape=[struct((width, ew), BF16)] * 2 + [struct((ew, ew), BF16)] * 2,
+        out_shape=[struct((2 * width, ew), BF16)] + [struct((ew, ew), BF16)] * 2,
         in_specs=[vmem()] * 4,
-        out_specs=[vmem()] * 4,
+        out_specs=[vmem()] * 3,
     )(*weights)
 
-    e30, e11, e31, *turned = after((e30, e11, e31, *turned))
-    kw_t, vw_t, wq_t, wo_t = turned
+    e30, e11, e31, own_kv, *turned = after((e30, e11, e31, own_kv, *turned))
+    kv_t, wq_t, wo_t = turned
     e20 = lax.ppermute(e30, "z", shift(NX, 1))
     e21 = lax.ppermute(e11, "z", shift(NX, -1))
-    kv = lax.all_gather(pieces[:, 1:], ("yl", "core"), axis=0)
+    kv = lax.all_gather(own_kv, ("yl", "core"), axis=0)
 
     queries, grads, _ = after((cross_q, mixed_grad, e11))
     qm_t, gm_t = call(
@@ -410,25 +410,23 @@
     cross, *p = call(
         cross_kernel,
         out_shape=[struct((rows, width), F32)] + [struct((slots, nl, ew), BF16)] * 8,
-        in_specs=[smem()] + [hbm()] * 16,
+        in_specs=[smem()] + [hbm()] * 15,
         out_specs=[vmem()] + [hbm()] * 8,
         scratch_shapes=[
             pltpu.SMEM((16,), jnp.int32),
             pltpu.VMEM((n_named, nl, ew), BF16),
             pltpu.VMEM((n_named, nl, ew), BF16),
-            pltpu.VMEM((n_named * nl, width), BF16),
-            pltpu.VMEM((n_named * nl, width), BF16),
-            pltpu.VMEM((n_named * nl, width), BF16),
-            pltpu.VMEM((n_named * nl, width), BF16),
+            pltpu.VMEM((n_named * nl, 2 * width), BF16),
+            pltpu.VMEM((n_named * nl, 2 * width), BF16),
             pltpu.VMEM((nl, ew), BF16),
             pltpu.SemaphoreType.DMA((n_named,)),
             pltpu.SemaphoreType.DMA((16,)),
-            pltpu.SemaphoreType.DMA((8,)),
+            pltpu.SemaphoreType.DMA((7,)),
+            pltpu.VMEM((ew, 2 * width), BF16),
         ]
-        + [pltpu.VMEM((ew, width), BF16)] * 2
         + [pltpu.VMEM((spans, width, width // HSIZE * CL), BF16)] * 2
         + [pltpu.VMEM((rows, width), BF16)] * 2
-        + [pltpu.VMEM((width, ew), BF16)] * 2,
+        + [pltpu.VMEM((2 * width, ew), BF16)],
     )(
         ids,
         e00,
@@ -445,8 +443,7 @@
         gm_t,
         cross_q,
         mixed_grad,
-        kw_t,
-        vw_t,
+        kv_t,
     )
     p00, p01, p10, p11, p20, p21, p30, p31 = p
 
@@ -455,11 +452,7 @@
 
     far1 = lax.ppermute(p21, "z", shift(NX, -1))
     far0 = lax.ppermute(p20, "z", shift(NX, 1))
-    far1, far0, p11 = after((far1, far0, p11))
-    down1 = lax.ppermute(add(p31, far1), "z", shift(NX, -1))
-    up1 = lax.ppermute(p11, "z", shift(NX, 1))
-    near0 = add(p10, far0)
-    kv, _ = after((kv, far1))
+    kv, _ = after((kv, cross))
     outs = call(
         attend_kernel,
         out_shape=struct((NX, rows, HSIZE), BF16),
@@ -471,8 +464,12 @@
             pltpu.VMEM((rows, 1), F32),
         ],
     )(pieces, kv)
-    down1, up1, near0, p30, outs = after((down1, up1, near0, p30, outs))
+    far1, far0, p11, outs = after((far1, far0, p11, outs))
     selfs = lax.all_to_all(outs, "x", 0, 0)
+    down1 = lax.ppermute(add(p31, far1), "z", shift(NX, -1))
+    up1 = lax.ppermute(p11, "z", shift(NX, 1))
+    near0 = add(p10, far0)
+    down1, up1, near0, p30 = after((down1, up1, near0, p30))
     theirs = (p01.astype(F32) + up1.astype(F32) + down1.astype(F32)).astype(BF16)
     other = lax.ppermute(theirs, "yh", shift(2, 1))
     up0 = lax.ppermute(near0, "z", shift(NX, 1))

time: 144 us -> 132 us (0.917)
  blocking collectives: 25.3 us -> 10.8 us
  Pallas kernels: 52.6 us -> 45.8 us
  starting transfers between devices: 23.1 us -> 29.1 us
  waiting for transfers between devices: 23.8 us -> 28.1 us
    all_to_all x1 -> x0, blocking collectives: 15.5 us -> none  [local(): pieces = lax.all_to_all(packed, 'x', 0, 0)]
    ppermute x1, waiting for transfers between devices: 0.01 us -> 8.8 us  [local(): down1 = lax.ppermute(add(p31, far1), 'z', shift(NX, -1))]
    ppermute x1, waiting for transfers between devices: 8.77 us -> 0.01 us  [local(): far1 = lax.ppermute(p21, 'z', shift(NX, -1))]
    pallas_call x3 -> x2, Pallas kernels: 18.1 us -> 12.5 us  [the longest x1 7.25 us: local(): call(encode_kernel, out_shape=[struct((slots, nl, ew), BF16), struct((slo...]
    all_to_all x0 -> x1, starting transfers between devices: none -> 4.29 us  [local(): pieces = lax.all_to_all(packed, 'x', 0, 0)]
    ppermute x1, waiting for transfers between devices: 0.94 us -> 3.78 us  [local(): e30 = lax.ppermute(e00, 'z', shift(NX, 1))]
    ppermute x1, waiting for transfers between devices: 3.36 us -> 1.1 us  [local(): far0 = lax.ppermute(p20, 'z', shift(NX, 1))]
    ppermute x1, starting transfers between devices: 1.21 us -> 3.23 us  [local(): down0 = lax.ppermute(p30, 'z', shift(NX, -1))]
  transfers between devices with their start and end apart: 15 -> 16, of which waited for: 7 -> 8; matrix products, arithmetic and copies ran while one was open for 1% -> 1% of each run, Pallas kernels for 33% -> 25%
where the time goes in v4:
time: 132 us; the launch traced here: 131 us
  Pallas kernels  45.8 us (35%)
  starting transfers between devices  29.1 us (22%)
  waiting for transfers between devices  28.1 us (21%)
  between operations  14.2 us (11%)
  blocking collectives  10.8 us (8%)
  local copies, waits for them, and re-layouts  3 us (2%)
    pallas_call x1, Pallas kernels, local(): call(cross_kernel, out_shape=[struct((rows, width), F32)] + [struct((slot...  11.9 us
    all_to_all x1, blocking collectives, local(): selfs = lax.all_to_all(outs, 'x', 0, 0)  10.8 us
    ppermute x1, waiting for transfers between devices, local(): down1 = lax.ppermute(add(p31, far1), 'z', shift(NX, -1))  8.8 us
    pallas_call x1, Pallas kernels, local(): call(attend_kernel, out_shape=struct((NX, rows, HSIZE), BF16), in_specs=[...  8.78 us
    pallas_call x1, Pallas kernels, local(): call(encode_kernel, out_shape=[struct((slots, nl, ew), BF16), struct((slo...  7.25 us
    pallas_call x1, Pallas kernels, local(): call(pullback_kernel, out_shape=struct((slots, nl, ew), F32), in_specs=[h...  5.59 us
    pallas_call x1, Pallas kernels, local(): call(turn_kernel, out_shape=[struct((2 * width, ew), BF16)] + [struct((ew...  5.25 us
    ppermute x1, waiting for transfers between devices, local(): e20 = lax.ppermute(e30, 'z', shift(NX, 1))  4.87 us
  transfers between devices with their start and end apart: 16, of which 8 were waited for; matrix products, arithmetic and copies ran while one was open for 1% of the time, Pallas kernels for 25%

profile of v4, /device:TPU:0, one launch (start us, length us, event | category | flops | bytes accessed | tf_op | source)
XLA Modules:
  0.0 131.4 jit_solution(1829630324500432085)
XLA Ops:
  7.2 7.2 %shard_map.149 = (bf16[2,128,896]{2,1,0:T(8,128)(2,1)}, f32[2,256,128]{2,1,0:T(8,128)}, bf16[2,64,896]{2,1,0:T(8,128)(2,1)}, bf16[2,64,896]{2,1,0:T(8,128)(2,1)}) custom-call(s32[2,4]{1,0:T(2,128)} %bitcast.3, bf16[2,128,896]{2,1,0:T(8,128)(2,1)} %nb_h.1, bf16[256,896]{1,0:T(8,128)(2,1)} %ctx_h.1, bf16[896,896]{1,0:T(8,128)(2,1)} %wq, ...), custom_call_target="tpu_custom_call" | custom-call | tf_op jit(solution)/shard_map/pallas_call | solution.py:355
  14.4 3.4 %collective-permute-start = (bf16[2,128,896]{2,1,0:T(8,128)(2,1)}, bf16[2,128,896]{2,1,0:T(8,128)(2,1)S(1)}, u32[]{:S(2)}, u32[]{:S(2)}) collective-permute-start(bf16[2,128,896]{2,1,0:T(8,128)(2,1)} %get-tuple-element.48.e00), channel_id=1, source_target_pairs={{0,1},{1,0},{2,3},{3,2},{4,5},{5,4},{6,7},{7,6},{8,9},{9,8},{10,11... | collective-permute-start | bytes 1376264 | tf_op jit(solution)/shard_map/ppermute | solution.py:370
  17.8 1.9 %collective-permute-start.1 = (bf16[2,128,896]{2,1,0:T(8,128)(2,1)}, bf16[2,128,896]{2,1,0:T(8,128)(2,1)S(1)}, u32[]{:S(2)}, u32[]{:S(2)}) collective-permute-start(bf16[2,128,896]{2,1,0:T(8,128)(2,1)} %get-tuple-element.48.e00), channel_id=1, source_target_pairs={{0,2},{2,4},{4,6},{6,0},{1,3},{3,5},{5,7},{7,1},{8,10},{10,12},{12... | collective-permute-start | bytes 1376264 | tf_op jit(solution)/shard_map/ppermute | solution.py:371
  19.7 2.1 %collective-permute-start.2 = (bf16[2,128,896]{2,1,0:T(8,128)(2,1)}, bf16[2,128,896]{2,1,0:T(8,128)(2,1)S(1)}, u32[]{:S(2)}, u32[]{:S(2)}) collective-permute-start(bf16[2,128,896]{2,1,0:T(8,128)(2,1)} %get-tuple-element.48.e00), channel_id=1, source_target_pairs={{0,6},{2,0},{4,2},{6,4},{1,7},{3,1},{5,3},{7,5},{8,14},{10,8},{12,... | collective-permute-start | bytes 1376264 | tf_op jit(solution)/shard_map/ppermute | solution.py:372
  21.8 2.1 %shard_map.150 = bf16[4,3,256,128]{3,2,1,0:T(8,128)(2,1)} custom-call(bf16[256,512]{1,0:T(8,128)(2,1)} %q_ref, bf16[256,512]{1,0:T(8,128)(2,1)} %k_ref, bf16[256,512]{1,0:T(8,128)(2,1)} %v_ref), custom_call_target="tpu_custom_call" | custom-call | tf_op jit(solution)/shard_map/pallas_call | solution.py:375
  23.9 4.3 %all-to-all-start = ((bf16[4,3,256,128]{3,2,1,0:T(8,128)(2,1)}), bf16[4,3,256,128]{3,2,1,0:T(8,128)(2,1)S(1)}, u32[]{:S(2)}, u32[]{:S(2)}) async-start(bf16[4,3,256,128]{3,2,1,0:T(8,128)(2,1)} %shard_map.150), calls=%async_computation | async-start | bytes 1572864 | tf_op jit(solution)/shard_map/all_to_all | solution.py:381
  28.2 0.0 all-gather.3.cloned.1.call-start
  28.2 0.3 collective-permute-done.e01
  28.5 3.8 %collective-permute-done.1.e30 = bf16[2,128,896]{2,1,0:T(8,128)(2,1)S(1)} collective-permute-done((bf16[2,128,896]{2,1,0:T(8,128)(2,1)}, bf16[2,128,896]{2,1,0:T(8,128)(2,1)S(1)}, u32[]{:S(2)}, u32[]{:S(2)}) %collective-permute-start.1) | collective-permute-done | bytes 458784 | tf_op jit(solution)/shard_map/ppermute | solution.py:371
  32.3 0.0 collective-permute-done.2.e10
  32.3 2.9 %collective-permute-start.3 = (bf16[2,128,896]{2,1,0:T(8,128)(2,1)S(1)}, bf16[2,128,896]{2,1,0:T(8,128)(2,1)S(1)}, u32[]{:S(2)}, u32[]{:S(2)}) collective-permute-start(bf16[2,128,896]{2,1,0:T(8,128)(2,1)S(1)} %collective-permute-done.e01), channel_id=1, source_target_pairs={{0,6},{2,0},{4,2},{6,4},{1,7},{3,1},{5,3},{7,5},{8,14},{10,8},{12,... | collective-permute-start | bytes 1376264 | tf_op jit(solution)/shard_map/ppermute | solution.py:385
  35.2 0.0 collective-permute-start.4
  35.2 5.2 %shard_map.151 = (bf16[1024,896]{1,0:T(8,128)(2,1)}, bf16[896,896]{1,0:T(8,128)(2,1)}, bf16[896,896]{1,0:T(8,128)(2,1)}) custom-call(bf16[896,512]{1,0:T(8,128)(2,1)} %rest_0_.1, bf16[896,512]{1,0:T(8,128)(2,1)} %rest_1_.1, bf16[896,896]{1,0:T(8,128)(2,1)} %wq, bf16[896,896]{1,0:T(8,128)(2,1)} %wo), custom_call_target="tpu_custom_call" | custom-call | tf_op jit(solution)/shard_map/pallas_call | solution.py:389
  40.5 0.0 copy-done.6
  40.5 0.0 copy-done.8
  40.5 0.0 all-to-all-done.pieces
  40.5 0.0 copy-start
  40.5 0.9 slice.4
  41.4 2.4 %collective-permute-done.3.e11 = bf16[2,128,896]{2,1,0:T(8,128)(2,1)S(1)} collective-permute-done((bf16[2,128,896]{2,1,0:T(8,128)(2,1)S(1)}, bf16[2,128,896]{2,1,0:T(8,128)(2,1)S(1)}, u32[]{:S(2)}, u32[]{:S(2)}) %collective-permute-start.3) | collective-permute-done | bytes 458784 | tf_op jit(solution)/shard_map/ppermute | solution.py:385
  43.8 3.4 %collective-permute-done.4.e31 = bf16[2,128,896]{2,1,0:T(8,128)(2,1)S(1)} collective-permute-done((bf16[2,128,896]{2,1,0:T(8,128)(2,1)S(1)}, bf16[2,128,896]{2,1,0:T(8,128)(2,1)S(1)}, u32[]{:S(2)}, u32[]{:S(2)}) %collective-permute-start.4) | collective-permute-done | bytes 458784 | tf_op jit(solution)/shard_map/ppermute | solution.py:386
  47.2 0.0 all-gather.3.cloned.1.call-update
  47.3 0.0 copy-done.7
  47.3 0.1 collective-permute-start.5
  47.4 3.2 %collective-permute-start.6 = (bf16[2,128,896]{2,1,0:T(8,128)(2,1)S(1)}, bf16[2,128,896]{2,1,0:T(8,128)(2,1)S(1)}, u32[]{:S(2)}, u32[]{:S(2)}) collective-permute-start(bf16[2,128,896]{2,1,0:T(8,128)(2,1)S(1)} %collective-permute-done.3.e11), channel_id=1, source_target_pairs={{0,6},{2,0},{4,2},{6,4},{1,7},{3,1},{5,3},{7,5},{8,14},{10,8},{12,... | collective-permute-start | bytes 1376264 | tf_op jit(solution)/shard_map/ppermute | solution.py:399
  50.6 3.0 %shard_map.152 = (bf16[4,512,256]{2,1,0:T(8,128)(2,1)}, bf16[4,512,256]{2,1,0:T(8,128)(2,1)}) custom-call(bf16[256,512]{1,0:T(8,128)(2,1)} %rest_4_.1, bf16[256,512]{1,0:T(8,128)(2,1)} %rest_5_.1), custom_call_target="tpu_custom_call" | custom-call | tf_op jit(solution)/shard_map/pallas_call | solution.py:403
  53.5 4.9 %collective-permute-done.5.e20 = bf16[2,128,896]{2,1,0:T(8,128)(2,1)S(1)} collective-permute-done((bf16[2,128,896]{2,1,0:T(8,128)(2,1)S(1)}, bf16[2,128,896]{2,1,0:T(8,128)(2,1)S(1)}, u32[]{:S(2)}, u32[]{:S(2)}) %collective-permute-start.5) | collective-permute-done | bytes 458784 | tf_op jit(solution)/shard_map/ppermute | solution.py:398
  58.4 0.0 collective-permute-done.6.e21
  58.4 0.0 copy-done.9
  58.4 0.0 copy-done.10
  58.4 0.8 copy-done.13
  59.2 0.2 copy-done.14
  59.4 11.9 %shard_map.153 = (f32[256,512]{1,0:T(8,128)}, bf16[2,128,896]{2,1,0:T(8,128)(2,1)}, bf16[2,128,896]{2,1,0:T(8,128)(2,1)}, bf16[2,128,896]{2,1,0:T(8,128)(2,1)}, ...) custom-call(s32[2,4]{1,0:T(2,128)} %bitcast.4, ...), custom_call_target="tpu_custom_call" | custom-call | tf_op jit(solution)/shard_map/pallas_call | solution.py:410
  71.3 0.0 copy-done
  71.3 0.0 copy-start.12
  71.3 2.9 %collective-permute-start.7 = (bf16[2,128,896]{2,1,0:T(8,128)(2,1)}, bf16[2,128,896]{2,1,0:T(8,128)(2,1)S(1)}, u32[]{:S(2)}, u32[]{:S(2)}) collective-permute-start(bf16[2,128,896]{2,1,0:T(8,128)(2,1)} %get-tuple-element.71), channel_id=1, source_target_pairs={{0,6},{2,0},{4,2},{6,4},{1,7},{3,1},{5,3},{7,5},{8,14},{10,8},{12,... | collective-permute-start | bytes 1376264 | tf_op jit(solution)/shard_map/ppermute | solution.py:453
  74.2 0.0 collective-permute-start.8
  74.2 8.8 %shard_map.154 = bf16[4,256,128]{2,1,0:T(8,128)(2,1)} custom-call(bf16[4,3,256,128]{3,2,1,0:T(8,128)(2,1)} %copy-done, bf16[4,4,2,256,128]{4,3,2,1,0:T(8,128)(2,1)} %bitcast.2), custom_call_target="tpu_custom_call" | custom-call | tf_op jit(solution)/shard_map/pallas_call | solution.py:456
  83.0 0.0 collective-permute-done.7
  83.0 1.1 collective-permute-done.8
  84.1 0.0 copy-done.12
  84.1 0.1 add_convert_fusion.2
  84.3 2.2 %collective-permute-start.9 = (bf16[2,128,896]{2,1,0:T(8,128)(2,1)S(1)}, bf16[2,128,896]{2,1,0:T(8,128)(2,1)S(1)}, u32[]{:S(2)}, u32[]{:S(2)}) collective-permute-start(bf16[2,128,896]{2,1,0:T(8,128)(2,1)S(1)} %add_convert_fusion.2), channel_id=1, source_target_pairs={{0,6},{2,0},{4,2},{6,4},{1,7},{3,1},{5,3},{7,5},{8,14},{10,8},{12,... | collective-permute-start | bytes 1376264 | tf_op jit(solution)/shard_map/ppermute | solution.py:469
  86.5 0.0 copy-done.16
  86.5 0.0 collective-permute-start.10
  86.5 0.0 copy-done.11
  86.5 0.0 copy-start.1
  86.5 0.1 add_convert_fusion.1
  86.6 8.8 %collective-permute-done.9 = bf16[2,128,896]{2,1,0:T(8,128)(2,1)S(1)} collective-permute-done((bf16[2,128,896]{2,1,0:T(8,128)(2,1)S(1)}, bf16[2,128,896]{2,1,0:T(8,128)(2,1)S(1)}, u32[]{:S(2)}, u32[]{:S(2)}) %collective-permute-start.9) | collective-permute-done | bytes 458784 | tf_op jit(solution)/shard_map/ppermute | solution.py:469
  95.4 3.4 %collective-permute-done.10 = bf16[2,128,896]{2,1,0:T(8,128)(2,1)S(1)} collective-permute-done((bf16[2,128,896]{2,1,0:T(8,128)(2,1)S(1)}, bf16[2,128,896]{2,1,0:T(8,128)(2,1)S(1)}, u32[]{:S(2)}, u32[]{:S(2)}) %collective-permute-start.10) | collective-permute-done | bytes 458784 | tf_op jit(solution)/shard_map/ppermute | solution.py:470
  98.8 0.2 add_convert_fusion
  99.0 2.8 %collective-permute-start.13 = (bf16[2,128,896]{2,1,0:T(8,128)(2,1)S(1)}, bf16[2,128,896]{2,1,0:T(8,128)(2,1)S(1)}, u32[]{:S(2)}, u32[]{:S(2)}) collective-permute-start(bf16[2,128,896]{2,1,0:T(8,128)(2,1)S(1)} %add_convert_fusion), channel_id=1, source_target_pairs={{0,1},{1,0},{2,3},{3,2},{4,5},{5,4},{6,7},{7,6},{8,9},{9,8},{10,11... | collective-permute-start | bytes 1376264 | tf_op jit(solution)/shard_map/ppermute | solution.py:474
  101.8 0.0 collective-permute-start.11
  101.8 3.2 %collective-permute-start.12 = (bf16[2,128,896]{2,1,0:T(8,128)(2,1)S(1)}, bf16[2,128,896]{2,1,0:T(8,128)(2,1)S(1)}, u32[]{:S(2)}, u32[]{:S(2)}) collective-permute-start(bf16[2,128,896]{2,1,0:T(8,128)(2,1)S(1)} %copy-done.15), channel_id=1, source_target_pairs={{0,6},{2,0},{4,2},{6,4},{1,7},{3,1},{5,3},{7,5},{8,14},{10,8},{12,... | collective-permute-start | bytes 1376264 | tf_op jit(solution)/shard_map/ppermute | solution.py:476
  105.1 0.0 copy-done.1
  105.1 10.8 %all_to_all.10.pieces = bf16[4,256,128]{2,1,0:T(8,128)(2,1)} all-to-all(bf16[4,256,128]{2,1,0:T(8,128)(2,1)S(1)} %copy-done.1), channel_id=1, replica_groups=mesh['x'=4,'yl'=2,'core'=2,'z'=4,'yh'=2] {'x'}, dimensions={0} | all-to-all | bytes 524288 | tf_op jit(solution)/shard_map/all_to_all | solution.py:468
  115.9 1.9 %shard_map.155 = bf16[256,512]{1,0:T(8,128)(2,1)} custom-call(bf16[4,256,128]{2,1,0:T(8,128)(2,1)} %all_to_all.10.pieces, f32[256,512]{1,0:T(8,128)} %get-tuple-element.75.cross), custom_call_target="tpu_custom_call" | custom-call | tf_op jit(solution)/shard_map/pallas_call | solution.py:494
  117.7 0.0 collective-permute-done.13.refs_3_
  117.7 0.0 collective-permute-done.11.refs_1_
  117.8 0.0 copy-start.3
  117.8 0.0 collective-permute-done.12.refs_2_
  117.8 0.8 copy-done.2
  118.6 0.1 copy-done.3
  118.7 0.2 copy-done.4
  118.9 5.6 %shard_map.156 = f32[2,128,896]{2,1,0:T(8,128)} custom-call(bf16[2,128,896]{2,1,0:T(8,128)(2,1)} %get-tuple-element.78.refs_0_, bf16[2,128,896]{2,1,0:T(8,128)(2,1)} %copy-done.3, bf16[2,128,896]{2,1,0:T(8,128)(2,1)} %copy-done.4, bf16[2,128,896]{2,1,0:T(8,128)(2,1)} %copy-done.2, bf16[896,896]{1,0:T(8,128)(2,1)} %get-tuple-element.90.refs_4_, ...), custom_call_target="tpu_custom_call" | custom-call | tf_op jit(solution)/shard_map/pallas_call | solution.py:478
  (16 shorter events, 0.0 us)
Async XLA Ops:
  14.4 14.1 %collective-permute-start = (bf16[2,128,896]{2,1,0:T(8,128)(2,1)}, bf16[2,128,896]{2,1,0:T(8,128)(2,1)S(1)}, u32[]{:S(2)}, u32[]{:S(2)}) collective-permute-start(bf16[2,128,896]{2,1,0:T(8,128)(2,1)} %get-tuple-element.48.e00), channel_id=1, source_target_pairs={{0,1},{1,0},{2,3},{3,2},{4,5},{5,4},{6,7},{7,6},{8,9},{9,8},{10,11... | collective-permute-start | bytes 1376264 | tf_op jit(solution)/shard_map/ppermute | solution.py:370
  17.8 14.5 %collective-permute-start.1 = (bf16[2,128,896]{2,1,0:T(8,128)(2,1)}, bf16[2,128,896]{2,1,0:T(8,128)(2,1)S(1)}, u32[]{:S(2)}, u32[]{:S(2)}) collective-permute-start(bf16[2,128,896]{2,1,0:T(8,128)(2,1)} %get-tuple-element.48.e00), channel_id=1, source_target_pairs={{0,2},{2,4},{4,6},{6,0},{1,3},{3,5},{5,7},{7,1},{8,10},{10,12},{12... | collective-permute-start | bytes 1376264 | tf_op jit(solution)/shard_map/ppermute | solution.py:371
  19.7 12.6 %collective-permute-start.2 = (bf16[2,128,896]{2,1,0:T(8,128)(2,1)}, bf16[2,128,896]{2,1,0:T(8,128)(2,1)S(1)}, u32[]{:S(2)}, u32[]{:S(2)}) collective-permute-start(bf16[2,128,896]{2,1,0:T(8,128)(2,1)} %get-tuple-element.48.e00), channel_id=1, source_target_pairs={{0,6},{2,0},{4,2},{6,4},{1,7},{3,1},{5,3},{7,5},{8,14},{10,8},{12,... | collective-permute-start | bytes 1376264 | tf_op jit(solution)/shard_map/ppermute | solution.py:372
  23.9 16.5 %all-to-all-start = ((bf16[4,3,256,128]{3,2,1,0:T(8,128)(2,1)}), bf16[4,3,256,128]{3,2,1,0:T(8,128)(2,1)S(1)}, u32[]{:S(2)}, u32[]{:S(2)}) async-start(bf16[4,3,256,128]{3,2,1,0:T(8,128)(2,1)} %shard_map.150), calls=%async_computation | async-start | bytes 1572864 | tf_op jit(solution)/shard_map/all_to_all | solution.py:381
  28.2 46.0 %all-gather.3.cloned.1.call-start = ((), (), s32[]{:S(2)}) async-start(), calls=%async_computation.2 | async-start | bytes 2621440 | tf_op jit(solution)/shard_map/all_gather | solution.py:400
  28.5 12.0 %copy-start.6 = (bf16[2,128,896]{2,1,0:T(8,128)(2,1)}, bf16[2,128,896]{2,1,0:T(8,128)(2,1)S(1)}, u32[]{:S(2)}) copy-start(bf16[2,128,896]{2,1,0:T(8,128)(2,1)S(1)} %collective-permute-done.e01) | copy-start | bytes 1376260
  32.3 15.0 %copy-start.7 = (bf16[2,128,896]{2,1,0:T(8,128)(2,1)}, bf16[2,128,896]{2,1,0:T(8,128)(2,1)S(1)}, u32[]{:S(2)}) copy-start(bf16[2,128,896]{2,1,0:T(8,128)(2,1)S(1)} %collective-permute-done.1.e30) | copy-start | bytes 1376260
  32.3 8.2 %copy-start.8 = (bf16[2,128,896]{2,1,0:T(8,128)(2,1)}, bf16[2,128,896]{2,1,0:T(8,128)(2,1)S(1)}, u32[]{:S(2)}) copy-start(bf16[2,128,896]{2,1,0:T(8,128)(2,1)S(1)} %collective-permute-done.2.e10) | copy-start | bytes 1376260
  32.3 11.5 %collective-permute-start.3 = (bf16[2,128,896]{2,1,0:T(8,128)(2,1)S(1)}, bf16[2,128,896]{2,1,0:T(8,128)(2,1)S(1)}, u32[]{:S(2)}, u32[]{:S(2)}) collective-permute-start(bf16[2,128,896]{2,1,0:T(8,128)(2,1)S(1)} %collective-permute-done.e01), channel_id=1, source_target_pairs={{0,6},{2,0},{4,2},{6,4},{1,7},{3,1},{5,3},{7,5},{8,14},{10,8},{12,... | collective-permute-start | bytes 1376264 | tf_op jit(solution)/shard_map/ppermute | solution.py:385
  35.2 12.0 %collective-permute-start.4 = (bf16[2,128,896]{2,1,0:T(8,128)(2,1)S(1)}, bf16[2,128,896]{2,1,0:T(8,128)(2,1)S(1)}, u32[]{:S(2)}, u32[]{:S(2)}) collective-permute-start(bf16[2,128,896]{2,1,0:T(8,128)(2,1)S(1)} %collective-permute-done.e01), channel_id=1, source_target_pairs={{0,2},{2,4},{4,6},{6,0},{1,3},{3,5},{5,7},{7,1},{8,10},{10,12},{12... | collective-permute-start | bytes 1376264 | tf_op jit(solution)/shard_map/ppermute | solution.py:386
  40.5 30.8 %copy-start = (bf16[4,3,256,128]{3,2,1,0:T(8,128)(2,1)}, bf16[4,3,256,128]{3,2,1,0:T(8,128)(2,1)S(1)}, u32[]{:S(2)}) copy-start(bf16[4,3,256,128]{3,2,1,0:T(8,128)(2,1)S(1)} %all-to-all-done.pieces) | copy-start | bytes 2359300
  43.8 14.6 %copy-start.9 = (bf16[2,128,896]{2,1,0:T(8,128)(2,1)}, bf16[2,128,896]{2,1,0:T(8,128)(2,1)S(1)}, u32[]{:S(2)}) copy-start(bf16[2,128,896]{2,1,0:T(8,128)(2,1)S(1)} %collective-permute-done.3.e11) | copy-start | bytes 1376260
  47.2 11.2 %copy-start.10 = (bf16[2,128,896]{2,1,0:T(8,128)(2,1)}, bf16[2,128,896]{2,1,0:T(8,128)(2,1)S(1)}, u32[]{:S(2)}) copy-start(bf16[2,128,896]{2,1,0:T(8,128)(2,1)S(1)} %collective-permute-done.4.e31) | copy-start | bytes 1376260
  47.3 11.1 %collective-permute-start.5 = (bf16[2,128,896]{2,1,0:T(8,128)(2,1)S(1)}, bf16[2,128,896]{2,1,0:T(8,128)(2,1)S(1)}, u32[]{:S(2)}, u32[]{:S(2)}) collective-permute-start(bf16[2,128,896]{2,1,0:T(8,128)(2,1)S(1)} %collective-permute-done.1.e30), channel_id=1, source_target_pairs={{0,2},{2,4},{4,6},{6,0},{1,3},{3,5},{5,7},{7,1},{8,10},{10,12},{12... | collective-permute-start | bytes 1376264 | tf_op jit(solution)/shard_map/ppermute | solution.py:398
  47.4 11.1 %collective-permute-start.6 = (bf16[2,128,896]{2,1,0:T(8,128)(2,1)S(1)}, bf16[2,128,896]{2,1,0:T(8,128)(2,1)S(1)}, u32[]{:S(2)}, u32[]{:S(2)}) collective-permute-start(bf16[2,128,896]{2,1,0:T(8,128)(2,1)S(1)} %collective-permute-done.3.e11), channel_id=1, source_target_pairs={{0,6},{2,0},{4,2},{6,4},{1,7},{3,1},{5,3},{7,5},{8,14},{10,8},{12,... | collective-permute-start | bytes 1376264 | tf_op jit(solution)/shard_map/ppermute | solution.py:399
  58.4 0.8 copy-start.13
  58.4 0.9 copy-start.14
  71.3 12.9 %copy-start.12 = (bf16[2,128,896]{2,1,0:T(8,128)(2,1)S(1)}, bf16[2,128,896]{2,1,0:T(8,128)(2,1)}, u32[]{:S(2)}) copy-start(bf16[2,128,896]{2,1,0:T(8,128)(2,1)} %get-tuple-element.79) | copy-start | bytes 1376260
  71.3 11.7 %collective-permute-start.7 = (bf16[2,128,896]{2,1,0:T(8,128)(2,1)}, bf16[2,128,896]{2,1,0:T(8,128)(2,1)S(1)}, u32[]{:S(2)}, u32[]{:S(2)}) collective-permute-start(bf16[2,128,896]{2,1,0:T(8,128)(2,1)} %get-tuple-element.71), channel_id=1, source_target_pairs={{0,6},{2,0},{4,2},{6,4},{1,7},{3,1},{5,3},{7,5},{8,14},{10,8},{12,... | collective-permute-start | bytes 1376264 | tf_op jit(solution)/shard_map/ppermute | solution.py:453
  74.2 9.9 %collective-permute-start.8 = (bf16[2,128,896]{2,1,0:T(8,128)(2,1)}, bf16[2,128,896]{2,1,0:T(8,128)(2,1)S(1)}, u32[]{:S(2)}, u32[]{:S(2)}) collective-permute-start(bf16[2,128,896]{2,1,0:T(8,128)(2,1)} %get-tuple-element.72), channel_id=1, source_target_pairs={{0,2},{2,4},{4,6},{6,0},{1,3},{3,5},{5,7},{7,1},{8,10},{10,12},{12... | collective-permute-start | bytes 1376264 | tf_op jit(solution)/shard_map/ppermute | solution.py:454
  74.2 12.2 %copy-start.16 = (bf16[2,128,896]{2,1,0:T(8,128)(2,1)S(1)}, bf16[2,128,896]{2,1,0:T(8,128)(2,1)}, u32[]{:S(2)}) copy-start(bf16[2,128,896]{2,1,0:T(8,128)(2,1)} %get-tuple-element.81) | copy-start | bytes 1376260
  74.2 12.2 %copy-start.11 = (bf16[2,128,896]{2,1,0:T(8,128)(2,1)S(1)}, bf16[2,128,896]{2,1,0:T(8,128)(2,1)}, u32[]{:S(2)}) copy-start(bf16[2,128,896]{2,1,0:T(8,128)(2,1)} %get-tuple-element.82) | copy-start | bytes 1376260
  83.0 15.8 %copy-start.5 = (bf16[2,128,896]{2,1,0:T(8,128)(2,1)S(1)}, bf16[2,128,896]{2,1,0:T(8,128)(2,1)}, u32[]{:S(2)}) copy-start(bf16[2,128,896]{2,1,0:T(8,128)(2,1)} %get-tuple-element.87) | copy-start | bytes 1376260
  84.3 11.2 %collective-permute-start.9 = (bf16[2,128,896]{2,1,0:T(8,128)(2,1)S(1)}, bf16[2,128,896]{2,1,0:T(8,128)(2,1)S(1)}, u32[]{:S(2)}, u32[]{:S(2)}) collective-permute-start(bf16[2,128,896]{2,1,0:T(8,128)(2,1)S(1)} %add_convert_fusion.2), channel_id=1, source_target_pairs={{0,6},{2,0},{4,2},{6,4},{1,7},{3,1},{5,3},{7,5},{8,14},{10,8},{12,... | collective-permute-start | bytes 1376264 | tf_op jit(solution)/shard_map/ppermute | solution.py:469
  86.5 12.4 %collective-permute-start.10 = (bf16[2,128,896]{2,1,0:T(8,128)(2,1)S(1)}, bf16[2,128,896]{2,1,0:T(8,128)(2,1)S(1)}, u32[]{:S(2)}, u32[]{:S(2)}) collective-permute-start(bf16[2,128,896]{2,1,0:T(8,128)(2,1)S(1)} %copy-done.16), channel_id=1, source_target_pairs={{0,2},{2,4},{4,6},{6,0},{1,3},{3,5},{5,7},{7,1},{8,10},{10,12},{12... | collective-permute-start | bytes 1376264 | tf_op jit(solution)/shard_map/ppermute | solution.py:470
  86.5 15.3 %copy-start.15 = (bf16[2,128,896]{2,1,0:T(8,128)(2,1)S(1)}, bf16[2,128,896]{2,1,0:T(8,128)(2,1)}, u32[]{:S(2)}) copy-start(bf16[2,128,896]{2,1,0:T(8,128)(2,1)} %get-tuple-element.86) | copy-start | bytes 1376260
  86.5 18.6 %copy-start.1 = (bf16[4,256,128]{2,1,0:T(8,128)(2,1)S(1)}, bf16[4,256,128]{2,1,0:T(8,128)(2,1)}, u32[]{:S(2)}) copy-start(bf16[4,256,128]{2,1,0:T(8,128)(2,1)} %shard_map.154) | copy-start | bytes 786436
  99.0 18.7 %collective-permute-start.13 = (bf16[2,128,896]{2,1,0:T(8,128)(2,1)S(1)}, bf16[2,128,896]{2,1,0:T(8,128)(2,1)S(1)}, u32[]{:S(2)}, u32[]{:S(2)}) collective-permute-start(bf16[2,128,896]{2,1,0:T(8,128)(2,1)S(1)} %add_convert_fusion), channel_id=1, source_target_pairs={{0,1},{1,0},{2,3},{3,2},{4,5},{5,4},{6,7},{7,6},{8,9},{9,8},{10,11... | collective-permute-start | bytes 1376264 | tf_op jit(solution)/shard_map/ppermute | solution.py:474
  101.8 15.9 %collective-permute-start.11 = (bf16[2,128,896]{2,1,0:T(8,128)(2,1)S(1)}, bf16[2,128,896]{2,1,0:T(8,128)(2,1)S(1)}, u32[]{:S(2)}, u32[]{:S(2)}) collective-permute-start(bf16[2,128,896]{2,1,0:T(8,128)(2,1)S(1)} %add_convert_fusion.1), channel_id=1, source_target_pairs={{0,2},{2,4},{4,6},{6,0},{1,3},{3,5},{5,7},{7,1},{8,10},{10,12},{12... | collective-permute-start | bytes 1376264 | tf_op jit(solution)/shard_map/ppermute | solution.py:475
  101.8 15.9 %collective-permute-start.12 = (bf16[2,128,896]{2,1,0:T(8,128)(2,1)S(1)}, bf16[2,128,896]{2,1,0:T(8,128)(2,1)S(1)}, u32[]{:S(2)}, u32[]{:S(2)}) collective-permute-start(bf16[2,128,896]{2,1,0:T(8,128)(2,1)S(1)} %copy-done.15), channel_id=1, source_target_pairs={{0,6},{2,0},{4,2},{6,4},{1,7},{3,1},{5,3},{7,5},{8,14},{10,8},{12,... | collective-permute-start | bytes 1376264 | tf_op jit(solution)/shard_map/ppermute | solution.py:476
  117.7 0.8 copy-start.2
  117.8 1.0 copy-start.3
  117.8 1.1 copy-start.4
Sparse Core Ops, SparseCore 0:
  47.4 25.6 all-gather.2

commit v5 on v4

--- a/solution.py
+++ b/solution.py
@@ -60,7 +60,8 @@
             out[h, i] = src[:, cols]
 
 
-def attend_kernel(pieces, kv, out, acc, top, total):
+def attend_kernel(pieces, kv, o0, o1, o2, o3, acc, top, total):
+    x = lax.axis_index("x")
     r = lax.axis_index("yl") * 2 + lax.axis_index("core")
     scale = LOG2E / math.sqrt(HSIZE)
     for xq in range(NX):
@@ -97,13 +98,19 @@
         for xk in range(xq):
             group(xk, False)
         group(xq, True)
-        out[xq] = (acc[...] / total[...]).astype(BF16)
-
-
-def mix_kernel(pieces, cross, out):
-    for h in range(NX):
-        cols = slice(h * HSIZE, (h + 1) * HSIZE)
-        out[:, cols] = (pieces[h].astype(F32) + cross[:, cols]).astype(BF16)
+        result = (acc[...] / total[...]).astype(BF16)
+        for d, out in enumerate((o0, o1, o2, o3)):
+
+            @pl.when(lax.rem(xq + d, NX) == x)
+            def _():
+                out[...] = result
+
+
+def mix_kernel(s0, s1, s2, s3, cross, out):
+    x = lax.axis_index("x")
+    for d, piece in enumerate((s0, s1, s2, s3)):
+        cols = pl.ds(pl.multiple_of(lax.rem(x + d, NX) * HSIZE, HSIZE), HSIZE)
+        out[:, cols] = (piece[...].astype(F32) + cross[:, cols]).astype(BF16)
 
 
 def head_rows(rows):
@@ -123,15 +130,13 @@
     nb, ctx, wq, wk, wv, wo, sems = scratch
     both = ((nb_h, nb), (wq_h, wq), (ctx_h, ctx), (wk_h, wk), (wv_h, wv), (wo_h, wo))
     copies = [pltpu.make_async_copy(a, b, sems.at[i]) for i, (a, b) in enumerate(both)]
-    for c in copies[:3]:
+    for c in copies:
         c.start()
     slots, rows, width = nb.shape
     each = width // EHEADS
     copies[0].wait()
     x = nb[...].reshape(slots * rows, width)
     copies[1].wait()
-    for c in copies[3:]:
-        c.start()
     eq = mm(x, wq[...]).astype(BF16)
     copies[2].wait()
     contexts = []
@@ -221,8 +226,8 @@
 def cross_kernel(ids, e00, e01, e10, e11, e20, e21, e30, e31, *rest):
     blocks = (e00, e01, e10, e11, e20, e21, e30, e31)
     given, cross, outs = rest[:7], rest[7], rest[8:16]
-    table, held, sent, ckv, dkv, zero, in_sem, out_sem, given_sem = rest[16:25]
-    kvw, qm_t, gm_t, q, g, kv_t = rest[25:]
+    table, held, sent, ckv, dkv, zero, in_sem, out_sem, given_sem, mine, mine_sem = rest[16:27]
+    kvw, qm_t, gm_t, q, g, kv_t = rest[27:]
     width = q.shape[1]
     here = (kvw.at[:, :width], kvw.at[:, width:], qm_t, gm_t, q, g, kv_t)
     loads = [
@@ -291,7 +296,7 @@
         pt = pb.T
         for h in range(heads):
             cols = slice(h * HSIZE, (h + 1) * HSIZE)
-            cross[c * CL : (c + 1) * CL, cols] = mm(
+            mine[c * CL : (c + 1) * CL, cols] = mm(
                 pt[h * CL : (h + 1) * CL], ckv[at, width + h * HSIZE : width + (h + 1) * HSIZE]
             )
 
@@ -316,9 +321,12 @@
         if c >= 1:
             back(c - 1)
         products(c, *soft)
+    leave = pltpu.make_async_copy(mine, cross, mine_sem)
+    leave.start()
     send(0, n_named - 2)
     back(spans - 1)
     send(n_named - 2, n_named)
+    leave.wait()
     for i, t in places:
         pltpu.make_async_copy(zero, outs[i].at[t], out_sem.at[2 * i + t]).wait()
 
@@ -411,7 +419,7 @@
         cross_kernel,
         out_shape=[struct((rows, width), F32)] + [struct((slots, nl, ew), BF16)] * 8,
         in_specs=[smem()] + [hbm()] * 15,
-        out_specs=[vmem()] + [hbm()] * 8,
+        out_specs=[hbm()] * 9,
         scratch_shapes=[
             pltpu.SMEM((16,), jnp.int32),
             pltpu.VMEM((n_named, nl, ew), BF16),
@@ -422,6 +430,8 @@
             pltpu.SemaphoreType.DMA((n_named,)),
             pltpu.SemaphoreType.DMA((16,)),
             pltpu.SemaphoreType.DMA((7,)),
+            pltpu.VMEM((rows, width), F32),
+            pltpu.SemaphoreType.DMA,
             pltpu.VMEM((ew, 2 * width), BF16),
         ]
         + [pltpu.VMEM((spans, width, width // HSIZE * CL), BF16)] * 2
@@ -452,28 +462,28 @@
 
     far1 = lax.ppermute(p21, "z", shift(NX, -1))
     far0 = lax.ppermute(p20, "z", shift(NX, 1))
-    kv, _ = after((kv, cross))
+    far1, far0, p11 = after((far1, far0, p11))
+    down1 = lax.ppermute(add(p31, far1), "z", shift(NX, -1))
+    up1 = lax.ppermute(p11, "z", shift(NX, 1))
+    near0 = add(p10, far0)
+    kv, _ = after((kv, far1))
     outs = call(
         attend_kernel,
-        out_shape=struct((NX, rows, HSIZE), BF16),
+        out_shape=[struct((rows, HSIZE), BF16)] * NX,
         in_specs=[vmem()] * 2,
-        out_specs=vmem(),
+        out_specs=[vmem()] * NX,
         scratch_shapes=[
             pltpu.VMEM((rows, HSIZE), F32),
             pltpu.VMEM((rows, 1), F32),
             pltpu.VMEM((rows, 1), F32),
         ],
     )(pieces, kv)
-    far1, far0, p11, outs = after((far1, far0, p11, outs))
-    selfs = lax.all_to_all(outs, "x", 0, 0)
-    down1 = lax.ppermute(add(p31, far1), "z", shift(NX, -1))
-    up1 = lax.ppermute(p11, "z", shift(NX, 1))
-    near0 = add(p10, far0)
-    down1, up1, near0, p30 = after((down1, up1, near0, p30))
+    down1, up1, near0, p30, *outs = after((down1, up1, near0, p30, *outs))
     theirs = (p01.astype(F32) + up1.astype(F32) + down1.astype(F32)).astype(BF16)
     other = lax.ppermute(theirs, "yh", shift(2, 1))
     up0 = lax.ppermute(near0, "z", shift(NX, 1))
     down0 = lax.ppermute(p30, "z", shift(NX, -1))
+    selfs = [outs[0]] + [lax.ppermute(outs[d], "x", shift(NX, -d)) for d in range(1, NX)]
 
     grad = call(
         pullback_kernel,
@@ -494,9 +504,9 @@
     mixed = call(
         mix_kernel,
         out_shape=struct((rows, width), BF16),
-        in_specs=[vmem()] * 2,
+        in_specs=[vmem()] * 5,
         out_specs=vmem(),
-    )(selfs, cross)
+    )(*selfs, cross)
     return mixed, grad
 
 

time: 132 us -> 128 us (0.970)
  blocking collectives: 10.8 us -> 0 us
  starting transfers between devices: 29.1 us -> 32.2 us
  waiting for transfers between devices: 28.1 us -> 30.6 us
    all_to_all x1 -> x0, blocking collectives: 10.8 us -> none  [local(): selfs = lax.all_to_all(outs, 'x', 0, 0)]
    ppermute x1, waiting for transfers between devices: 8.8 us -> 0.01 us  [local(): down1 = lax.ppermute(add(p31, far1), 'z', shift(NX, -1))]
    ppermute x1, waiting for transfers between devices: 0.01 us -> 6.46 us  [local(): far1 = lax.ppermute(p21, 'z', shift(NX, -1))]
    ppermute x0 -> x3, waiting for transfers between devices: none -> 5.85 us  [local(): lax.ppermute(outs[d], 'x', shift(NX, -d))]
    ppermute x0 -> x3, starting transfers between devices: none -> 4.6 us  [local(): lax.ppermute(outs[d], 'x', shift(NX, -d))]
    ppermute x1, waiting for transfers between devices: 3.41 us -> 0.01 us  [local(): up1 = lax.ppermute(p11, 'z', shift(NX, 1))]
    ppermute x1, waiting for transfers between devices: 1.1 us -> 3.44 us  [local(): far0 = lax.ppermute(p20, 'z', shift(NX, 1))]
    ppermute x1, starting transfers between devices: 2.21 us -> 0.22 us  [local(): down1 = lax.ppermute(add(p31, far1), 'z', shift(NX, -1))]
  transfers between devices with their start and end apart: 16 -> 19, of which waited for: 8 -> 10; matrix products, arithmetic and copies ran while one was open for 1% -> 2% of each run, Pallas kernels for 25% -> 26%
where the time goes in v5:
time: 128 us; the launch traced here: 127 us
  Pallas kernels  45.3 us (35%)
  starting transfers between devices  32.2 us (25%)
  waiting for transfers between devices  30.6 us (24%)
  between operations  14.2 us (11%)
  local copies, waits for them, and re-layouts  3.67 us (3%)
  other arithmetic  1.41 us (1%)
    pallas_call x1, Pallas kernels, local(): call(cross_kernel, out_shape=[struct((rows, width), F32)] + [struct((slot...  11.2 us
    pallas_call x1, Pallas kernels, local(): call(attend_kernel, out_shape=[struct((rows, HSIZE), BF16)] * NX, in_spec...  9.69 us
    pallas_call x1, Pallas kernels, local(): call(encode_kernel, out_shape=[struct((slots, nl, ew), BF16), struct((slo...  6.54 us
    ppermute x1, waiting for transfers between devices, local(): far1 = lax.ppermute(p21, 'z', shift(NX, -1))  6.46 us
    ppermute x3, waiting for transfers between devices, local(): lax.ppermute(outs[d], 'x', shift(NX, -d))  5.85 us
    pallas_call x1, Pallas kernels, local(): call(pullback_kernel, out_shape=struct((slots, nl, ew), F32), in_specs=[h...  5.59 us
    pallas_call x1, Pallas kernels, local(): call(turn_kernel, out_shape=[struct((2 * width, ew), BF16)] + [struct((ew...  5.23 us
    ppermute x1, waiting for transfers between devices, local(): e20 = lax.ppermute(e30, 'z', shift(NX, 1))  4.87 us
  transfers between devices with their start and end apart: 19, of which 10 were waited for; matrix products, arithmetic and copies ran while one was open for 2% of the time, Pallas kernels for 26%

profile of v5, /device:TPU:0, one launch (start us, length us, event | category | flops | bytes accessed | tf_op | source)
XLA Modules:
  0.0 127.5 jit_solution(8826340047557996910)
XLA Ops:
  7.2 6.5 %shard_map.149 = (bf16[2,128,896]{2,1,0:T(8,128)(2,1)}, f32[2,256,128]{2,1,0:T(8,128)}, bf16[2,64,896]{2,1,0:T(8,128)(2,1)}, bf16[2,64,896]{2,1,0:T(8,128)(2,1)}) custom-call(s32[2,4]{1,0:T(2,128)} %bitcast.3, bf16[2,128,896]{2,1,0:T(8,128)(2,1)} %nb_h.1, bf16[256,896]{1,0:T(8,128)(2,1)} %ctx_h.1, bf16[896,896]{1,0:T(8,128)(2,1)} %wq, ...), custom_call_target="tpu_custom_call" | custom-call | tf_op jit(solution)/shard_map/pallas_call | solution.py:363
  13.7 3.4 %collective-permute-start = (bf16[2,128,896]{2,1,0:T(8,128)(2,1)}, bf16[2,128,896]{2,1,0:T(8,128)(2,1)S(1)}, u32[]{:S(2)}, u32[]{:S(2)}) collective-permute-start(bf16[2,128,896]{2,1,0:T(8,128)(2,1)} %get-tuple-element.55.e00), channel_id=1, source_target_pairs={{0,1},{1,0},{2,3},{3,2},{4,5},{5,4},{6,7},{7,6},{8,9},{9,8},{10,11... | collective-permute-start | bytes 1376264 | tf_op jit(solution)/shard_map/ppermute | solution.py:378
  17.1 1.9 %collective-permute-start.1 = (bf16[2,128,896]{2,1,0:T(8,128)(2,1)}, bf16[2,128,896]{2,1,0:T(8,128)(2,1)S(1)}, u32[]{:S(2)}, u32[]{:S(2)}) collective-permute-start(bf16[2,128,896]{2,1,0:T(8,128)(2,1)} %get-tuple-element.55.e00), channel_id=1, source_target_pairs={{0,2},{2,4},{4,6},{6,0},{1,3},{3,5},{5,7},{7,1},{8,10},{10,12},{12... | collective-permute-start | bytes 1376264 | tf_op jit(solution)/shard_map/ppermute | solution.py:379
  19.0 2.1 %collective-permute-start.2 = (bf16[2,128,896]{2,1,0:T(8,128)(2,1)}, bf16[2,128,896]{2,1,0:T(8,128)(2,1)S(1)}, u32[]{:S(2)}, u32[]{:S(2)}) collective-permute-start(bf16[2,128,896]{2,1,0:T(8,128)(2,1)} %get-tuple-element.55.e00), channel_id=1, source_target_pairs={{0,6},{2,0},{4,2},{6,4},{1,7},{3,1},{5,3},{7,5},{8,14},{10,8},{12,... | collective-permute-start | bytes 1376264 | tf_op jit(solution)/shard_map/ppermute | solution.py:380
  21.1 2.1 %shard_map.150 = bf16[4,3,256,128]{3,2,1,0:T(8,128)(2,1)} custom-call(bf16[256,512]{1,0:T(8,128)(2,1)} %q_ref, bf16[256,512]{1,0:T(8,128)(2,1)} %k_ref, bf16[256,512]{1,0:T(8,128)(2,1)} %v_ref), custom_call_target="tpu_custom_call" | custom-call | tf_op jit(solution)/shard_map/pallas_call | solution.py:383
  23.2 4.3 %all-to-all-start = ((bf16[4,3,256,128]{3,2,1,0:T(8,128)(2,1)}), bf16[4,3,256,128]{3,2,1,0:T(8,128)(2,1)S(1)}, u32[]{:S(2)}, u32[]{:S(2)}) async-start(bf16[4,3,256,128]{3,2,1,0:T(8,128)(2,1)} %shard_map.150), calls=%async_computation | async-start | bytes 1572864 | tf_op jit(solution)/shard_map/all_to_all | solution.py:389
  27.5 0.0 all-gather.3.cloned.1.call-start
  27.5 0.3 collective-permute-done.e01
  27.8 3.8 %collective-permute-done.1.e30 = bf16[2,128,896]{2,1,0:T(8,128)(2,1)S(1)} collective-permute-done((bf16[2,128,896]{2,1,0:T(8,128)(2,1)}, bf16[2,128,896]{2,1,0:T(8,128)(2,1)S(1)}, u32[]{:S(2)}, u32[]{:S(2)}) %collective-permute-start.1) | collective-permute-done | bytes 458784 | tf_op jit(solution)/shard_map/ppermute | solution.py:379
  31.6 0.0 collective-permute-done.2.e10
  31.6 2.9 %collective-permute-start.3 = (bf16[2,128,896]{2,1,0:T(8,128)(2,1)S(1)}, bf16[2,128,896]{2,1,0:T(8,128)(2,1)S(1)}, u32[]{:S(2)}, u32[]{:S(2)}) collective-permute-start(bf16[2,128,896]{2,1,0:T(8,128)(2,1)S(1)} %collective-permute-done.e01), channel_id=1, source_target_pairs={{0,6},{2,0},{4,2},{6,4},{1,7},{3,1},{5,3},{7,5},{8,14},{10,8},{12,... | collective-permute-start | bytes 1376264 | tf_op jit(solution)/shard_map/ppermute | solution.py:393
  34.5 0.0 collective-permute-start.4
  34.5 5.2 %shard_map.151 = (bf16[1024,896]{1,0:T(8,128)(2,1)}, bf16[896,896]{1,0:T(8,128)(2,1)}, bf16[896,896]{1,0:T(8,128)(2,1)}) custom-call(bf16[896,512]{1,0:T(8,128)(2,1)} %rest_0_.1, bf16[896,512]{1,0:T(8,128)(2,1)} %rest_1_.1, bf16[896,896]{1,0:T(8,128)(2,1)} %wq, bf16[896,896]{1,0:T(8,128)(2,1)} %wo), custom_call_target="tpu_custom_call" | custom-call | tf_op jit(solution)/shard_map/pallas_call | solution.py:397
  39.8 0.0 copy-done.5
  39.8 0.0 all-to-all-done.pieces
  39.8 0.0 copy-start
  39.8 0.9 slice.4
  40.7 2.4 %collective-permute-done.3.e11 = bf16[2,128,896]{2,1,0:T(8,128)(2,1)S(1)} collective-permute-done((bf16[2,128,896]{2,1,0:T(8,128)(2,1)S(1)}, bf16[2,128,896]{2,1,0:T(8,128)(2,1)S(1)}, u32[]{:S(2)}, u32[]{:S(2)}) %collective-permute-start.3) | collective-permute-done | bytes 458784 | tf_op jit(solution)/shard_map/ppermute | solution.py:393
  43.1 3.4 %collective-permute-done.4.e31 = bf16[2,128,896]{2,1,0:T(8,128)(2,1)S(1)} collective-permute-done((bf16[2,128,896]{2,1,0:T(8,128)(2,1)S(1)}, bf16[2,128,896]{2,1,0:T(8,128)(2,1)S(1)}, u32[]{:S(2)}, u32[]{:S(2)}) %collective-permute-start.4) | collective-permute-done | bytes 458784 | tf_op jit(solution)/shard_map/ppermute | solution.py:394
  46.5 0.0 all-gather.3.cloned.1.call-update
  46.6 0.0 copy-done.6
  46.6 0.1 collective-permute-start.5
  46.6 3.2 %collective-permute-start.6 = (bf16[2,128,896]{2,1,0:T(8,128)(2,1)S(1)}, bf16[2,128,896]{2,1,0:T(8,128)(2,1)S(1)}, u32[]{:S(2)}, u32[]{:S(2)}) collective-permute-start(bf16[2,128,896]{2,1,0:T(8,128)(2,1)S(1)} %collective-permute-done.3.e11), channel_id=1, source_target_pairs={{0,6},{2,0},{4,2},{6,4},{1,7},{3,1},{5,3},{7,5},{8,14},{10,8},{12,... | collective-permute-start | bytes 1376264 | tf_op jit(solution)/shard_map/ppermute | solution.py:407
  49.9 3.0 %shard_map.152 = (bf16[4,512,256]{2,1,0:T(8,128)(2,1)}, bf16[4,512,256]{2,1,0:T(8,128)(2,1)}) custom-call(bf16[256,512]{1,0:T(8,128)(2,1)} %rest_4_.1, bf16[256,512]{1,0:T(8,128)(2,1)} %rest_5_.1), custom_call_target="tpu_custom_call" | custom-call | tf_op jit(solution)/shard_map/pallas_call | solution.py:411
  52.8 4.9 %collective-permute-done.5.e20 = bf16[2,128,896]{2,1,0:T(8,128)(2,1)S(1)} collective-permute-done((bf16[2,128,896]{2,1,0:T(8,128)(2,1)S(1)}, bf16[2,128,896]{2,1,0:T(8,128)(2,1)S(1)}, u32[]{:S(2)}, u32[]{:S(2)}) %collective-permute-start.5) | collective-permute-done | bytes 458784 | tf_op jit(solution)/shard_map/ppermute | solution.py:406
  57.7 0.0 collective-permute-done.6.e21
  57.7 0.0 copy-done.8
  57.7 0.8 copy-done.11
  58.5 0.2 copy-done.12
  58.7 11.2 %shard_map.153 = (f32[256,512]{1,0:T(8,128)}, bf16[2,128,896]{2,1,0:T(8,128)(2,1)}, bf16[2,128,896]{2,1,0:T(8,128)(2,1)}, bf16[2,128,896]{2,1,0:T(8,128)(2,1)}, ...) custom-call(s32[2,4]{1,0:T(2,128)} %bitcast.4, ...), custom_call_target="tpu_custom_call" | custom-call | tf_op jit(solution)/shard_map/pallas_call | solution.py:418
  69.9 2.8 %collective-permute-start.7 = (bf16[2,128,896]{2,1,0:T(8,128)(2,1)}, bf16[2,128,896]{2,1,0:T(8,128)(2,1)S(1)}, u32[]{:S(2)}, u32[]{:S(2)}) collective-permute-start(bf16[2,128,896]{2,1,0:T(8,128)(2,1)} %get-tuple-element.79), channel_id=1, source_target_pairs={{0,6},{2,0},{4,2},{6,4},{1,7},{3,1},{5,3},{7,5},{8,14},{10,8},{12,... | collective-permute-start | bytes 1376264 | tf_op jit(solution)/shard_map/ppermute | solution.py:463
  72.7 0.0 collective-permute-start.8
  72.7 6.5 %collective-permute-done.7 = bf16[2,128,896]{2,1,0:T(8,128)(2,1)S(1)} collective-permute-done((bf16[2,128,896]{2,1,0:T(8,128)(2,1)}, bf16[2,128,896]{2,1,0:T(8,128)(2,1)S(1)}, u32[]{:S(2)}, u32[]{:S(2)}) %collective-permute-start.7) | collective-permute-done | bytes 458784 | tf_op jit(solution)/shard_map/ppermute | solution.py:463
  79.2 3.4 %collective-permute-done.8 = bf16[2,128,896]{2,1,0:T(8,128)(2,1)S(1)} collective-permute-done((bf16[2,128,896]{2,1,0:T(8,128)(2,1)}, bf16[2,128,896]{2,1,0:T(8,128)(2,1)S(1)}, u32[]{:S(2)}, u32[]{:S(2)}) %collective-permute-start.8) | collective-permute-done | bytes 458784 | tf_op jit(solution)/shard_map/ppermute | solution.py:464
  82.6 1.1 add_convert_fusion.2
  83.8 0.2 collective-permute-start.9
  84.0 1.9 %collective-permute-start.10 = (bf16[2,128,896]{2,1,0:T(8,128)(2,1)}, bf16[2,128,896]{2,1,0:T(8,128)(2,1)S(1)}, u32[]{:S(2)}, u32[]{:S(2)}) collective-permute-start(bf16[2,128,896]{2,1,0:T(8,128)(2,1)} %get-tuple-element.83), channel_id=1, source_target_pairs={{0,2},{2,4},{4,6},{6,0},{1,3},{3,5},{5,7},{7,1},{8,10},{10,12},{12... | collective-permute-start | bytes 1376264 | tf_op jit(solution)/shard_map/ppermute | solution.py:467
  85.9 0.1 add_convert_fusion.1
  86.0 0.0 all-gather.3.cloned.1.call-done
  86.0 9.7 %shard_map.154 = (bf16[256,128]{1,0:T(8,128)(2,1)}, bf16[256,128]{1,0:T(8,128)(2,1)}, bf16[256,128]{1,0:T(8,128)(2,1)}, bf16[256,128]{1,0:T(8,128)(2,1)}) custom-call(bf16[4,3,256,128]{3,2,1,0:T(8,128)(2,1)} %copy-done, bf16[4,4,2,256,128]{4,3,2,1,0:T(8,128)(2,1)} %bitcast.2), custom_call_target="tpu_custom_call" | custom-call | tf_op jit(solution)/shard_map/pallas_call | solution.py:470
  95.7 0.0 copy-start.17
  95.7 0.0 collective-permute-done.9
  95.7 0.0 collective-permute-done.10
  95.8 0.2 add_convert_fusion
  95.9 1.6 %collective-permute-start.16 = (bf16[2,128,896]{2,1,0:T(8,128)(2,1)S(1)}, bf16[2,128,896]{2,1,0:T(8,128)(2,1)S(1)}, u32[]{:S(2)}, u32[]{:S(2)}) collective-permute-start(bf16[2,128,896]{2,1,0:T(8,128)(2,1)S(1)} %add_convert_fusion), channel_id=1, source_target_pairs={{0,1},{1,0},{2,3},{3,2},{4,5},{5,4},{6,7},{7,6},{8,9},{9,8},{10,11... | collective-permute-start | bytes 1376264 | tf_op jit(solution)/shard_map/ppermute | solution.py:483
  97.5 0.0 collective-permute-start.14
  97.5 3.2 %collective-permute-start.15 = (bf16[2,128,896]{2,1,0:T(8,128)(2,1)S(1)}, bf16[2,128,896]{2,1,0:T(8,128)(2,1)S(1)}, u32[]{:S(2)}, u32[]{:S(2)}) collective-permute-start(bf16[2,128,896]{2,1,0:T(8,128)(2,1)S(1)} %copy-done.16), channel_id=1, source_target_pairs={{0,6},{2,0},{4,2},{6,4},{1,7},{3,1},{5,3},{7,5},{8,14},{10,8},{12,... | collective-permute-start | bytes 1376264 | tf_op jit(solution)/shard_map/ppermute | solution.py:485
  100.8 2.7 %collective-permute-start.11 = (bf16[256,128]{1,0:T(8,128)(2,1)S(1)}, bf16[256,128]{1,0:T(8,128)(2,1)S(1)}, u32[]{:S(2)}, u32[]{:S(2)}) collective-permute-start(bf16[256,128]{1,0:T(8,128)(2,1)S(1)} %copy-done.19), channel_id=1, source_target_pairs={{0,96},{32,0},{64,32},{96,64},{1,97},{33,1},{65,33},{97,65},{2,98}... | collective-permute-start | bytes 196616 | tf_op jit(solution)/shard_map/ppermute | solution.py:486
  103.5 0.8 collective-permute-start.12
  104.3 1.1 collective-permute-done.11.s1
  105.4 0.0 copy-done.17
  105.4 1.1 collective-permute-start.13
  106.5 2.8 %collective-permute-done.12.s2 = bf16[256,128]{1,0:T(8,128)(2,1)S(1)} collective-permute-done((bf16[256,128]{1,0:T(8,128)(2,1)S(1)}, bf16[256,128]{1,0:T(8,128)(2,1)S(1)}, u32[]{:S(2)}, u32[]{:S(2)}) %collective-permute-start.12) | collective-permute-done | bytes 65568 | tf_op jit(solution)/shard_map/ppermute | solution.py:486
  109.3 1.9 %collective-permute-done.13.s3 = bf16[256,128]{1,0:T(8,128)(2,1)S(1)} collective-permute-done((bf16[256,128]{1,0:T(8,128)(2,1)S(1)}, bf16[256,128]{1,0:T(8,128)(2,1)S(1)}, u32[]{:S(2)}, u32[]{:S(2)}) %collective-permute-start.13) | collective-permute-done | bytes 65568 | tf_op jit(solution)/shard_map/ppermute | solution.py:486
  111.2 0.6 copy-done.15
  111.9 2.0 %shard_map.155 = bf16[256,512]{1,0:T(8,128)(2,1)} custom-call(bf16[256,128]{1,0:T(8,128)(2,1)} %get-tuple-element.93.s0, bf16[256,128]{1,0:T(8,128)(2,1)} %copy-done.13, bf16[256,128]{1,0:T(8,128)(2,1)} %copy-done.14, bf16[256,128]{1,0:T(8,128)(2,1)} %copy-done.15, f32[256,512]{1,0:T(8,128)} %get-tuple-element.97.cross), custom_call_target="tpu_custom_call" | custom-call | tf_op jit(solution)/shard_map/pallas_call | solution.py:504
  113.9 0.0 collective-permute-done.16.refs_3_
  113.9 0.0 collective-permute-done.14.refs_1_
  113.9 0.0 copy-start.2
  113.9 0.0 collective-permute-done.15.refs_2_
  113.9 0.8 copy-done.1
  114.7 0.1 copy-done.2
  114.8 0.2 copy-done.3
  115.0 5.6 %shard_map.156 = f32[2,128,896]{2,1,0:T(8,128)} custom-call(bf16[2,128,896]{2,1,0:T(8,128)(2,1)} %get-tuple-element.98.refs_0_, bf16[2,128,896]{2,1,0:T(8,128)(2,1)} %copy-done.2, bf16[2,128,896]{2,1,0:T(8,128)(2,1)} %copy-done.3, bf16[2,128,896]{2,1,0:T(8,128)(2,1)} %copy-done.1, bf16[896,896]{1,0:T(8,128)(2,1)} %get-tuple-element.104.refs_4_, ...), custom_call_target="tpu_custom_call" | custom-call | tf_op jit(solution)/shard_map/pallas_call | solution.py:488
  (27 shorter events, 0.0 us)
Async XLA Ops:
  13.7 14.1 %collective-permute-start = (bf16[2,128,896]{2,1,0:T(8,128)(2,1)}, bf16[2,128,896]{2,1,0:T(8,128)(2,1)S(1)}, u32[]{:S(2)}, u32[]{:S(2)}) collective-permute-start(bf16[2,128,896]{2,1,0:T(8,128)(2,1)} %get-tuple-element.55.e00), channel_id=1, source_target_pairs={{0,1},{1,0},{2,3},{3,2},{4,5},{5,4},{6,7},{7,6},{8,9},{9,8},{10,11... | collective-permute-start | bytes 1376264 | tf_op jit(solution)/shard_map/ppermute | solution.py:378
  17.1 14.5 %collective-permute-start.1 = (bf16[2,128,896]{2,1,0:T(8,128)(2,1)}, bf16[2,128,896]{2,1,0:T(8,128)(2,1)S(1)}, u32[]{:S(2)}, u32[]{:S(2)}) collective-permute-start(bf16[2,128,896]{2,1,0:T(8,128)(2,1)} %get-tuple-element.55.e00), channel_id=1, source_target_pairs={{0,2},{2,4},{4,6},{6,0},{1,3},{3,5},{5,7},{7,1},{8,10},{10,12},{12... | collective-permute-start | bytes 1376264 | tf_op jit(solution)/shard_map/ppermute | solution.py:379
  19.0 12.6 %collective-permute-start.2 = (bf16[2,128,896]{2,1,0:T(8,128)(2,1)}, bf16[2,128,896]{2,1,0:T(8,128)(2,1)S(1)}, u32[]{:S(2)}, u32[]{:S(2)}) collective-permute-start(bf16[2,128,896]{2,1,0:T(8,128)(2,1)} %get-tuple-element.55.e00), channel_id=1, source_target_pairs={{0,6},{2,0},{4,2},{6,4},{1,7},{3,1},{5,3},{7,5},{8,14},{10,8},{12,... | collective-permute-start | bytes 1376264 | tf_op jit(solution)/shard_map/ppermute | solution.py:380
  23.2 16.5 %all-to-all-start = ((bf16[4,3,256,128]{3,2,1,0:T(8,128)(2,1)}), bf16[4,3,256,128]{3,2,1,0:T(8,128)(2,1)S(1)}, u32[]{:S(2)}, u32[]{:S(2)}) async-start(bf16[4,3,256,128]{3,2,1,0:T(8,128)(2,1)} %shard_map.150), calls=%async_computation | async-start | bytes 1572864 | tf_op jit(solution)/shard_map/all_to_all | solution.py:389
  27.5 58.5 %all-gather.3.cloned.1.call-start = ((), (), s32[]{:S(2)}) async-start(), calls=%async_computation.1 | async-start | bytes 2621440 | tf_op jit(solution)/shard_map/all_gather | solution.py:408
  27.8 12.0 %copy-start.5 = (bf16[2,128,896]{2,1,0:T(8,128)(2,1)}, bf16[2,128,896]{2,1,0:T(8,128)(2,1)S(1)}, u32[]{:S(2)}) copy-start(bf16[2,128,896]{2,1,0:T(8,128)(2,1)S(1)} %collective-permute-done.e01) | copy-start | bytes 1376260
  31.6 15.0 %copy-start.6 = (bf16[2,128,896]{2,1,0:T(8,128)(2,1)}, bf16[2,128,896]{2,1,0:T(8,128)(2,1)S(1)}, u32[]{:S(2)}) copy-start(bf16[2,128,896]{2,1,0:T(8,128)(2,1)S(1)} %collective-permute-done.1.e30) | copy-start | bytes 1376260
  31.6 8.2 %copy-start.7 = (bf16[2,128,896]{2,1,0:T(8,128)(2,1)}, bf16[2,128,896]{2,1,0:T(8,128)(2,1)S(1)}, u32[]{:S(2)}) copy-start(bf16[2,128,896]{2,1,0:T(8,128)(2,1)S(1)} %collective-permute-done.2.e10) | copy-start | bytes 1376260
  31.6 11.5 %collective-permute-start.3 = (bf16[2,128,896]{2,1,0:T(8,128)(2,1)S(1)}, bf16[2,128,896]{2,1,0:T(8,128)(2,1)S(1)}, u32[]{:S(2)}, u32[]{:S(2)}) collective-permute-start(bf16[2,128,896]{2,1,0:T(8,128)(2,1)S(1)} %collective-permute-done.e01), channel_id=1, source_target_pairs={{0,6},{2,0},{4,2},{6,4},{1,7},{3,1},{5,3},{7,5},{8,14},{10,8},{12,... | collective-permute-start | bytes 1376264 | tf_op jit(solution)/shard_map/ppermute | solution.py:393
  34.5 12.0 %collective-permute-start.4 = (bf16[2,128,896]{2,1,0:T(8,128)(2,1)S(1)}, bf16[2,128,896]{2,1,0:T(8,128)(2,1)S(1)}, u32[]{:S(2)}, u32[]{:S(2)}) collective-permute-start(bf16[2,128,896]{2,1,0:T(8,128)(2,1)S(1)} %collective-permute-done.e01), channel_id=1, source_target_pairs={{0,2},{2,4},{4,6},{6,0},{1,3},{3,5},{5,7},{7,1},{8,10},{10,12},{12... | collective-permute-start | bytes 1376264 | tf_op jit(solution)/shard_map/ppermute | solution.py:394
  39.8 30.2 %copy-start = (bf16[4,3,256,128]{3,2,1,0:T(8,128)(2,1)}, bf16[4,3,256,128]{3,2,1,0:T(8,128)(2,1)S(1)}, u32[]{:S(2)}) copy-start(bf16[4,3,256,128]{3,2,1,0:T(8,128)(2,1)S(1)} %all-to-all-done.pieces) | copy-start | bytes 2359300
  43.1 14.6 %copy-start.8 = (bf16[2,128,896]{2,1,0:T(8,128)(2,1)}, bf16[2,128,896]{2,1,0:T(8,128)(2,1)S(1)}, u32[]{:S(2)}) copy-start(bf16[2,128,896]{2,1,0:T(8,128)(2,1)S(1)} %collective-permute-done.3.e11) | copy-start | bytes 1376260
  46.5 11.2 %copy-start.9 = (bf16[2,128,896]{2,1,0:T(8,128)(2,1)}, bf16[2,128,896]{2,1,0:T(8,128)(2,1)S(1)}, u32[]{:S(2)}) copy-start(bf16[2,128,896]{2,1,0:T(8,128)(2,1)S(1)} %collective-permute-done.4.e31) | copy-start | bytes 1376260
  46.6 11.2 %collective-permute-start.5 = (bf16[2,128,896]{2,1,0:T(8,128)(2,1)S(1)}, bf16[2,128,896]{2,1,0:T(8,128)(2,1)S(1)}, u32[]{:S(2)}, u32[]{:S(2)}) collective-permute-start(bf16[2,128,896]{2,1,0:T(8,128)(2,1)S(1)} %collective-permute-done.1.e30), channel_id=1, source_target_pairs={{0,2},{2,4},{4,6},{6,0},{1,3},{3,5},{5,7},{7,1},{8,10},{10,12},{12... | collective-permute-start | bytes 1376264 | tf_op jit(solution)/shard_map/ppermute | solution.py:406
  46.6 11.1 %collective-permute-start.6 = (bf16[2,128,896]{2,1,0:T(8,128)(2,1)S(1)}, bf16[2,128,896]{2,1,0:T(8,128)(2,1)S(1)}, u32[]{:S(2)}, u32[]{:S(2)}) collective-permute-start(bf16[2,128,896]{2,1,0:T(8,128)(2,1)S(1)} %collective-permute-done.3.e11), channel_id=1, source_target_pairs={{0,6},{2,0},{4,2},{6,4},{1,7},{3,1},{5,3},{7,5},{8,14},{10,8},{12,... | collective-permute-start | bytes 1376264 | tf_op jit(solution)/shard_map/ppermute | solution.py:407
  57.7 0.8 copy-start.11
  57.7 1.0 copy-start.12
  69.9 15.9 %copy-start.10 = (bf16[2,128,896]{2,1,0:T(8,128)(2,1)S(1)}, bf16[2,128,896]{2,1,0:T(8,128)(2,1)}, u32[]{:S(2)}) copy-start(bf16[2,128,896]{2,1,0:T(8,128)(2,1)} %get-tuple-element.84) | copy-start | bytes 1376260
  69.9 9.2 %collective-permute-start.7 = (bf16[2,128,896]{2,1,0:T(8,128)(2,1)}, bf16[2,128,896]{2,1,0:T(8,128)(2,1)S(1)}, u32[]{:S(2)}, u32[]{:S(2)}) collective-permute-start(bf16[2,128,896]{2,1,0:T(8,128)(2,1)} %get-tuple-element.79), channel_id=1, source_target_pairs={{0,6},{2,0},{4,2},{6,4},{1,7},{3,1},{5,3},{7,5},{8,14},{10,8},{12,... | collective-permute-start | bytes 1376264 | tf_op jit(solution)/shard_map/ppermute | solution.py:463
  72.7 9.9 %collective-permute-start.8 = (bf16[2,128,896]{2,1,0:T(8,128)(2,1)}, bf16[2,128,896]{2,1,0:T(8,128)(2,1)S(1)}, u32[]{:S(2)}, u32[]{:S(2)}) collective-permute-start(bf16[2,128,896]{2,1,0:T(8,128)(2,1)} %get-tuple-element.80), channel_id=1, source_target_pairs={{0,2},{2,4},{4,6},{6,0},{1,3},{3,5},{5,7},{7,1},{8,10},{10,12},{12... | collective-permute-start | bytes 1376264 | tf_op jit(solution)/shard_map/ppermute | solution.py:464
  83.8 12.0 %collective-permute-start.9 = (bf16[2,128,896]{2,1,0:T(8,128)(2,1)S(1)}, bf16[2,128,896]{2,1,0:T(8,128)(2,1)S(1)}, u32[]{:S(2)}, u32[]{:S(2)}) collective-permute-start(bf16[2,128,896]{2,1,0:T(8,128)(2,1)S(1)} %add_convert_fusion.2), channel_id=1, source_target_pairs={{0,6},{2,0},{4,2},{6,4},{1,7},{3,1},{5,3},{7,5},{8,14},{10,8},{12,... | collective-permute-start | bytes 1376264 | tf_op jit(solution)/shard_map/ppermute | solution.py:466
  84.0 11.8 %collective-permute-start.10 = (bf16[2,128,896]{2,1,0:T(8,128)(2,1)}, bf16[2,128,896]{2,1,0:T(8,128)(2,1)S(1)}, u32[]{:S(2)}, u32[]{:S(2)}) collective-permute-start(bf16[2,128,896]{2,1,0:T(8,128)(2,1)} %get-tuple-element.83), channel_id=1, source_target_pairs={{0,2},{2,4},{4,6},{6,0},{1,3},{3,5},{5,7},{7,1},{8,10},{10,12},{12... | collective-permute-start | bytes 1376264 | tf_op jit(solution)/shard_map/ppermute | solution.py:467
  86.0 9.8 %copy-start.4 = (bf16[2,128,896]{2,1,0:T(8,128)(2,1)S(1)}, bf16[2,128,896]{2,1,0:T(8,128)(2,1)}, u32[]{:S(2)}) copy-start(bf16[2,128,896]{2,1,0:T(8,128)(2,1)} %get-tuple-element.101) | copy-start | bytes 1376260
  95.7 1.8 %copy-start.16 = (bf16[2,128,896]{2,1,0:T(8,128)(2,1)S(1)}, bf16[2,128,896]{2,1,0:T(8,128)(2,1)}, u32[]{:S(2)}) copy-start(bf16[2,128,896]{2,1,0:T(8,128)(2,1)} %get-tuple-element.100) | copy-start | bytes 1376260
  95.7 5.1 %copy-start.19 = (bf16[256,128]{1,0:T(8,128)(2,1)S(1)}, bf16[256,128]{1,0:T(8,128)(2,1)}, u32[]{:S(2)}) copy-start(bf16[256,128]{1,0:T(8,128)(2,1)} %get-tuple-element.94) | copy-start | bytes 196612
  95.7 7.8 %copy-start.18 = (bf16[256,128]{1,0:T(8,128)(2,1)S(1)}, bf16[256,128]{1,0:T(8,128)(2,1)}, u32[]{:S(2)}) copy-start(bf16[256,128]{1,0:T(8,128)(2,1)} %get-tuple-element.95) | copy-start | bytes 196612
  95.7 9.7 %copy-start.17 = (bf16[256,128]{1,0:T(8,128)(2,1)S(1)}, bf16[256,128]{1,0:T(8,128)(2,1)}, u32[]{:S(2)}) copy-start(bf16[256,128]{1,0:T(8,128)(2,1)} %get-tuple-element.96) | copy-start | bytes 196612
  95.9 17.9 %collective-permute-start.16 = (bf16[2,128,896]{2,1,0:T(8,128)(2,1)S(1)}, bf16[2,128,896]{2,1,0:T(8,128)(2,1)S(1)}, u32[]{:S(2)}, u32[]{:S(2)}) collective-permute-start(bf16[2,128,896]{2,1,0:T(8,128)(2,1)S(1)} %add_convert_fusion), channel_id=1, source_target_pairs={{0,1},{1,0},{2,3},{3,2},{4,5},{5,4},{6,7},{7,6},{8,9},{9,8},{10,11... | collective-permute-start | bytes 1376264 | tf_op jit(solution)/shard_map/ppermute | solution.py:483
  97.5 16.3 %collective-permute-start.14 = (bf16[2,128,896]{2,1,0:T(8,128)(2,1)S(1)}, bf16[2,128,896]{2,1,0:T(8,128)(2,1)S(1)}, u32[]{:S(2)}, u32[]{:S(2)}) collective-permute-start(bf16[2,128,896]{2,1,0:T(8,128)(2,1)S(1)} %add_convert_fusion.1), channel_id=1, source_target_pairs={{0,2},{2,4},{4,6},{6,0},{1,3},{3,5},{5,7},{7,1},{8,10},{10,12},{12... | collective-permute-start | bytes 1376264 | tf_op jit(solution)/shard_map/ppermute | solution.py:484
  97.5 16.3 %collective-permute-start.15 = (bf16[2,128,896]{2,1,0:T(8,128)(2,1)S(1)}, bf16[2,128,896]{2,1,0:T(8,128)(2,1)S(1)}, u32[]{:S(2)}, u32[]{:S(2)}) collective-permute-start(bf16[2,128,896]{2,1,0:T(8,128)(2,1)S(1)} %copy-done.16), channel_id=1, source_target_pairs={{0,6},{2,0},{4,2},{6,4},{1,7},{3,1},{5,3},{7,5},{8,14},{10,8},{12,... | collective-permute-start | bytes 1376264 | tf_op jit(solution)/shard_map/ppermute | solution.py:485
  100.8 4.6 %collective-permute-start.11 = (bf16[256,128]{1,0:T(8,128)(2,1)S(1)}, bf16[256,128]{1,0:T(8,128)(2,1)S(1)}, u32[]{:S(2)}, u32[]{:S(2)}) collective-permute-start(bf16[256,128]{1,0:T(8,128)(2,1)S(1)} %copy-done.19), channel_id=1, source_target_pairs={{0,96},{32,0},{64,32},{96,64},{1,97},{33,1},{65,33},{97,65},{2,98}... | collective-permute-start | bytes 196616 | tf_op jit(solution)/shard_map/ppermute | solution.py:486
  103.5 5.8 %collective-permute-start.12 = (bf16[256,128]{1,0:T(8,128)(2,1)S(1)}, bf16[256,128]{1,0:T(8,128)(2,1)S(1)}, u32[]{:S(2)}, u32[]{:S(2)}) collective-permute-start(bf16[256,128]{1,0:T(8,128)(2,1)S(1)} %copy-done.18), channel_id=1, source_target_pairs={{0,64},{32,96},{64,0},{96,32},{1,65},{33,97},{65,1},{97,33},{2,66}... | collective-permute-start | bytes 196616 | tf_op jit(solution)/shard_map/ppermute | solution.py:486
  105.4 5.8 %copy-start.13 = (bf16[256,128]{1,0:T(8,128)(2,1)}, bf16[256,128]{1,0:T(8,128)(2,1)S(1)}, u32[]{:S(2)}) copy-start(bf16[256,128]{1,0:T(8,128)(2,1)S(1)} %collective-permute-done.11.s1) | copy-start | bytes 196612
  105.4 5.8 %collective-permute-start.13 = (bf16[256,128]{1,0:T(8,128)(2,1)S(1)}, bf16[256,128]{1,0:T(8,128)(2,1)S(1)}, u32[]{:S(2)}, u32[]{:S(2)}) collective-permute-start(bf16[256,128]{1,0:T(8,128)(2,1)S(1)} %copy-done.17), channel_id=1, source_target_pairs={{0,32},{32,64},{64,96},{96,0},{1,33},{33,65},{65,97},{97,1},{2,34}... | collective-permute-start | bytes 196616 | tf_op jit(solution)/shard_map/ppermute | solution.py:486
  109.3 2.0 %copy-start.14 = (bf16[256,128]{1,0:T(8,128)(2,1)}, bf16[256,128]{1,0:T(8,128)(2,1)S(1)}, u32[]{:S(2)}) copy-start(bf16[256,128]{1,0:T(8,128)(2,1)S(1)} %collective-permute-done.12.s2) | copy-start | bytes 196612
  111.2 0.6 copy-start.15
  113.9 0.8 copy-start.1
  113.9 0.9 copy-start.2
  113.9 1.1 copy-start.3
Sparse Core Ops, SparseCore 0:
  46.7 25.6 all-gather.2

commit v6 on v5

--- a/solution.py
+++ b/solution.py
@@ -60,45 +60,49 @@
             out[h, i] = src[:, cols]
 
 
-def attend_kernel(pieces, kv, o0, o1, o2, o3, acc, top, total):
+def attend_kernel(pieces, kv_h, o0, o1, o2, o3, kv, acc, top, sems):
+    loads = [pltpu.make_async_copy(kv_h.at[:, c], kv.at[:, c], sems.at[c]) for c in range(NX)]
+    for c in loads:
+        c.start()
     x = lax.axis_index("x")
     r = lax.axis_index("yl") * 2 + lax.axis_index("core")
     scale = LOG2E / math.sqrt(HSIZE)
+    rows = pieces.shape[2]
+    ones = jnp.ones((rows, HSIZE), BF16)
     for xq in range(NX):
+        loads[xq].wait()
         q = pieces[xq, 0]
-        rows = q.shape[0]
-        acc[...] = jnp.zeros_like(acc)
-        top[...] = jnp.full_like(top, -1e30)
-        total[...] = jnp.zeros_like(total)
-
-        def group(xk, masked):
+
+        def group(xk):
             scores = [mm_nt(q, kv[i, xk, 0]) for i in range(4)]
-            if masked:
+            if xk == xq:
                 at = lax.broadcasted_iota(jnp.int32, (rows, rows), 1)
                 upto = lax.broadcasted_iota(jnp.int32, (rows, rows), 0)
                 scores = [
-                    jnp.where(at + i * rows <= upto + r * rows, s, -1e30)
+                    jnp.where(at + (i % 2 * 2 + i // 2) * rows <= upto + r * rows, s, -1e30)
                     for i, s in enumerate(scores)
                 ]
             best = jnp.maximum(
                 jnp.maximum(scores[0], scores[1]), jnp.maximum(scores[2], scores[3])
             )
-            old = top[...]
-            new = jnp.maximum(old, jnp.max(best, axis=-1, keepdims=True))
-            fade = jnp.exp2((old - new) * scale)
-            weights = [jnp.exp2((s - new) * scale) for s in scores]
-            added = (weights[0] + weights[1]) + (weights[2] + weights[3])
-            total[...] = total[...] * fade + jnp.sum(added, axis=-1, keepdims=True)
-            out = mm(weights[0].astype(BF16), kv[0, xk, 1])
-            for i in range(1, 4):
-                out = out + mm(weights[i].astype(BF16), kv[i, xk, 1])
-            acc[...] = acc[...] * fade + out
+            new = jnp.max(best, axis=-1, keepdims=True)
+            if xk > 0:
+                old = top[...]
+                new = jnp.maximum(old, new)
+            out = None
+            for i, s in enumerate(scores):
+                weights = jnp.exp2((s - new) * scale).astype(BF16)
+                term = mm(weights, jnp.concatenate([kv[i, xk, 1], ones], axis=1))
+                out = term if out is None else out + term
+            if xk > 0:
+                out = acc[...] * jnp.exp2((old - new) * scale) + out
+            acc[...] = out
             top[...] = new
 
-        for xk in range(xq):
-            group(xk, False)
-        group(xq, True)
-        result = (acc[...] / total[...]).astype(BF16)
+        for xk in range(xq + 1):
+            group(xk)
+        total = acc[...]
+        result = (total[:, :HSIZE] / total[:, HSIZE:]).astype(BF16)
         for d, out in enumerate((o0, o1, o2, o3)):
 
             @pl.when(lax.rem(xq + d, NX) == x)
@@ -387,11 +391,11 @@
         out_specs=vmem(),
     )(self_q, self_k, self_v)
     pieces = lax.all_to_all(packed, "x", 0, 0)
-    own_kv = pieces[:, 1:]
 
     e01, e30, e10, packed = after((e01, e30, e10, packed))
     e11 = lax.ppermute(e01, "z", shift(NX, -1))
     e31 = lax.ppermute(e01, "z", shift(NX, 1))
+
 
     weights = after((cross_k_weight, cross_v_weight, enc_q, enc_o, e01))[:4]
     turned = call(
@@ -401,11 +405,15 @@
         out_specs=[vmem()] * 3,
     )(*weights)
 
+    own_kv = pieces[:, 1:]
     e30, e11, e31, own_kv, *turned = after((e30, e11, e31, own_kv, *turned))
+    half_kv = lax.all_gather(own_kv, "yl", axis=0)
     kv_t, wq_t, wo_t = turned
     e20 = lax.ppermute(e30, "z", shift(NX, 1))
     e21 = lax.ppermute(e11, "z", shift(NX, -1))
-    kv = lax.all_gather(own_kv, ("yl", "core"), axis=0)
+
+    half_kv, _ = after((half_kv, e20))
+    kv = lax.all_gather(half_kv, "core", axis=0).reshape((4,) + own_kv.shape)
 
     queries, grads, _ = after((cross_q, mixed_grad, e11))
     qm_t, gm_t = call(
@@ -462,28 +470,29 @@
 
     far1 = lax.ppermute(p21, "z", shift(NX, -1))
     far0 = lax.ppermute(p20, "z", shift(NX, 1))
-    far1, far0, p11 = after((far1, far0, p11))
+    kv, _ = after((kv, cross))
+    outs = call(
+        attend_kernel,
+        out_shape=[struct((rows, HSIZE), BF16)] * NX,
+        in_specs=[vmem(), hbm()],
+        out_specs=[vmem()] * NX,
+        scratch_shapes=[
+            pltpu.VMEM(kv.shape, BF16),
+            pltpu.VMEM((rows, 2 * HSIZE), F32),
+            pltpu.VMEM((rows, 1), F32),
+            pltpu.SemaphoreType.DMA((NX,)),
+        ],
+    )(pieces, kv)
+    far1, far0, p11, *outs = after((far1, far0, p11, *outs))
+    selfs = [outs[0]] + [lax.ppermute(outs[d], "x", shift(NX, -d)) for d in range(1, NX)]
     down1 = lax.ppermute(add(p31, far1), "z", shift(NX, -1))
     up1 = lax.ppermute(p11, "z", shift(NX, 1))
     near0 = add(p10, far0)
-    kv, _ = after((kv, far1))
-    outs = call(
-        attend_kernel,
-        out_shape=[struct((rows, HSIZE), BF16)] * NX,
-        in_specs=[vmem()] * 2,
-        out_specs=[vmem()] * NX,
-        scratch_shapes=[
-            pltpu.VMEM((rows, HSIZE), F32),
-            pltpu.VMEM((rows, 1), F32),
-            pltpu.VMEM((rows, 1), F32),
-        ],
-    )(pieces, kv)
-    down1, up1, near0, p30, *outs = after((down1, up1, near0, p30, *outs))
+    down1, up1, near0, p30, *selfs = after((down1, up1, near0, p30, *selfs))
     theirs = (p01.astype(F32) + up1.astype(F32) + down1.astype(F32)).astype(BF16)
     other = lax.ppermute(theirs, "yh", shift(2, 1))
     up0 = lax.ppermute(near0, "z", shift(NX, 1))
     down0 = lax.ppermute(p30, "z", shift(NX, -1))
-    selfs = [outs[0]] + [lax.ppermute(outs[d], "x", shift(NX, -d)) for d in range(1, NX)]
 
     grad = call(
         pullback_kernel,

time: 128 us -> 148 us (1.16)
  waiting for transfers between devices: 30.6 us -> 51.8 us
  starting transfers between devices: 32.2 us -> 34.1 us
    all_gather x1 -> x2, waiting for transfers between devices: 0.02 us -> 9.51 us  [the longest x1 9.51 us: local(): half_kv = lax.all_gather(own_kv, 'yl', axis=0)]
    ppermute x1, waiting for transfers between devices: 0.01 us -> 6.84 us  [local(): e21 = lax.ppermute(e11, 'z', shift(NX, -1))]
    ppermute x1, waiting for transfers between devices: 4.87 us -> 11.1 us  [local(): e20 = lax.ppermute(e30, 'z', shift(NX, 1))]
    ppermute x1, waiting for transfers between devices: 6.46 us -> 0.27 us  [local(): far1 = lax.ppermute(p21, 'z', shift(NX, -1))]
    ppermute x1, waiting for transfers between devices: 0.01 us -> 3.22 us  [local(): other = lax.ppermute(theirs, 'yh', shift(2, 1))]
    ppermute x1, waiting for transfers between devices: 0.01 us -> 2.4 us  [local(): up0 = lax.ppermute(near0, 'z', shift(NX, 1))]
  transfers between devices with their start and end apart: 19 -> 20, of which waited for: 10 -> 15; matrix products, arithmetic and copies ran while one was open for 2% -> 1% of each run, Pallas kernels for 26% -> 22%
where the time goes in v6:
time: 148 us; the launch traced here: 147 us
  waiting for transfers between devices  51.8 us (35%)
  Pallas kernels  44.4 us (30%)
  starting transfers between devices  34.1 us (23%)
  between operations  14.2 us (10%)
  local copies, waits for them, and re-layouts  2.55 us (2%)
    pallas_call x1, Pallas kernels, local(): call(cross_kernel, out_shape=[struct((rows, width), F32)] + [struct((slot...  11.1 us
    ppermute x1, waiting for transfers between devices, local(): e20 = lax.ppermute(e30, 'z', shift(NX, 1))  11.1 us
    all_gather x1, waiting for transfers between devices, local(): half_kv = lax.all_gather(own_kv, 'yl', axis=0)  9.51 us
    pallas_call x1, Pallas kernels, local(): call(attend_kernel, out_shape=[struct((rows, HSIZE), BF16)] * NX, in_spec...  8.92 us
    ppermute x1, waiting for transfers between devices, local(): e21 = lax.ppermute(e11, 'z', shift(NX, -1))  6.84 us
    pallas_call x1, Pallas kernels, local(): call(encode_kernel, out_shape=[struct((slots, nl, ew), BF16), struct((slo...  6.54 us
    pallas_call x1, Pallas kernels, local(): call(pullback_kernel, out_shape=struct((slots, nl, ew), F32), in_specs=[h...  5.59 us
    pallas_call x1, Pallas kernels, local(): call(turn_kernel, out_shape=[struct((2 * width, ew), BF16)] + [struct((ew...  5.22 us
  transfers between devices with their start and end apart: 20, of which 15 were waited for; matrix products, arithmetic and copies ran while one was open for 1% of the time, Pallas kernels for 22%

profile of v6, /device:TPU:0, one launch (start us, length us, event | category | flops | bytes accessed | tf_op | source)
XLA Modules:
  0.0 147.4 jit_solution(10895371390190476758)
XLA Ops:
  7.2 6.5 %shard_map.149 = (bf16[2,128,896]{2,1,0:T(8,128)(2,1)}, f32[2,256,128]{2,1,0:T(8,128)}, bf16[2,64,896]{2,1,0:T(8,128)(2,1)}, bf16[2,64,896]{2,1,0:T(8,128)(2,1)}) custom-call(s32[2,4]{1,0:T(2,128)} %bitcast.3, bf16[2,128,896]{2,1,0:T(8,128)(2,1)} %nb_h.1, bf16[256,896]{1,0:T(8,128)(2,1)} %ctx_h.1, bf16[896,896]{1,0:T(8,128)(2,1)} %wq, ...), custom_call_target="tpu_custom_call" | custom-call | tf_op jit(solution)/shard_map/pallas_call | solution.py:367
  13.7 3.4 %collective-permute-start = (bf16[2,128,896]{2,1,0:T(8,128)(2,1)}, bf16[2,128,896]{2,1,0:T(8,128)(2,1)S(1)}, u32[]{:S(2)}, u32[]{:S(2)}) collective-permute-start(bf16[2,128,896]{2,1,0:T(8,128)(2,1)} %get-tuple-element.60.e00), channel_id=1, source_target_pairs={{0,1},{1,0},{2,3},{3,2},{4,5},{5,4},{6,7},{7,6},{8,9},{9,8},{10,11... | collective-permute-start | bytes 1376264 | tf_op jit(solution)/shard_map/ppermute | solution.py:382
  17.1 1.9 %collective-permute-start.1 = (bf16[2,128,896]{2,1,0:T(8,128)(2,1)}, bf16[2,128,896]{2,1,0:T(8,128)(2,1)S(1)}, u32[]{:S(2)}, u32[]{:S(2)}) collective-permute-start(bf16[2,128,896]{2,1,0:T(8,128)(2,1)} %get-tuple-element.60.e00), channel_id=1, source_target_pairs={{0,2},{2,4},{4,6},{6,0},{1,3},{3,5},{5,7},{7,1},{8,10},{10,12},{12... | collective-permute-start | bytes 1376264 | tf_op jit(solution)/shard_map/ppermute | solution.py:383
  19.0 2.1 %collective-permute-start.2 = (bf16[2,128,896]{2,1,0:T(8,128)(2,1)}, bf16[2,128,896]{2,1,0:T(8,128)(2,1)S(1)}, u32[]{:S(2)}, u32[]{:S(2)}) collective-permute-start(bf16[2,128,896]{2,1,0:T(8,128)(2,1)} %get-tuple-element.60.e00), channel_id=1, source_target_pairs={{0,6},{2,0},{4,2},{6,4},{1,7},{3,1},{5,3},{7,5},{8,14},{10,8},{12,... | collective-permute-start | bytes 1376264 | tf_op jit(solution)/shard_map/ppermute | solution.py:384
  21.1 2.1 %shard_map.150 = bf16[4,3,256,128]{3,2,1,0:T(8,128)(2,1)} custom-call(bf16[256,512]{1,0:T(8,128)(2,1)} %q_ref, bf16[256,512]{1,0:T(8,128)(2,1)} %k_ref, bf16[256,512]{1,0:T(8,128)(2,1)} %v_ref), custom_call_target="tpu_custom_call" | custom-call | tf_op jit(solution)/shard_map/pallas_call | solution.py:387
  23.2 4.3 %all-to-all-start = ((bf16[4,3,256,128]{3,2,1,0:T(8,128)(2,1)}), bf16[4,3,256,128]{3,2,1,0:T(8,128)(2,1)S(1)}, u32[]{:S(2)}, u32[]{:S(2)}) async-start(bf16[4,3,256,128]{3,2,1,0:T(8,128)(2,1)} %shard_map.150), calls=%async_computation | async-start | bytes 1572864 | tf_op jit(solution)/shard_map/all_to_all | solution.py:393
  27.5 0.0 all-gather.5.cloned.1.call-start
  27.5 0.3 collective-permute-done.e01
  27.8 3.8 %collective-permute-done.1.e30 = bf16[2,128,896]{2,1,0:T(8,128)(2,1)S(1)} collective-permute-done((bf16[2,128,896]{2,1,0:T(8,128)(2,1)}, bf16[2,128,896]{2,1,0:T(8,128)(2,1)S(1)}, u32[]{:S(2)}, u32[]{:S(2)}) %collective-permute-start.1) | collective-permute-done | bytes 458784 | tf_op jit(solution)/shard_map/ppermute | solution.py:383
  31.6 0.0 collective-permute-done.2.e10
  31.6 2.9 %collective-permute-start.3 = (bf16[2,128,896]{2,1,0:T(8,128)(2,1)S(1)}, bf16[2,128,896]{2,1,0:T(8,128)(2,1)S(1)}, u32[]{:S(2)}, u32[]{:S(2)}) collective-permute-start(bf16[2,128,896]{2,1,0:T(8,128)(2,1)S(1)} %collective-permute-done.e01), channel_id=1, source_target_pairs={{0,6},{2,0},{4,2},{6,4},{1,7},{3,1},{5,3},{7,5},{8,14},{10,8},{12,... | collective-permute-start | bytes 1376264 | tf_op jit(solution)/shard_map/ppermute | solution.py:396
  34.5 0.0 collective-permute-start.4
  34.5 5.2 %shard_map.151 = (bf16[1024,896]{1,0:T(8,128)(2,1)}, bf16[896,896]{1,0:T(8,128)(2,1)}, bf16[896,896]{1,0:T(8,128)(2,1)}) custom-call(bf16[896,512]{1,0:T(8,128)(2,1)} %rest_0_.1, bf16[896,512]{1,0:T(8,128)(2,1)} %rest_1_.1, bf16[896,896]{1,0:T(8,128)(2,1)} %wq, bf16[896,896]{1,0:T(8,128)(2,1)} %wo), custom_call_target="tpu_custom_call" | custom-call | tf_op jit(solution)/shard_map/pallas_call | solution.py:401
  39.7 0.0 copy-done.5
  39.7 0.0 copy-done.7
  39.7 0.0 all-to-all-done.pieces
  39.8 0.0 copy-start
  39.8 0.9 slice.4
  40.7 2.5 %collective-permute-done.3.e11 = bf16[2,128,896]{2,1,0:T(8,128)(2,1)S(1)} collective-permute-done((bf16[2,128,896]{2,1,0:T(8,128)(2,1)S(1)}, bf16[2,128,896]{2,1,0:T(8,128)(2,1)S(1)}, u32[]{:S(2)}, u32[]{:S(2)}) %collective-permute-start.3) | collective-permute-done | bytes 458784 | tf_op jit(solution)/shard_map/ppermute | solution.py:396
  43.1 3.4 %collective-permute-done.4.e31 = bf16[2,128,896]{2,1,0:T(8,128)(2,1)S(1)} collective-permute-done((bf16[2,128,896]{2,1,0:T(8,128)(2,1)S(1)}, bf16[2,128,896]{2,1,0:T(8,128)(2,1)S(1)}, u32[]{:S(2)}, u32[]{:S(2)}) %collective-permute-start.4) | collective-permute-done | bytes 458784 | tf_op jit(solution)/shard_map/ppermute | solution.py:397
  46.5 0.0 all-gather.5.cloned.1.call-update
  46.6 0.0 all-gather.7.cloned.1.call-start
  46.6 0.1 collective-permute-start.5
  46.7 11.1 %collective-permute-done.5.e20 = bf16[2,128,896]{2,1,0:T(8,128)(2,1)S(1)} collective-permute-done((bf16[2,128,896]{2,1,0:T(8,128)(2,1)S(1)}, bf16[2,128,896]{2,1,0:T(8,128)(2,1)S(1)}, u32[]{:S(2)}, u32[]{:S(2)}) %collective-permute-start.5) | collective-permute-done | bytes 458784 | tf_op jit(solution)/shard_map/ppermute | solution.py:412
  57.8 9.5 %all-gather.5.cloned.1.call-done = bf16[8,2,256,128]{3,2,1,0:T(8,128)(2,1)} async-done(((bf16[4,2,256,128]{3,2,1,0:T(8,128)(2,1)}), bf16[8,2,256,128]{3,2,1,0:T(8,128)(2,1)}) %all-gather.5.cloned.1.call-update) | async-done | bytes 1048592 | tf_op jit(solution)/shard_map/all_gather | solution.py:410
  67.3 0.0 all-gather.7.cloned.1.call-update
  67.3 3.2 %collective-permute-start.6 = (bf16[2,128,896]{2,1,0:T(8,128)(2,1)S(1)}, bf16[2,128,896]{2,1,0:T(8,128)(2,1)S(1)}, u32[]{:S(2)}, u32[]{:S(2)}) collective-permute-start(bf16[2,128,896]{2,1,0:T(8,128)(2,1)S(1)} %collective-permute-done.3.e11), channel_id=1, source_target_pairs={{0,6},{2,0},{4,2},{6,4},{1,7},{3,1},{5,3},{7,5},{8,14},{10,8},{12,... | collective-permute-start | bytes 1376264 | tf_op jit(solution)/shard_map/ppermute | solution.py:413
  70.5 2.9 %shard_map.152 = (bf16[4,512,256]{2,1,0:T(8,128)(2,1)}, bf16[4,512,256]{2,1,0:T(8,128)(2,1)}) custom-call(bf16[256,512]{1,0:T(8,128)(2,1)} %rest_4_.1, bf16[256,512]{1,0:T(8,128)(2,1)} %rest_5_.1), custom_call_target="tpu_custom_call" | custom-call | tf_op jit(solution)/shard_map/pallas_call | solution.py:419
  73.4 6.8 %collective-permute-done.6.e21 = bf16[2,128,896]{2,1,0:T(8,128)(2,1)S(1)} collective-permute-done((bf16[2,128,896]{2,1,0:T(8,128)(2,1)S(1)}, bf16[2,128,896]{2,1,0:T(8,128)(2,1)S(1)}, u32[]{:S(2)}, u32[]{:S(2)}) %collective-permute-start.6) | collective-permute-done | bytes 458784 | tf_op jit(solution)/shard_map/ppermute | solution.py:413
  80.3 0.0 copy-done.12
  80.3 0.7 copy-done.13
  81.0 11.1 %shard_map.153 = (f32[256,512]{1,0:T(8,128)}, bf16[2,128,896]{2,1,0:T(8,128)(2,1)}, bf16[2,128,896]{2,1,0:T(8,128)(2,1)}, bf16[2,128,896]{2,1,0:T(8,128)(2,1)}, ...) custom-call(s32[2,4]{1,0:T(2,128)} %bitcast.4, ...), custom_call_target="tpu_custom_call" | custom-call | tf_op jit(solution)/shard_map/pallas_call | solution.py:426
  92.1 3.8 %collective-permute-start.7 = (bf16[2,128,896]{2,1,0:T(8,128)(2,1)}, bf16[2,128,896]{2,1,0:T(8,128)(2,1)S(1)}, u32[]{:S(2)}, u32[]{:S(2)}) collective-permute-start(bf16[2,128,896]{2,1,0:T(8,128)(2,1)} %get-tuple-element.84), channel_id=1, source_target_pairs={{0,6},{2,0},{4,2},{6,4},{1,7},{3,1},{5,3},{7,5},{8,14},{10,8},{12,... | collective-permute-start | bytes 1376264 | tf_op jit(solution)/shard_map/ppermute | solution.py:471
  96.0 0.0 collective-permute-start.8
  96.0 8.9 %shard_map.154 = (bf16[256,128]{1,0:T(8,128)(2,1)}, bf16[256,128]{1,0:T(8,128)(2,1)}, bf16[256,128]{1,0:T(8,128)(2,1)}, bf16[256,128]{1,0:T(8,128)(2,1)}) custom-call(bf16[4,3,256,128]{3,2,1,0:T(8,128)(2,1)} %copy-done, bf16[4,4,2,256,128]{4,3,2,1,0:T(8,128)(2,1)} %all-gather.7.cloned.1.call-done.kv_h), custom_call_target="tpu_custom_call" | custom-call | tf_op jit(solution)/shard_map/pallas_call | solution.py:474
  104.9 0.0 copy-start.17
  104.9 0.0 copy-start.4
  104.9 0.3 collective-permute-done.7
  105.2 3.3 %collective-permute-done.8 = bf16[2,128,896]{2,1,0:T(8,128)(2,1)S(1)} collective-permute-done((bf16[2,128,896]{2,1,0:T(8,128)(2,1)}, bf16[2,128,896]{2,1,0:T(8,128)(2,1)S(1)}, u32[]{:S(2)}, u32[]{:S(2)}) %collective-permute-start.8) | collective-permute-done | bytes 458784 | tf_op jit(solution)/shard_map/ppermute | solution.py:472
  108.5 0.0 copy-done.11
  108.5 0.1 add_convert_fusion.2
  108.6 0.4 collective-permute-start.9
  109.0 1.7 %collective-permute-start.10 = (bf16[2,128,896]{2,1,0:T(8,128)(2,1)S(1)}, bf16[2,128,896]{2,1,0:T(8,128)(2,1)S(1)}, u32[]{:S(2)}, u32[]{:S(2)}) collective-permute-start(bf16[2,128,896]{2,1,0:T(8,128)(2,1)S(1)} %copy-done.18), channel_id=1, source_target_pairs={{0,2},{2,4},{4,6},{6,0},{1,3},{3,5},{5,7},{7,1},{8,10},{10,12},{12... | collective-permute-start | bytes 1376264 | tf_op jit(solution)/shard_map/ppermute | solution.py:489
  110.7 2.7 %collective-permute-start.11 = (bf16[256,128]{1,0:T(8,128)(2,1)}, bf16[256,128]{1,0:T(8,128)(2,1)S(1)}, u32[]{:S(2)}, u32[]{:S(2)}) collective-permute-start(bf16[256,128]{1,0:T(8,128)(2,1)} %get-tuple-element.101), channel_id=1, source_target_pairs={{0,96},{32,0},{64,32},{96,64},{1,97},{33,1},{65,33},{97,65},{2,98}... | collective-permute-start | bytes 196616 | tf_op jit(solution)/shard_map/ppermute | solution.py:487
  113.4 0.8 collective-permute-start.12
  114.3 0.8 collective-permute-start.13
  115.0 0.1 add_convert_fusion.1
  115.2 0.5 collective-permute-done.11.s1
  115.7 3.8 %collective-permute-done.12.s2 = bf16[256,128]{1,0:T(8,128)(2,1)S(1)} collective-permute-done((bf16[256,128]{1,0:T(8,128)(2,1)}, bf16[256,128]{1,0:T(8,128)(2,1)S(1)}, u32[]{:S(2)}, u32[]{:S(2)}) %collective-permute-start.12) | collective-permute-done | bytes 65568 | tf_op jit(solution)/shard_map/ppermute | solution.py:487
  119.4 0.7 collective-permute-done.13.s3
  120.1 0.0 collective-permute-done.9
  120.1 0.3 collective-permute-done.10
  120.4 0.7 collective-permute-start.14
  121.1 2.5 %collective-permute-start.15 = (bf16[2,128,896]{2,1,0:T(8,128)(2,1)S(1)}, bf16[2,128,896]{2,1,0:T(8,128)(2,1)S(1)}, u32[]{:S(2)}, u32[]{:S(2)}) collective-permute-start(bf16[2,128,896]{2,1,0:T(8,128)(2,1)S(1)} %copy-done.17), channel_id=1, source_target_pairs={{0,6},{2,0},{4,2},{6,4},{1,7},{3,1},{5,3},{7,5},{8,14},{10,8},{12,... | collective-permute-start | bytes 1376264 | tf_op jit(solution)/shard_map/ppermute | solution.py:495
  123.6 0.0 copy-done.4
  123.6 0.2 add_convert_fusion
  123.8 2.7 %collective-permute-start.16 = (bf16[2,128,896]{2,1,0:T(8,128)(2,1)S(1)}, bf16[2,128,896]{2,1,0:T(8,128)(2,1)S(1)}, u32[]{:S(2)}, u32[]{:S(2)}) collective-permute-start(bf16[2,128,896]{2,1,0:T(8,128)(2,1)S(1)} %add_convert_fusion), channel_id=1, source_target_pairs={{0,1},{1,0},{2,3},{3,2},{4,5},{5,4},{6,7},{7,6},{8,9},{9,8},{10,11... | collective-permute-start | bytes 1376264 | tf_op jit(solution)/shard_map/ppermute | solution.py:493
  126.5 0.0 copy-done.16
  126.5 2.0 %shard_map.155 = bf16[256,512]{1,0:T(8,128)(2,1)} custom-call(bf16[256,128]{1,0:T(8,128)(2,1)} %get-tuple-element.104.s0, bf16[256,128]{1,0:T(8,128)(2,1)} %copy-done.14, bf16[256,128]{1,0:T(8,128)(2,1)} %copy-done.15, bf16[256,128]{1,0:T(8,128)(2,1)} %copy-done.16, f32[256,512]{1,0:T(8,128)} %get-tuple-element.89.cross), custom_call_target="tpu_custom_call" | custom-call | tf_op jit(solution)/shard_map/pallas_call | solution.py:513
  128.5 2.4 %collective-permute-done.14.refs_1_ = bf16[2,128,896]{2,1,0:T(8,128)(2,1)S(1)} collective-permute-done((bf16[2,128,896]{2,1,0:T(8,128)(2,1)S(1)}, bf16[2,128,896]{2,1,0:T(8,128)(2,1)S(1)}, u32[]{:S(2)}, u32[]{:S(2)}) %collective-permute-start.14) | collective-permute-done | bytes 458784 | tf_op jit(solution)/shard_map/ppermute | solution.py:494
  130.9 0.0 collective-permute-done.15.refs_2_
  130.9 3.2 %collective-permute-done.16.refs_3_ = bf16[2,128,896]{2,1,0:T(8,128)(2,1)S(1)} collective-permute-done((bf16[2,128,896]{2,1,0:T(8,128)(2,1)S(1)}, bf16[2,128,896]{2,1,0:T(8,128)(2,1)S(1)}, u32[]{:S(2)}, u32[]{:S(2)}) %collective-permute-start.16) | collective-permute-done | bytes 458784 | tf_op jit(solution)/shard_map/ppermute | solution.py:493
  134.1 0.8 copy-done.3
  134.9 5.6 %shard_map.156 = f32[2,128,896]{2,1,0:T(8,128)} custom-call(bf16[2,128,896]{2,1,0:T(8,128)(2,1)} %get-tuple-element.108.refs_0_, bf16[2,128,896]{2,1,0:T(8,128)(2,1)} %copy-done.1, bf16[2,128,896]{2,1,0:T(8,128)(2,1)} %copy-done.2, bf16[2,128,896]{2,1,0:T(8,128)(2,1)} %copy-done.3, bf16[896,896]{1,0:T(8,128)(2,1)} %get-tuple-element.114.refs_4_, ...), custom_call_target="tpu_custom_call" | custom-call | tf_op jit(solution)/shard_map/pallas_call | solution.py:497
  (28 shorter events, 0.1 us)
Async XLA Ops:
  13.7 14.1 %collective-permute-start = (bf16[2,128,896]{2,1,0:T(8,128)(2,1)}, bf16[2,128,896]{2,1,0:T(8,128)(2,1)S(1)}, u32[]{:S(2)}, u32[]{:S(2)}) collective-permute-start(bf16[2,128,896]{2,1,0:T(8,128)(2,1)} %get-tuple-element.60.e00), channel_id=1, source_target_pairs={{0,1},{1,0},{2,3},{3,2},{4,5},{5,4},{6,7},{7,6},{8,9},{9,8},{10,11... | collective-permute-start | bytes 1376264 | tf_op jit(solution)/shard_map/ppermute | solution.py:382
  17.1 14.5 %collective-permute-start.1 = (bf16[2,128,896]{2,1,0:T(8,128)(2,1)}, bf16[2,128,896]{2,1,0:T(8,128)(2,1)S(1)}, u32[]{:S(2)}, u32[]{:S(2)}) collective-permute-start(bf16[2,128,896]{2,1,0:T(8,128)(2,1)} %get-tuple-element.60.e00), channel_id=1, source_target_pairs={{0,2},{2,4},{4,6},{6,0},{1,3},{3,5},{5,7},{7,1},{8,10},{10,12},{12... | collective-permute-start | bytes 1376264 | tf_op jit(solution)/shard_map/ppermute | solution.py:383
  19.0 12.6 %collective-permute-start.2 = (bf16[2,128,896]{2,1,0:T(8,128)(2,1)}, bf16[2,128,896]{2,1,0:T(8,128)(2,1)S(1)}, u32[]{:S(2)}, u32[]{:S(2)}) collective-permute-start(bf16[2,128,896]{2,1,0:T(8,128)(2,1)} %get-tuple-element.60.e00), channel_id=1, source_target_pairs={{0,6},{2,0},{4,2},{6,4},{1,7},{3,1},{5,3},{7,5},{8,14},{10,8},{12,... | collective-permute-start | bytes 1376264 | tf_op jit(solution)/shard_map/ppermute | solution.py:384
  23.2 16.5 %all-to-all-start = ((bf16[4,3,256,128]{3,2,1,0:T(8,128)(2,1)}), bf16[4,3,256,128]{3,2,1,0:T(8,128)(2,1)S(1)}, u32[]{:S(2)}, u32[]{:S(2)}) async-start(bf16[4,3,256,128]{3,2,1,0:T(8,128)(2,1)} %shard_map.150), calls=%async_computation | async-start | bytes 1572864 | tf_op jit(solution)/shard_map/all_to_all | solution.py:393
  27.5 39.8 %all-gather.5.cloned.1.call-start = ((), (), s32[]{:S(2)}) async-start(), calls=%async_computation.1 | async-start | bytes 1572864 | tf_op jit(solution)/shard_map/all_gather | solution.py:410
  27.8 12.0 %copy-start.5 = (bf16[2,128,896]{2,1,0:T(8,128)(2,1)}, bf16[2,128,896]{2,1,0:T(8,128)(2,1)S(1)}, u32[]{:S(2)}) copy-start(bf16[2,128,896]{2,1,0:T(8,128)(2,1)S(1)} %collective-permute-done.e01) | copy-start | bytes 1376260
  31.6 15.0 %copy-start.6 = (bf16[2,128,896]{2,1,0:T(8,128)(2,1)}, bf16[2,128,896]{2,1,0:T(8,128)(2,1)S(1)}, u32[]{:S(2)}) copy-start(bf16[2,128,896]{2,1,0:T(8,128)(2,1)S(1)} %collective-permute-done.1.e30) | copy-start | bytes 1376260
  31.6 8.1 %copy-start.7 = (bf16[2,128,896]{2,1,0:T(8,128)(2,1)}, bf16[2,128,896]{2,1,0:T(8,128)(2,1)S(1)}, u32[]{:S(2)}) copy-start(bf16[2,128,896]{2,1,0:T(8,128)(2,1)S(1)} %collective-permute-done.2.e10) | copy-start | bytes 1376260
  31.6 11.5 %collective-permute-start.3 = (bf16[2,128,896]{2,1,0:T(8,128)(2,1)S(1)}, bf16[2,128,896]{2,1,0:T(8,128)(2,1)S(1)}, u32[]{:S(2)}, u32[]{:S(2)}) collective-permute-start(bf16[2,128,896]{2,1,0:T(8,128)(2,1)S(1)} %collective-permute-done.e01), channel_id=1, source_target_pairs={{0,6},{2,0},{4,2},{6,4},{1,7},{3,1},{5,3},{7,5},{8,14},{10,8},{12,... | collective-permute-start | bytes 1376264 | tf_op jit(solution)/shard_map/ppermute | solution.py:396
  34.5 12.0 %collective-permute-start.4 = (bf16[2,128,896]{2,1,0:T(8,128)(2,1)S(1)}, bf16[2,128,896]{2,1,0:T(8,128)(2,1)S(1)}, u32[]{:S(2)}, u32[]{:S(2)}) collective-permute-start(bf16[2,128,896]{2,1,0:T(8,128)(2,1)S(1)} %collective-permute-done.e01), channel_id=1, source_target_pairs={{0,2},{2,4},{4,6},{6,0},{1,3},{3,5},{5,7},{7,1},{8,10},{10,12},{12... | collective-permute-start | bytes 1376264 | tf_op jit(solution)/shard_map/ppermute | solution.py:397
  39.8 52.4 %copy-start = (bf16[4,3,256,128]{3,2,1,0:T(8,128)(2,1)}, bf16[4,3,256,128]{3,2,1,0:T(8,128)(2,1)S(1)}, u32[]{:S(2)}) copy-start(bf16[4,3,256,128]{3,2,1,0:T(8,128)(2,1)S(1)} %all-to-all-done.pieces) | copy-start | bytes 2359300
  43.1 37.2 %copy-start.8 = (bf16[2,128,896]{2,1,0:T(8,128)(2,1)}, bf16[2,128,896]{2,1,0:T(8,128)(2,1)S(1)}, u32[]{:S(2)}) copy-start(bf16[2,128,896]{2,1,0:T(8,128)(2,1)S(1)} %collective-permute-done.3.e11) | copy-start | bytes 1376260
  46.5 33.8 %copy-start.9 = (bf16[2,128,896]{2,1,0:T(8,128)(2,1)}, bf16[2,128,896]{2,1,0:T(8,128)(2,1)S(1)}, u32[]{:S(2)}) copy-start(bf16[2,128,896]{2,1,0:T(8,128)(2,1)S(1)} %collective-permute-done.4.e31) | copy-start | bytes 1376260
  46.6 49.4 %all-gather.7.cloned.1.call-start = ((), (), s32[]{:S(2)}) async-start(), calls=%async_computation.2 | async-start | bytes 3145728 | tf_op jit(solution)/shard_map/all_gather | solution.py:416
  46.6 11.2 %collective-permute-start.5 = (bf16[2,128,896]{2,1,0:T(8,128)(2,1)S(1)}, bf16[2,128,896]{2,1,0:T(8,128)(2,1)S(1)}, u32[]{:S(2)}, u32[]{:S(2)}) collective-permute-start(bf16[2,128,896]{2,1,0:T(8,128)(2,1)S(1)} %collective-permute-done.1.e30), channel_id=1, source_target_pairs={{0,2},{2,4},{4,6},{6,0},{1,3},{3,5},{5,7},{7,1},{8,10},{10,12},{12... | collective-permute-start | bytes 1376264 | tf_op jit(solution)/shard_map/ppermute | solution.py:412
  57.8 22.5 %copy-start.12 = (bf16[2,128,896]{2,1,0:T(8,128)(2,1)}, bf16[2,128,896]{2,1,0:T(8,128)(2,1)S(1)}, u32[]{:S(2)}) copy-start(bf16[2,128,896]{2,1,0:T(8,128)(2,1)S(1)} %collective-permute-done.5.e20) | copy-start | bytes 1376260
  67.3 13.0 %collective-permute-start.6 = (bf16[2,128,896]{2,1,0:T(8,128)(2,1)S(1)}, bf16[2,128,896]{2,1,0:T(8,128)(2,1)S(1)}, u32[]{:S(2)}, u32[]{:S(2)}) collective-permute-start(bf16[2,128,896]{2,1,0:T(8,128)(2,1)S(1)} %collective-permute-done.3.e11), channel_id=1, source_target_pairs={{0,6},{2,0},{4,2},{6,4},{1,7},{3,1},{5,3},{7,5},{8,14},{10,8},{12,... | collective-permute-start | bytes 1376264 | tf_op jit(solution)/shard_map/ppermute | solution.py:413
  80.3 0.8 copy-start.13
  92.1 16.4 %copy-start.11 = (bf16[2,128,896]{2,1,0:T(8,128)(2,1)S(1)}, bf16[2,128,896]{2,1,0:T(8,128)(2,1)}, u32[]{:S(2)}) copy-start(bf16[2,128,896]{2,1,0:T(8,128)(2,1)} %get-tuple-element.83) | copy-start | bytes 1376260
  92.1 13.1 %collective-permute-start.7 = (bf16[2,128,896]{2,1,0:T(8,128)(2,1)}, bf16[2,128,896]{2,1,0:T(8,128)(2,1)S(1)}, u32[]{:S(2)}, u32[]{:S(2)}) collective-permute-start(bf16[2,128,896]{2,1,0:T(8,128)(2,1)} %get-tuple-element.84), channel_id=1, source_target_pairs={{0,6},{2,0},{4,2},{6,4},{1,7},{3,1},{5,3},{7,5},{8,14},{10,8},{12,... | collective-permute-start | bytes 1376264 | tf_op jit(solution)/shard_map/ppermute | solution.py:471
  96.0 12.5 %collective-permute-start.8 = (bf16[2,128,896]{2,1,0:T(8,128)(2,1)}, bf16[2,128,896]{2,1,0:T(8,128)(2,1)S(1)}, u32[]{:S(2)}, u32[]{:S(2)}) collective-permute-start(bf16[2,128,896]{2,1,0:T(8,128)(2,1)} %get-tuple-element.85), channel_id=1, source_target_pairs={{0,2},{2,4},{4,6},{6,0},{1,3},{3,5},{5,7},{7,1},{8,10},{10,12},{12... | collective-permute-start | bytes 1376264 | tf_op jit(solution)/shard_map/ppermute | solution.py:472
  96.0 13.0 %copy-start.18 = (bf16[2,128,896]{2,1,0:T(8,128)(2,1)S(1)}, bf16[2,128,896]{2,1,0:T(8,128)(2,1)}, u32[]{:S(2)}) copy-start(bf16[2,128,896]{2,1,0:T(8,128)(2,1)} %get-tuple-element.96) | copy-start | bytes 1376260
  96.0 19.1 %copy-start.10 = (bf16[2,128,896]{2,1,0:T(8,128)(2,1)S(1)}, bf16[2,128,896]{2,1,0:T(8,128)(2,1)}, u32[]{:S(2)}) copy-start(bf16[2,128,896]{2,1,0:T(8,128)(2,1)} %get-tuple-element.97) | copy-start | bytes 1376260
  104.9 16.2 %copy-start.17 = (bf16[2,128,896]{2,1,0:T(8,128)(2,1)S(1)}, bf16[2,128,896]{2,1,0:T(8,128)(2,1)}, u32[]{:S(2)}) copy-start(bf16[2,128,896]{2,1,0:T(8,128)(2,1)} %get-tuple-element.110) | copy-start | bytes 1376260
  104.9 18.7 %copy-start.4 = (bf16[2,128,896]{2,1,0:T(8,128)(2,1)S(1)}, bf16[2,128,896]{2,1,0:T(8,128)(2,1)}, u32[]{:S(2)}) copy-start(bf16[2,128,896]{2,1,0:T(8,128)(2,1)} %get-tuple-element.111) | copy-start | bytes 1376260
  108.6 11.5 %collective-permute-start.9 = (bf16[2,128,896]{2,1,0:T(8,128)(2,1)S(1)}, bf16[2,128,896]{2,1,0:T(8,128)(2,1)S(1)}, u32[]{:S(2)}, u32[]{:S(2)}) collective-permute-start(bf16[2,128,896]{2,1,0:T(8,128)(2,1)S(1)} %add_convert_fusion.2), channel_id=1, source_target_pairs={{0,6},{2,0},{4,2},{6,4},{1,7},{3,1},{5,3},{7,5},{8,14},{10,8},{12,... | collective-permute-start | bytes 1376264 | tf_op jit(solution)/shard_map/ppermute | solution.py:488
  109.0 11.4 %collective-permute-start.10 = (bf16[2,128,896]{2,1,0:T(8,128)(2,1)S(1)}, bf16[2,128,896]{2,1,0:T(8,128)(2,1)S(1)}, u32[]{:S(2)}, u32[]{:S(2)}) collective-permute-start(bf16[2,128,896]{2,1,0:T(8,128)(2,1)S(1)} %copy-done.18), channel_id=1, source_target_pairs={{0,2},{2,4},{4,6},{6,0},{1,3},{3,5},{5,7},{7,1},{8,10},{10,12},{12... | collective-permute-start | bytes 1376264 | tf_op jit(solution)/shard_map/ppermute | solution.py:489
  110.7 4.9 %collective-permute-start.11 = (bf16[256,128]{1,0:T(8,128)(2,1)}, bf16[256,128]{1,0:T(8,128)(2,1)S(1)}, u32[]{:S(2)}, u32[]{:S(2)}) collective-permute-start(bf16[256,128]{1,0:T(8,128)(2,1)} %get-tuple-element.101), channel_id=1, source_target_pairs={{0,96},{32,0},{64,32},{96,64},{1,97},{33,1},{65,33},{97,65},{2,98}... | collective-permute-start | bytes 196616 | tf_op jit(solution)/shard_map/ppermute | solution.py:487
  113.4 6.0 %collective-permute-start.12 = (bf16[256,128]{1,0:T(8,128)(2,1)}, bf16[256,128]{1,0:T(8,128)(2,1)S(1)}, u32[]{:S(2)}, u32[]{:S(2)}) collective-permute-start(bf16[256,128]{1,0:T(8,128)(2,1)} %get-tuple-element.102), channel_id=1, source_target_pairs={{0,64},{32,96},{64,0},{96,32},{1,65},{33,97},{65,1},{97,33},{2,66}... | collective-permute-start | bytes 196616 | tf_op jit(solution)/shard_map/ppermute | solution.py:487
  114.3 5.8 %collective-permute-start.13 = (bf16[256,128]{1,0:T(8,128)(2,1)}, bf16[256,128]{1,0:T(8,128)(2,1)S(1)}, u32[]{:S(2)}, u32[]{:S(2)}) collective-permute-start(bf16[256,128]{1,0:T(8,128)(2,1)} %get-tuple-element.103), channel_id=1, source_target_pairs={{0,32},{32,64},{64,96},{96,0},{1,33},{33,65},{65,97},{97,1},{2,34}... | collective-permute-start | bytes 196616 | tf_op jit(solution)/shard_map/ppermute | solution.py:487
  115.7 10.8 %copy-start.14 = (bf16[256,128]{1,0:T(8,128)(2,1)}, bf16[256,128]{1,0:T(8,128)(2,1)S(1)}, u32[]{:S(2)}) copy-start(bf16[256,128]{1,0:T(8,128)(2,1)S(1)} %collective-permute-done.11.s1) | copy-start | bytes 196612
  119.4 7.1 %copy-start.15 = (bf16[256,128]{1,0:T(8,128)(2,1)}, bf16[256,128]{1,0:T(8,128)(2,1)S(1)}, u32[]{:S(2)}) copy-start(bf16[256,128]{1,0:T(8,128)(2,1)S(1)} %collective-permute-done.12.s2) | copy-start | bytes 196612
  120.1 6.4 %copy-start.16 = (bf16[256,128]{1,0:T(8,128)(2,1)}, bf16[256,128]{1,0:T(8,128)(2,1)S(1)}, u32[]{:S(2)}) copy-start(bf16[256,128]{1,0:T(8,128)(2,1)S(1)} %collective-permute-done.13.s3) | copy-start | bytes 196612
  120.4 10.5 %collective-permute-start.14 = (bf16[2,128,896]{2,1,0:T(8,128)(2,1)S(1)}, bf16[2,128,896]{2,1,0:T(8,128)(2,1)S(1)}, u32[]{:S(2)}, u32[]{:S(2)}) collective-permute-start(bf16[2,128,896]{2,1,0:T(8,128)(2,1)S(1)} %add_convert_fusion.1), channel_id=1, source_target_pairs={{0,2},{2,4},{4,6},{6,0},{1,3},{3,5},{5,7},{7,1},{8,10},{10,12},{12... | collective-permute-start | bytes 1376264 | tf_op jit(solution)/shard_map/ppermute | solution.py:494
  121.1 9.8 %collective-permute-start.15 = (bf16[2,128,896]{2,1,0:T(8,128)(2,1)S(1)}, bf16[2,128,896]{2,1,0:T(8,128)(2,1)S(1)}, u32[]{:S(2)}, u32[]{:S(2)}) collective-permute-start(bf16[2,128,896]{2,1,0:T(8,128)(2,1)S(1)} %copy-done.17), channel_id=1, source_target_pairs={{0,6},{2,0},{4,2},{6,4},{1,7},{3,1},{5,3},{7,5},{8,14},{10,8},{12,... | collective-permute-start | bytes 1376264 | tf_op jit(solution)/shard_map/ppermute | solution.py:495
  123.8 10.3 %collective-permute-start.16 = (bf16[2,128,896]{2,1,0:T(8,128)(2,1)S(1)}, bf16[2,128,896]{2,1,0:T(8,128)(2,1)S(1)}, u32[]{:S(2)}, u32[]{:S(2)}) collective-permute-start(bf16[2,128,896]{2,1,0:T(8,128)(2,1)S(1)} %add_convert_fusion), channel_id=1, source_target_pairs={{0,1},{1,0},{2,3},{3,2},{4,5},{5,4},{6,7},{7,6},{8,9},{9,8},{10,11... | collective-permute-start | bytes 1376264 | tf_op jit(solution)/shard_map/ppermute | solution.py:493
  130.9 3.2 %copy-start.1 = (bf16[2,128,896]{2,1,0:T(8,128)(2,1)}, bf16[2,128,896]{2,1,0:T(8,128)(2,1)S(1)}, u32[]{:S(2)}) copy-start(bf16[2,128,896]{2,1,0:T(8,128)(2,1)S(1)} %collective-permute-done.14.refs_1_) | copy-start | bytes 1376260
  130.9 3.2 %copy-start.2 = (bf16[2,128,896]{2,1,0:T(8,128)(2,1)}, bf16[2,128,896]{2,1,0:T(8,128)(2,1)S(1)}, u32[]{:S(2)}) copy-start(bf16[2,128,896]{2,1,0:T(8,128)(2,1)S(1)} %collective-permute-done.15.refs_2_) | copy-start | bytes 1376260
  134.1 0.8 copy-start.3
Sparse Core Ops, SparseCore 0:
  46.7 20.5 all-gather.4
  68.9 14.2 all-gather.6

commit v7 on v6

--- a/solution.py
+++ b/solution.py
@@ -60,17 +60,25 @@
             out[h, i] = src[:, cols]
 
 
-def attend_kernel(pieces, kv_h, o0, o1, o2, o3, kv, acc, top, sems):
-    loads = [pltpu.make_async_copy(kv_h.at[:, c], kv.at[:, c], sems.at[c]) for c in range(NX)]
-    for c in loads:
-        c.start()
+def attend_kernel(pieces, kv0, kv1, kv2, kv3, o0, o1, o2, o3, kv, acc, top, sems):
+    loads = [
+        [
+            pltpu.make_async_copy(a.at[c], kv.at[i, c], sems.at[c, i])
+            for i, a in enumerate((kv0, kv1, kv2, kv3))
+        ]
+        for c in range(NX)
+    ]
+    for chunk in loads:
+        for c in chunk:
+            c.start()
     x = lax.axis_index("x")
     r = lax.axis_index("yl") * 2 + lax.axis_index("core")
     scale = LOG2E / math.sqrt(HSIZE)
     rows = pieces.shape[2]
     ones = jnp.ones((rows, HSIZE), BF16)
     for xq in range(NX):
-        loads[xq].wait()
+        for c in loads[xq]:
+            c.wait()
         q = pieces[xq, 0]
 
         def group(xk):
@@ -79,7 +87,7 @@
                 at = lax.broadcasted_iota(jnp.int32, (rows, rows), 1)
                 upto = lax.broadcasted_iota(jnp.int32, (rows, rows), 0)
                 scores = [
-                    jnp.where(at + (i % 2 * 2 + i // 2) * rows <= upto + r * rows, s, -1e30)
+                    jnp.where(at + jnp.bitwise_xor(r, i) * rows <= upto + r * rows, s, -1e30)
                     for i, s in enumerate(scores)
                 ]
             best = jnp.maximum(
@@ -407,13 +415,16 @@
 
     own_kv = pieces[:, 1:]
     e30, e11, e31, own_kv, *turned = after((e30, e11, e31, own_kv, *turned))
-    half_kv = lax.all_gather(own_kv, "yl", axis=0)
+    swap = [(0, 3), (1, 2), (2, 1), (3, 0)]
+    kvs = [
+        own_kv,
+        lax.ppermute(own_kv, "core", shift(2, 1)),
+        lax.ppermute(own_kv, "yl", shift(2, 1)),
+        lax.ppermute(own_kv, ("yl", "core"), swap),
+    ]
     kv_t, wq_t, wo_t = turned
     e20 = lax.ppermute(e30, "z", shift(NX, 1))
     e21 = lax.ppermute(e11, "z", shift(NX, -1))
-
-    half_kv, _ = after((half_kv, e20))
-    kv = lax.all_gather(half_kv, "core", axis=0).reshape((4,) + own_kv.shape)
 
     queries, grads, _ = after((cross_q, mixed_grad, e11))
     qm_t, gm_t = call(
@@ -470,19 +481,19 @@
 
     far1 = lax.ppermute(p21, "z", shift(NX, -1))
     far0 = lax.ppermute(p20, "z", shift(NX, 1))
-    kv, _ = after((kv, cross))
+    *kvs, _ = after((*kvs, cross))
     outs = call(
         attend_kernel,
         out_shape=[struct((rows, HSIZE), BF16)] * NX,
-        in_specs=[vmem(), hbm()],
+        in_specs=[vmem()] + [hbm()] * 4,
         out_specs=[vmem()] * NX,
         scratch_shapes=[
-            pltpu.VMEM(kv.shape, BF16),
+            pltpu.VMEM((4,) + own_kv.shape, BF16),
             pltpu.VMEM((rows, 2 * HSIZE), F32),
             pltpu.VMEM((rows, 1), F32),
-            pltpu.SemaphoreType.DMA((NX,)),
+            pltpu.SemaphoreType.DMA((NX, 4)),
         ],
-    )(pieces, kv)
+    )(pieces, *kvs)
     far1, far0, p11, *outs = after((far1, far0, p11, *outs))
     selfs = [outs[0]] + [lax.ppermute(outs[d], "x", shift(NX, -d)) for d in range(1, NX)]
     down1 = lax.ppermute(add(p31, far1), "z", shift(NX, -1))

time: 148 us -> 108 us (0.73)
  waiting for transfers between devices: 51.8 us -> 23.3 us
  between operations: 14.2 us -> 1.02 us
    all_gather x2 -> x0, waiting for transfers between devices: 9.51 us -> none  [the longest x1 9.51 us: local(): half_kv = lax.all_gather(own_kv, 'yl', axis=0)]
    ppermute x1, waiting for transfers between devices: 11.1 us -> 2.84 us  [local(): e20 = lax.ppermute(e30, 'z', shift(NX, 1))]
    ppermute x1, waiting for transfers between devices: 6.84 us -> 0.01 us  [local(): e21 = lax.ppermute(e11, 'z', shift(NX, -1))]
    ppermute x1, waiting for transfers between devices: 3.31 us -> 0.01 us  [local(): far0 = lax.ppermute(p20, 'z', shift(NX, 1))]
    ppermute x1, starting transfers between devices: 0.35 us -> 3.3 us  [local(): down1 = lax.ppermute(add(p31, far1), 'z', shift(NX, -1))]
    ppermute x0 -> x3, starting transfers between devices: none -> 2.14 us  [the longest x1 1.46 us: local(): lax.ppermute(own_kv, 'core', shift(2, 1))]
    ppermute x1, starting transfers between devices: 1.74 us -> 0.01 us  [local(): up1 = lax.ppermute(p11, 'z', shift(NX, 1))]
    unnamed x38 -> x46, local copies, waits for them, and re-layouts: 1.66 us -> 3.02 us
  transfers between devices with their start and end apart: 20 -> 21, of which waited for: 15 -> 11; matrix products, arithmetic and copies ran while one was open for 1% -> 0% of each run, Pallas kernels for 22% -> 30%
where the time goes in v7:
time: 108 us; the launch traced here: 107 us
  Pallas kernels  44.5 us (41%)
  starting transfers between devices  35.2 us (33%)
  waiting for transfers between devices  23.3 us (22%)
  local copies, waits for them, and re-layouts  3.06 us (3%)
    pallas_call x1, Pallas kernels, local(): call(cross_kernel, out_shape=[struct((rows, width), F32)] + [struct((slot...  11.1 us
    pallas_call x1, Pallas kernels, local(): call(attend_kernel, out_shape=[struct((rows, HSIZE), BF16)] * NX, in_spec...  9.03 us
    pallas_call x1, Pallas kernels, local(): call(encode_kernel, out_shape=[struct((slots, nl, ew), BF16), struct((slo...  6.54 us
    pallas_call x1, Pallas kernels, local(): call(pullback_kernel, out_shape=struct((slots, nl, ew), F32), in_specs=[h...  5.59 us
    pallas_call x1, Pallas kernels, local(): call(turn_kernel, out_shape=[struct((2 * width, ew), BF16)] + [struct((ew...  5.26 us
    ppermute x3, waiting for transfers between devices, local(): lax.ppermute(outs[d], 'x', shift(NX, -d))  4.86 us
    ppermute x3, starting transfers between devices, local(): lax.ppermute(outs[d], 'x', shift(NX, -d))  4.36 us
    all_to_all x1, starting transfers between devices, local(): pieces = lax.all_to_all(packed, 'x', 0, 0)  4.3 us
  transfers between devices with their start and end apart: 21, of which 11 were waited for; matrix products, arithmetic and copies ran while one was open for 0% of the time, Pallas kernels for 30%

profile of v7, /device:TPU:0, one launch (start us, length us, event | category | flops | bytes accessed | tf_op | source)
XLA Modules:
  0.0 107.4 jit_solution(15689299939764675863)
XLA Ops:
  0.6 6.5 %shard_map.149 = (bf16[2,128,896]{2,1,0:T(8,128)(2,1)}, f32[2,256,128]{2,1,0:T(8,128)}, bf16[2,64,896]{2,1,0:T(8,128)(2,1)}, bf16[2,64,896]{2,1,0:T(8,128)(2,1)}) custom-call(s32[2,4]{1,0:T(2,128)} %bitcast.1, bf16[2,128,896]{2,1,0:T(8,128)(2,1)} %nb_h.1, bf16[256,896]{1,0:T(8,128)(2,1)} %ctx_h.1, bf16[896,896]{1,0:T(8,128)(2,1)} %wq, ...), custom_call_target="tpu_custom_call" | custom-call | tf_op jit(solution)/shard_map/pallas_call | solution.py:375
  7.2 3.4 %collective-permute-start = (bf16[2,128,896]{2,1,0:T(8,128)(2,1)}, bf16[2,128,896]{2,1,0:T(8,128)(2,1)S(1)}, u32[]{:S(2)}, u32[]{:S(2)}) collective-permute-start(bf16[2,128,896]{2,1,0:T(8,128)(2,1)} %get-tuple-element.62.e00), channel_id=1, source_target_pairs={{0,1},{1,0},{2,3},{3,2},{4,5},{5,4},{6,7},{7,6},{8,9},{9,8},{10,11... | collective-permute-start | bytes 1376264 | tf_op jit(solution)/shard_map/ppermute | solution.py:390
  10.6 1.9 %collective-permute-start.1 = (bf16[2,128,896]{2,1,0:T(8,128)(2,1)}, bf16[2,128,896]{2,1,0:T(8,128)(2,1)S(1)}, u32[]{:S(2)}, u32[]{:S(2)}) collective-permute-start(bf16[2,128,896]{2,1,0:T(8,128)(2,1)} %get-tuple-element.62.e00), channel_id=1, source_target_pairs={{0,2},{2,4},{4,6},{6,0},{1,3},{3,5},{5,7},{7,1},{8,10},{10,12},{12... | collective-permute-start | bytes 1376264 | tf_op jit(solution)/shard_map/ppermute | solution.py:391
  12.5 2.1 %collective-permute-start.2 = (bf16[2,128,896]{2,1,0:T(8,128)(2,1)}, bf16[2,128,896]{2,1,0:T(8,128)(2,1)S(1)}, u32[]{:S(2)}, u32[]{:S(2)}) collective-permute-start(bf16[2,128,896]{2,1,0:T(8,128)(2,1)} %get-tuple-element.62.e00), channel_id=1, source_target_pairs={{0,6},{2,0},{4,2},{6,4},{1,7},{3,1},{5,3},{7,5},{8,14},{10,8},{12,... | collective-permute-start | bytes 1376264 | tf_op jit(solution)/shard_map/ppermute | solution.py:392
  14.6 2.1 %shard_map.150 = bf16[4,3,256,128]{3,2,1,0:T(8,128)(2,1)} custom-call(bf16[256,512]{1,0:T(8,128)(2,1)} %q_ref, bf16[256,512]{1,0:T(8,128)(2,1)} %k_ref, bf16[256,512]{1,0:T(8,128)(2,1)} %v_ref), custom_call_target="tpu_custom_call" | custom-call | tf_op jit(solution)/shard_map/pallas_call | solution.py:395
  16.7 4.3 %all-to-all-start = ((bf16[4,3,256,128]{3,2,1,0:T(8,128)(2,1)}), bf16[4,3,256,128]{3,2,1,0:T(8,128)(2,1)S(1)}, u32[]{:S(2)}, u32[]{:S(2)}) async-start(bf16[4,3,256,128]{3,2,1,0:T(8,128)(2,1)} %shard_map.150), calls=%async_computation | async-start | bytes 1572864 | tf_op jit(solution)/shard_map/all_to_all | solution.py:401
  21.0 0.3 collective-permute-done.e01
  21.3 3.8 %collective-permute-done.1.e30 = bf16[2,128,896]{2,1,0:T(8,128)(2,1)S(1)} collective-permute-done((bf16[2,128,896]{2,1,0:T(8,128)(2,1)}, bf16[2,128,896]{2,1,0:T(8,128)(2,1)S(1)}, u32[]{:S(2)}, u32[]{:S(2)}) %collective-permute-start.1) | collective-permute-done | bytes 458784 | tf_op jit(solution)/shard_map/ppermute | solution.py:391
  25.1 0.0 collective-permute-done.2.e10
  25.1 2.9 %collective-permute-start.3 = (bf16[2,128,896]{2,1,0:T(8,128)(2,1)S(1)}, bf16[2,128,896]{2,1,0:T(8,128)(2,1)S(1)}, u32[]{:S(2)}, u32[]{:S(2)}) collective-permute-start(bf16[2,128,896]{2,1,0:T(8,128)(2,1)S(1)} %collective-permute-done.e01), channel_id=1, source_target_pairs={{0,6},{2,0},{4,2},{6,4},{1,7},{3,1},{5,3},{7,5},{8,14},{10,8},{12,... | collective-permute-start | bytes 1376264 | tf_op jit(solution)/shard_map/ppermute | solution.py:404
  28.0 0.0 collective-permute-start.4
  28.0 5.3 %shard_map.151 = (bf16[1024,896]{1,0:T(8,128)(2,1)}, bf16[896,896]{1,0:T(8,128)(2,1)}, bf16[896,896]{1,0:T(8,128)(2,1)}) custom-call(bf16[896,512]{1,0:T(8,128)(2,1)} %rest_0_.1, bf16[896,512]{1,0:T(8,128)(2,1)} %rest_1_.1, bf16[896,896]{1,0:T(8,128)(2,1)} %wq, bf16[896,896]{1,0:T(8,128)(2,1)} %wo), custom_call_target="tpu_custom_call" | custom-call | tf_op jit(solution)/shard_map/pallas_call | solution.py:409
  33.3 0.0 all-to-all-done.pieces
  33.3 0.0 copy-start
  33.3 3.3 %collective-permute-done.3.e11 = bf16[2,128,896]{2,1,0:T(8,128)(2,1)S(1)} collective-permute-done((bf16[2,128,896]{2,1,0:T(8,128)(2,1)S(1)}, bf16[2,128,896]{2,1,0:T(8,128)(2,1)S(1)}, u32[]{:S(2)}, u32[]{:S(2)}) %collective-permute-start.3) | collective-permute-done | bytes 458784 | tf_op jit(solution)/shard_map/ppermute | solution.py:404
  36.6 3.4 %collective-permute-done.4.e31 = bf16[2,128,896]{2,1,0:T(8,128)(2,1)S(1)} collective-permute-done((bf16[2,128,896]{2,1,0:T(8,128)(2,1)S(1)}, bf16[2,128,896]{2,1,0:T(8,128)(2,1)S(1)}, u32[]{:S(2)}, u32[]{:S(2)}) %collective-permute-start.4) | collective-permute-done | bytes 458784 | tf_op jit(solution)/shard_map/ppermute | solution.py:405
  40.0 0.0 copy-done.10
  40.0 0.0 collective-permute-start.5
  40.0 3.2 %collective-permute-start.6 = (bf16[2,128,896]{2,1,0:T(8,128)(2,1)S(1)}, bf16[2,128,896]{2,1,0:T(8,128)(2,1)S(1)}, u32[]{:S(2)}, u32[]{:S(2)}) collective-permute-start(bf16[2,128,896]{2,1,0:T(8,128)(2,1)S(1)} %collective-permute-done.3.e11), channel_id=1, source_target_pairs={{0,6},{2,0},{4,2},{6,4},{1,7},{3,1},{5,3},{7,5},{8,14},{10,8},{12,... | collective-permute-start | bytes 1376264 | tf_op jit(solution)/shard_map/ppermute | solution.py:427
  43.3 0.7 collective-permute-start.10
  43.9 0.0 collective-permute-start.11
  43.9 1.5 %collective-permute-start.9 = (bf16[4,2,256,128]{3,2,1,0:T(8,128)(2,1)S(1)}, bf16[4,2,256,128]{3,2,1,0:T(8,128)(2,1)S(1)}, u32[]{:S(2)}, u32[]{:S(2)}) collective-permute-start(bf16[4,2,256,128]{3,2,1,0:T(8,128)(2,1)S(1)} %slice.4.kv0), channel_id=1, source_target_pairs={{0,8},{8,0},{1,9},{9,1},{2,10},{10,2},{3,11},{11,3},{4,12},{12,4},... | collective-permute-start | bytes 1572872 | tf_op jit(solution)/shard_map/ppermute | solution.py:421
  45.4 2.9 %shard_map.152 = (bf16[4,512,256]{2,1,0:T(8,128)(2,1)}, bf16[4,512,256]{2,1,0:T(8,128)(2,1)}) custom-call(bf16[256,512]{1,0:T(8,128)(2,1)} %rest_4_.1, bf16[256,512]{1,0:T(8,128)(2,1)} %rest_5_.1), custom_call_target="tpu_custom_call" | custom-call | tf_op jit(solution)/shard_map/pallas_call | solution.py:430
  48.3 2.8 %collective-permute-done.5.e20 = bf16[2,128,896]{2,1,0:T(8,128)(2,1)S(1)} collective-permute-done((bf16[2,128,896]{2,1,0:T(8,128)(2,1)S(1)}, bf16[2,128,896]{2,1,0:T(8,128)(2,1)S(1)}, u32[]{:S(2)}, u32[]{:S(2)}) %collective-permute-start.5) | collective-permute-done | bytes 458784 | tf_op jit(solution)/shard_map/ppermute | solution.py:426
  51.1 0.0 collective-permute-done.6.e21
  51.1 0.7 copy-done.16
  51.9 0.2 copy-done.17
  52.0 11.1 %shard_map.153 = (f32[256,512]{1,0:T(8,128)}, bf16[2,128,896]{2,1,0:T(8,128)(2,1)}, bf16[2,128,896]{2,1,0:T(8,128)(2,1)}, bf16[2,128,896]{2,1,0:T(8,128)(2,1)}, ...) custom-call(s32[2,4]{1,0:T(2,128)} %bitcast.2, ...), custom_call_target="tpu_custom_call" | custom-call | tf_op jit(solution)/shard_map/pallas_call | solution.py:437
  63.2 3.0 %collective-permute-start.7 = (bf16[2,128,896]{2,1,0:T(8,128)(2,1)}, bf16[2,128,896]{2,1,0:T(8,128)(2,1)S(1)}, u32[]{:S(2)}, u32[]{:S(2)}) collective-permute-start(bf16[2,128,896]{2,1,0:T(8,128)(2,1)} %get-tuple-element.86), channel_id=1, source_target_pairs={{0,6},{2,0},{4,2},{6,4},{1,7},{3,1},{5,3},{7,5},{8,14},{10,8},{12,... | collective-permute-start | bytes 1376264 | tf_op jit(solution)/shard_map/ppermute | solution.py:482
  66.1 0.0 collective-permute-start.8
  66.1 0.0 collective-permute-done.10.kv2
  66.1 0.0 collective-permute-done.11.kv3
  66.2 0.0 collective-permute-done.9.kv1
  66.2 0.0 copy-start.4
  66.2 0.8 copy-done.2
  67.0 0.2 copy-done.3
  67.1 0.1 copy-done.4
  67.3 9.0 %shard_map.154 = (bf16[256,128]{1,0:T(8,128)(2,1)}, bf16[256,128]{1,0:T(8,128)(2,1)}, bf16[256,128]{1,0:T(8,128)(2,1)}, bf16[256,128]{1,0:T(8,128)(2,1)}) custom-call(bf16[4,3,256,128]{3,2,1,0:T(8,128)(2,1)} %copy-done, bf16[4,2,256,128]{3,2,1,0:T(8,128)(2,1)} %copy-done.1, bf16[4,2,256,128]{3,2,1,0:T(8,128)(2,1)} %copy-done.4, ...), custom_call_target="tpu_custom_call" | custom-call | tf_op jit(solution)/shard_map/pallas_call | solution.py:485
  76.3 0.0 collective-permute-done.7
  76.3 0.0 collective-permute-done.8
  76.4 0.1 add_convert_fusion.2
  76.5 3.3 %collective-permute-start.12 = (bf16[2,128,896]{2,1,0:T(8,128)(2,1)S(1)}, bf16[2,128,896]{2,1,0:T(8,128)(2,1)S(1)}, u32[]{:S(2)}, u32[]{:S(2)}) collective-permute-start(bf16[2,128,896]{2,1,0:T(8,128)(2,1)S(1)} %add_convert_fusion.2), channel_id=1, source_target_pairs={{0,6},{2,0},{4,2},{6,4},{1,7},{3,1},{5,3},{7,5},{8,14},{10,8},{12,... | collective-permute-start | bytes 1376264 | tf_op jit(solution)/shard_map/ppermute | solution.py:499
  79.8 0.0 collective-permute-start.13
  79.8 2.7 %collective-permute-start.14 = (bf16[256,128]{1,0:T(8,128)(2,1)}, bf16[256,128]{1,0:T(8,128)(2,1)S(1)}, u32[]{:S(2)}, u32[]{:S(2)}) collective-permute-start(bf16[256,128]{1,0:T(8,128)(2,1)} %get-tuple-element.105), channel_id=1, source_target_pairs={{0,96},{32,0},{64,32},{96,64},{1,97},{33,1},{65,33},{97,65},{2,98}... | collective-permute-start | bytes 196616 | tf_op jit(solution)/shard_map/ppermute | solution.py:498
  82.4 0.9 collective-permute-start.15
  83.3 0.8 collective-permute-start.16
  84.1 0.1 add_convert_fusion.1
  84.3 0.4 collective-permute-done.14.s1
  84.7 3.8 %collective-permute-done.15.s2 = bf16[256,128]{1,0:T(8,128)(2,1)S(1)} collective-permute-done((bf16[256,128]{1,0:T(8,128)(2,1)}, bf16[256,128]{1,0:T(8,128)(2,1)S(1)}, u32[]{:S(2)}, u32[]{:S(2)}) %collective-permute-start.15) | collective-permute-done | bytes 65568 | tf_op jit(solution)/shard_map/ppermute | solution.py:498
  88.4 0.7 collective-permute-done.16.s3
  89.1 0.0 collective-permute-done.12
  89.1 0.3 collective-permute-done.13
  89.5 0.0 copy-done.8
  89.5 0.2 add_convert_fusion
  89.6 1.4 %collective-permute-start.19 = (bf16[2,128,896]{2,1,0:T(8,128)(2,1)S(1)}, bf16[2,128,896]{2,1,0:T(8,128)(2,1)S(1)}, u32[]{:S(2)}, u32[]{:S(2)}) collective-permute-start(bf16[2,128,896]{2,1,0:T(8,128)(2,1)S(1)} %add_convert_fusion), channel_id=1, source_target_pairs={{0,1},{1,0},{2,3},{3,2},{4,5},{5,4},{6,7},{7,6},{8,9},{9,8},{10,11... | collective-permute-start | bytes 1376264 | tf_op jit(solution)/shard_map/ppermute | solution.py:504
  91.0 0.0 collective-permute-start.17
  91.0 3.2 %collective-permute-start.18 = (bf16[2,128,896]{2,1,0:T(8,128)(2,1)S(1)}, bf16[2,128,896]{2,1,0:T(8,128)(2,1)S(1)}, u32[]{:S(2)}, u32[]{:S(2)}) collective-permute-start(bf16[2,128,896]{2,1,0:T(8,128)(2,1)S(1)} %copy-done.21), channel_id=1, source_target_pairs={{0,6},{2,0},{4,2},{6,4},{1,7},{3,1},{5,3},{7,5},{8,14},{10,8},{12,... | collective-permute-start | bytes 1376264 | tf_op jit(solution)/shard_map/ppermute | solution.py:506
  94.2 2.0 %shard_map.155 = bf16[256,512]{1,0:T(8,128)(2,1)} custom-call(bf16[256,128]{1,0:T(8,128)(2,1)} %get-tuple-element.108.s0, bf16[256,128]{1,0:T(8,128)(2,1)} %copy-done.18, bf16[256,128]{1,0:T(8,128)(2,1)} %copy-done.19, bf16[256,128]{1,0:T(8,128)(2,1)} %copy-done.20, f32[256,512]{1,0:T(8,128)} %get-tuple-element.90.cross), custom_call_target="tpu_custom_call" | custom-call | tf_op jit(solution)/shard_map/pallas_call | solution.py:524
  96.2 3.5 %collective-permute-done.19.refs_3_ = bf16[2,128,896]{2,1,0:T(8,128)(2,1)S(1)} collective-permute-done((bf16[2,128,896]{2,1,0:T(8,128)(2,1)S(1)}, bf16[2,128,896]{2,1,0:T(8,128)(2,1)S(1)}, u32[]{:S(2)}, u32[]{:S(2)}) %collective-permute-start.19) | collective-permute-done | bytes 458784 | tf_op jit(solution)/shard_map/ppermute | solution.py:504
  99.7 1.0 collective-permute-done.17.refs_1_
  100.7 0.0 collective-permute-done.18.refs_2_
  100.7 0.8 copy-done.6
  101.5 0.2 copy-done.7
  101.6 5.6 %shard_map.156 = f32[2,128,896]{2,1,0:T(8,128)} custom-call(bf16[2,128,896]{2,1,0:T(8,128)(2,1)} %get-tuple-element.112.refs_0_, bf16[2,128,896]{2,1,0:T(8,128)(2,1)} %copy-done.6, bf16[2,128,896]{2,1,0:T(8,128)(2,1)} %copy-done.7, bf16[2,128,896]{2,1,0:T(8,128)(2,1)} %copy-done.5, bf16[896,896]{1,0:T(8,128)(2,1)} %get-tuple-element.118.refs_4_, ...), custom_call_target="tpu_custom_call" | custom-call | tf_op jit(solution)/shard_map/pallas_call | solution.py:508
  (36 shorter events, 0.1 us)
Async XLA Ops:
  7.2 14.1 %collective-permute-start = (bf16[2,128,896]{2,1,0:T(8,128)(2,1)}, bf16[2,128,896]{2,1,0:T(8,128)(2,1)S(1)}, u32[]{:S(2)}, u32[]{:S(2)}) collective-permute-start(bf16[2,128,896]{2,1,0:T(8,128)(2,1)} %get-tuple-element.62.e00), channel_id=1, source_target_pairs={{0,1},{1,0},{2,3},{3,2},{4,5},{5,4},{6,7},{7,6},{8,9},{9,8},{10,11... | collective-permute-start | bytes 1376264 | tf_op jit(solution)/shard_map/ppermute | solution.py:390
  10.6 14.5 %collective-permute-start.1 = (bf16[2,128,896]{2,1,0:T(8,128)(2,1)}, bf16[2,128,896]{2,1,0:T(8,128)(2,1)S(1)}, u32[]{:S(2)}, u32[]{:S(2)}) collective-permute-start(bf16[2,128,896]{2,1,0:T(8,128)(2,1)} %get-tuple-element.62.e00), channel_id=1, source_target_pairs={{0,2},{2,4},{4,6},{6,0},{1,3},{3,5},{5,7},{7,1},{8,10},{10,12},{12... | collective-permute-start | bytes 1376264 | tf_op jit(solution)/shard_map/ppermute | solution.py:391
  12.5 12.6 %collective-permute-start.2 = (bf16[2,128,896]{2,1,0:T(8,128)(2,1)}, bf16[2,128,896]{2,1,0:T(8,128)(2,1)S(1)}, u32[]{:S(2)}, u32[]{:S(2)}) collective-permute-start(bf16[2,128,896]{2,1,0:T(8,128)(2,1)} %get-tuple-element.62.e00), channel_id=1, source_target_pairs={{0,6},{2,0},{4,2},{6,4},{1,7},{3,1},{5,3},{7,5},{8,14},{10,8},{12,... | collective-permute-start | bytes 1376264 | tf_op jit(solution)/shard_map/ppermute | solution.py:392
  16.7 16.6 %all-to-all-start = ((bf16[4,3,256,128]{3,2,1,0:T(8,128)(2,1)}), bf16[4,3,256,128]{3,2,1,0:T(8,128)(2,1)S(1)}, u32[]{:S(2)}, u32[]{:S(2)}) async-start(bf16[4,3,256,128]{3,2,1,0:T(8,128)(2,1)} %shard_map.150), calls=%async_computation | async-start | bytes 1572864 | tf_op jit(solution)/shard_map/all_to_all | solution.py:401
  21.3 12.0 %copy-start.9 = (bf16[2,128,896]{2,1,0:T(8,128)(2,1)}, bf16[2,128,896]{2,1,0:T(8,128)(2,1)S(1)}, u32[]{:S(2)}) copy-start(bf16[2,128,896]{2,1,0:T(8,128)(2,1)S(1)} %collective-permute-done.e01) | copy-start | bytes 1376260
  25.1 14.9 %copy-start.10 = (bf16[2,128,896]{2,1,0:T(8,128)(2,1)}, bf16[2,128,896]{2,1,0:T(8,128)(2,1)S(1)}, u32[]{:S(2)}) copy-start(bf16[2,128,896]{2,1,0:T(8,128)(2,1)S(1)} %collective-permute-done.1.e30) | copy-start | bytes 1376260
  25.1 8.2 %copy-start.11 = (bf16[2,128,896]{2,1,0:T(8,128)(2,1)}, bf16[2,128,896]{2,1,0:T(8,128)(2,1)S(1)}, u32[]{:S(2)}) copy-start(bf16[2,128,896]{2,1,0:T(8,128)(2,1)S(1)} %collective-permute-done.2.e10) | copy-start | bytes 1376260
  25.1 11.5 %collective-permute-start.3 = (bf16[2,128,896]{2,1,0:T(8,128)(2,1)S(1)}, bf16[2,128,896]{2,1,0:T(8,128)(2,1)S(1)}, u32[]{:S(2)}, u32[]{:S(2)}) collective-permute-start(bf16[2,128,896]{2,1,0:T(8,128)(2,1)S(1)} %collective-permute-done.e01), channel_id=1, source_target_pairs={{0,6},{2,0},{4,2},{6,4},{1,7},{3,1},{5,3},{7,5},{8,14},{10,8},{12,... | collective-permute-start | bytes 1376264 | tf_op jit(solution)/shard_map/ppermute | solution.py:404
  28.0 12.0 %collective-permute-start.4 = (bf16[2,128,896]{2,1,0:T(8,128)(2,1)S(1)}, bf16[2,128,896]{2,1,0:T(8,128)(2,1)S(1)}, u32[]{:S(2)}, u32[]{:S(2)}) collective-permute-start(bf16[2,128,896]{2,1,0:T(8,128)(2,1)S(1)} %collective-permute-done.e01), channel_id=1, source_target_pairs={{0,2},{2,4},{4,6},{6,0},{1,3},{3,5},{5,7},{7,1},{8,10},{10,12},{12... | collective-permute-start | bytes 1376264 | tf_op jit(solution)/shard_map/ppermute | solution.py:405
  33.3 29.9 %copy-start = (bf16[4,3,256,128]{3,2,1,0:T(8,128)(2,1)}, bf16[4,3,256,128]{3,2,1,0:T(8,128)(2,1)S(1)}, u32[]{:S(2)}) copy-start(bf16[4,3,256,128]{3,2,1,0:T(8,128)(2,1)S(1)} %all-to-all-done.pieces) | copy-start | bytes 2359300
  33.3 29.8 %copy-start.1 = (bf16[4,2,256,128]{3,2,1,0:T(8,128)(2,1)}, bf16[4,2,256,128]{3,2,1,0:T(8,128)(2,1)S(1)}, u32[]{:S(2)}) copy-start(bf16[4,2,256,128]{3,2,1,0:T(8,128)(2,1)S(1)} %slice.4.kv0) | copy-start | bytes 1572868
  36.6 14.5 %copy-start.13 = (bf16[2,128,896]{2,1,0:T(8,128)(2,1)}, bf16[2,128,896]{2,1,0:T(8,128)(2,1)S(1)}, u32[]{:S(2)}) copy-start(bf16[2,128,896]{2,1,0:T(8,128)(2,1)S(1)} %collective-permute-done.3.e11) | copy-start | bytes 1376260
  40.0 11.1 %copy-start.14 = (bf16[2,128,896]{2,1,0:T(8,128)(2,1)}, bf16[2,128,896]{2,1,0:T(8,128)(2,1)S(1)}, u32[]{:S(2)}) copy-start(bf16[2,128,896]{2,1,0:T(8,128)(2,1)S(1)} %collective-permute-done.4.e31) | copy-start | bytes 1376260
  40.0 11.1 %collective-permute-start.5 = (bf16[2,128,896]{2,1,0:T(8,128)(2,1)S(1)}, bf16[2,128,896]{2,1,0:T(8,128)(2,1)S(1)}, u32[]{:S(2)}, u32[]{:S(2)}) collective-permute-start(bf16[2,128,896]{2,1,0:T(8,128)(2,1)S(1)} %collective-permute-done.1.e30), channel_id=1, source_target_pairs={{0,2},{2,4},{4,6},{6,0},{1,3},{3,5},{5,7},{7,1},{8,10},{10,12},{12... | collective-permute-start | bytes 1376264 | tf_op jit(solution)/shard_map/ppermute | solution.py:426
  40.0 11.1 %collective-permute-start.6 = (bf16[2,128,896]{2,1,0:T(8,128)(2,1)S(1)}, bf16[2,128,896]{2,1,0:T(8,128)(2,1)S(1)}, u32[]{:S(2)}, u32[]{:S(2)}) collective-permute-start(bf16[2,128,896]{2,1,0:T(8,128)(2,1)S(1)} %collective-permute-done.3.e11), channel_id=1, source_target_pairs={{0,6},{2,0},{4,2},{6,4},{1,7},{3,1},{5,3},{7,5},{8,14},{10,8},{12,... | collective-permute-start | bytes 1376264 | tf_op jit(solution)/shard_map/ppermute | solution.py:427
  43.3 22.9 %collective-permute-start.10 = (bf16[4,2,256,128]{3,2,1,0:T(8,128)(2,1)S(1)}, bf16[4,2,256,128]{3,2,1,0:T(8,128)(2,1)S(1)}, u32[]{:S(2)}, u32[]{:S(2)}) collective-permute-start(bf16[4,2,256,128]{3,2,1,0:T(8,128)(2,1)S(1)} %slice.4.kv0), channel_id=1, source_target_pairs={{0,16},{16,0},{1,17},{17,1},{2,18},{18,2},{3,19},{19,3},{4,20},{20... | collective-permute-start | bytes 1572872 | tf_op jit(solution)/shard_map/ppermute | solution.py:422
  43.9 22.2 %collective-permute-start.11 = (bf16[4,2,256,128]{3,2,1,0:T(8,128)(2,1)S(1)}, bf16[4,2,256,128]{3,2,1,0:T(8,128)(2,1)S(1)}, u32[]{:S(2)}, u32[]{:S(2)}) collective-permute-start(bf16[4,2,256,128]{3,2,1,0:T(8,128)(2,1)S(1)} %slice.4.kv0), channel_id=1, source_target_pairs={{0,24},{8,16},{16,8},{24,0},{1,25},{9,17},{17,9},{25,1},{2,26},{10... | collective-permute-start | bytes 1572872 | tf_op jit(solution)/shard_map/ppermute | solution.py:423
  43.9 22.2 %collective-permute-start.9 = (bf16[4,2,256,128]{3,2,1,0:T(8,128)(2,1)S(1)}, bf16[4,2,256,128]{3,2,1,0:T(8,128)(2,1)S(1)}, u32[]{:S(2)}, u32[]{:S(2)}) collective-permute-start(bf16[4,2,256,128]{3,2,1,0:T(8,128)(2,1)S(1)} %slice.4.kv0), channel_id=1, source_target_pairs={{0,8},{8,0},{1,9},{9,1},{2,10},{10,2},{3,11},{11,3},{4,12},{12,4},... | collective-permute-start | bytes 1572872 | tf_op jit(solution)/shard_map/ppermute | solution.py:421
  51.1 0.8 copy-start.16
  51.1 0.9 copy-start.17
  63.1 13.2 %copy-start.15 = (bf16[2,128,896]{2,1,0:T(8,128)(2,1)S(1)}, bf16[2,128,896]{2,1,0:T(8,128)(2,1)}, u32[]{:S(2)}) copy-start(bf16[2,128,896]{2,1,0:T(8,128)(2,1)} %get-tuple-element.85) | copy-start | bytes 1376260
  63.2 13.2 %collective-permute-start.7 = (bf16[2,128,896]{2,1,0:T(8,128)(2,1)}, bf16[2,128,896]{2,1,0:T(8,128)(2,1)S(1)}, u32[]{:S(2)}, u32[]{:S(2)}) collective-permute-start(bf16[2,128,896]{2,1,0:T(8,128)(2,1)} %get-tuple-element.86), channel_id=1, source_target_pairs={{0,6},{2,0},{4,2},{6,4},{1,7},{3,1},{5,3},{7,5},{8,14},{10,8},{12,... | collective-permute-start | bytes 1376264 | tf_op jit(solution)/shard_map/ppermute | solution.py:482
  66.1 10.2 %collective-permute-start.8 = (bf16[2,128,896]{2,1,0:T(8,128)(2,1)}, bf16[2,128,896]{2,1,0:T(8,128)(2,1)S(1)}, u32[]{:S(2)}, u32[]{:S(2)}) collective-permute-start(bf16[2,128,896]{2,1,0:T(8,128)(2,1)} %get-tuple-element.87), channel_id=1, source_target_pairs={{0,2},{2,4},{4,6},{6,0},{1,3},{3,5},{5,7},{7,1},{8,10},{10,12},{12... | collective-permute-start | bytes 1376264 | tf_op jit(solution)/shard_map/ppermute | solution.py:483
  66.1 0.8 copy-start.2
  66.1 1.0 copy-start.3
  66.2 1.1 %copy-start.4 = (bf16[4,2,256,128]{3,2,1,0:T(8,128)(2,1)}, bf16[4,2,256,128]{3,2,1,0:T(8,128)(2,1)S(1)}, u32[]{:S(2)}) copy-start(bf16[4,2,256,128]{3,2,1,0:T(8,128)(2,1)S(1)} %collective-permute-done.9.kv1) | copy-start | bytes 1572868
  67.3 12.5 %copy-start.22 = (bf16[2,128,896]{2,1,0:T(8,128)(2,1)S(1)}, bf16[2,128,896]{2,1,0:T(8,128)(2,1)}, u32[]{:S(2)}) copy-start(bf16[2,128,896]{2,1,0:T(8,128)(2,1)} %get-tuple-element.100) | copy-start | bytes 1376260
  67.3 16.9 %copy-start.12 = (bf16[2,128,896]{2,1,0:T(8,128)(2,1)S(1)}, bf16[2,128,896]{2,1,0:T(8,128)(2,1)}, u32[]{:S(2)}) copy-start(bf16[2,128,896]{2,1,0:T(8,128)(2,1)} %get-tuple-element.101) | copy-start | bytes 1376260
  76.3 13.2 %copy-start.8 = (bf16[2,128,896]{2,1,0:T(8,128)(2,1)S(1)}, bf16[2,128,896]{2,1,0:T(8,128)(2,1)}, u32[]{:S(2)}) copy-start(bf16[2,128,896]{2,1,0:T(8,128)(2,1)} %get-tuple-element.115) | copy-start | bytes 1376260
  76.5 12.7 %collective-permute-start.12 = (bf16[2,128,896]{2,1,0:T(8,128)(2,1)S(1)}, bf16[2,128,896]{2,1,0:T(8,128)(2,1)S(1)}, u32[]{:S(2)}, u32[]{:S(2)}) collective-permute-start(bf16[2,128,896]{2,1,0:T(8,128)(2,1)S(1)} %add_convert_fusion.2), channel_id=1, source_target_pairs={{0,6},{2,0},{4,2},{6,4},{1,7},{3,1},{5,3},{7,5},{8,14},{10,8},{12,... | collective-permute-start | bytes 1376264 | tf_op jit(solution)/shard_map/ppermute | solution.py:499
  79.8 9.7 %collective-permute-start.13 = (bf16[2,128,896]{2,1,0:T(8,128)(2,1)S(1)}, bf16[2,128,896]{2,1,0:T(8,128)(2,1)S(1)}, u32[]{:S(2)}, u32[]{:S(2)}) collective-permute-start(bf16[2,128,896]{2,1,0:T(8,128)(2,1)S(1)} %copy-done.22), channel_id=1, source_target_pairs={{0,2},{2,4},{4,6},{6,0},{1,3},{3,5},{5,7},{7,1},{8,10},{10,12},{12... | collective-permute-start | bytes 1376264 | tf_op jit(solution)/shard_map/ppermute | solution.py:500
  79.8 4.9 %collective-permute-start.14 = (bf16[256,128]{1,0:T(8,128)(2,1)}, bf16[256,128]{1,0:T(8,128)(2,1)S(1)}, u32[]{:S(2)}, u32[]{:S(2)}) collective-permute-start(bf16[256,128]{1,0:T(8,128)(2,1)} %get-tuple-element.105), channel_id=1, source_target_pairs={{0,96},{32,0},{64,32},{96,64},{1,97},{33,1},{65,33},{97,65},{2,98}... | collective-permute-start | bytes 196616 | tf_op jit(solution)/shard_map/ppermute | solution.py:498
  82.4 6.0 %collective-permute-start.15 = (bf16[256,128]{1,0:T(8,128)(2,1)}, bf16[256,128]{1,0:T(8,128)(2,1)S(1)}, u32[]{:S(2)}, u32[]{:S(2)}) collective-permute-start(bf16[256,128]{1,0:T(8,128)(2,1)} %get-tuple-element.106), channel_id=1, source_target_pairs={{0,64},{32,96},{64,0},{96,32},{1,65},{33,97},{65,1},{97,33},{2,66}... | collective-permute-start | bytes 196616 | tf_op jit(solution)/shard_map/ppermute | solution.py:498
  83.3 5.8 %collective-permute-start.16 = (bf16[256,128]{1,0:T(8,128)(2,1)}, bf16[256,128]{1,0:T(8,128)(2,1)S(1)}, u32[]{:S(2)}, u32[]{:S(2)}) collective-permute-start(bf16[256,128]{1,0:T(8,128)(2,1)} %get-tuple-element.107), channel_id=1, source_target_pairs={{0,32},{32,64},{64,96},{96,0},{1,33},{33,65},{65,97},{97,1},{2,34}... | collective-permute-start | bytes 196616 | tf_op jit(solution)/shard_map/ppermute | solution.py:498
  84.1 6.9 %copy-start.21 = (bf16[2,128,896]{2,1,0:T(8,128)(2,1)S(1)}, bf16[2,128,896]{2,1,0:T(8,128)(2,1)}, u32[]{:S(2)}) copy-start(bf16[2,128,896]{2,1,0:T(8,128)(2,1)} %get-tuple-element.114) | copy-start | bytes 1376260
  84.7 9.6 %copy-start.18 = (bf16[256,128]{1,0:T(8,128)(2,1)}, bf16[256,128]{1,0:T(8,128)(2,1)S(1)}, u32[]{:S(2)}) copy-start(bf16[256,128]{1,0:T(8,128)(2,1)S(1)} %collective-permute-done.14.s1) | copy-start | bytes 196612
  88.4 5.8 %copy-start.19 = (bf16[256,128]{1,0:T(8,128)(2,1)}, bf16[256,128]{1,0:T(8,128)(2,1)S(1)}, u32[]{:S(2)}) copy-start(bf16[256,128]{1,0:T(8,128)(2,1)S(1)} %collective-permute-done.15.s2) | copy-start | bytes 196612
  89.1 5.1 %copy-start.20 = (bf16[256,128]{1,0:T(8,128)(2,1)}, bf16[256,128]{1,0:T(8,128)(2,1)S(1)}, u32[]{:S(2)}) copy-start(bf16[256,128]{1,0:T(8,128)(2,1)S(1)} %collective-permute-done.16.s3) | copy-start | bytes 196612
  89.6 10.1 %collective-permute-start.19 = (bf16[2,128,896]{2,1,0:T(8,128)(2,1)S(1)}, bf16[2,128,896]{2,1,0:T(8,128)(2,1)S(1)}, u32[]{:S(2)}, u32[]{:S(2)}) collective-permute-start(bf16[2,128,896]{2,1,0:T(8,128)(2,1)S(1)} %add_convert_fusion), channel_id=1, source_target_pairs={{0,1},{1,0},{2,3},{3,2},{4,5},{5,4},{6,7},{7,6},{8,9},{9,8},{10,11... | collective-permute-start | bytes 1376264 | tf_op jit(solution)/shard_map/ppermute | solution.py:504
  91.0 9.7 %collective-permute-start.17 = (bf16[2,128,896]{2,1,0:T(8,128)(2,1)S(1)}, bf16[2,128,896]{2,1,0:T(8,128)(2,1)S(1)}, u32[]{:S(2)}, u32[]{:S(2)}) collective-permute-start(bf16[2,128,896]{2,1,0:T(8,128)(2,1)S(1)} %add_convert_fusion.1), channel_id=1, source_target_pairs={{0,2},{2,4},{4,6},{6,0},{1,3},{3,5},{5,7},{7,1},{8,10},{10,12},{12... | collective-permute-start | bytes 1376264 | tf_op jit(solution)/shard_map/ppermute | solution.py:505
  91.0 9.7 %collective-permute-start.18 = (bf16[2,128,896]{2,1,0:T(8,128)(2,1)S(1)}, bf16[2,128,896]{2,1,0:T(8,128)(2,1)S(1)}, u32[]{:S(2)}, u32[]{:S(2)}) collective-permute-start(bf16[2,128,896]{2,1,0:T(8,128)(2,1)S(1)} %copy-done.21), channel_id=1, source_target_pairs={{0,6},{2,0},{4,2},{6,4},{1,7},{3,1},{5,3},{7,5},{8,14},{10,8},{12,... | collective-permute-start | bytes 1376264 | tf_op jit(solution)/shard_map/ppermute | solution.py:506
  99.7 1.0 copy-start.5
  100.7 0.8 copy-start.6
  100.7 0.9 copy-start.7
